TPU v7x, 32 devices: a whole 2x2x4 slice. The times are simulated.
32 devices in a mesh: seq: 8 (over z, x), tp: 4 (over y, core).
Axes of the slice: x: 2, y: 2, z: 4, core: 2. Of those that a mesh axis runs over, the one named last changes fastest.
Arguments:
- tokens: bfloat16 [4, 4096, 768], P(None, 'seq'), may hold values from -6 to 6
- query_weight: bfloat16 [768, 768], P(None, 'tp'), may hold values from -0.21875 to 0.21875
- query_bias: bfloat16 [12, 64], P('tp'), may hold values from -4 to 4
- key_weight: bfloat16 [768, 768], P(None, 'tp'), may hold values from -0.21875 to 0.21875
- value_weight: bfloat16 [768, 768], P(None, 'tp'), may hold values from -0.21875 to 0.21875
- value_bias: bfloat16 [12, 64], P('tp'), may hold values from -4 to 4
- conv_weight: bfloat16 [12, 33], P('tp'), may hold values from -1 to 1
- output_weight: bfloat16 [768, 768], P('tp'), may hold values from -0.21875 to 0.21875
- output_bias: bfloat16 [768], replicated, may hold values from -3 to 3
- first_gain: bfloat16 [768], replicated, may hold values from 0.5 to 1.5
- first_shift: bfloat16 [768], replicated, may hold values from -3 to 3
- up_weight: bfloat16 [768, 3072], P(None, 'tp'), may hold values from -0.21875 to 0.21875
- up_bias: bfloat16 [3072], P('tp'), may hold values from -6 to 6
- down_weight: bfloat16 [3072, 768], P('tp'), may hold values from -0.109375 to 0.109375
- down_bias: bfloat16 [768], replicated, may hold values from -3 to 3
- second_gain: bfloat16 [768], replicated, may hold values from 0.5 to 1.5
- second_shift: bfloat16 [768], replicated, may hold values from -3 to 3
- segment_sizes: int32 [4, 8, 64], replicated, may hold values from 0 to 96, as said below
- cotangent: bfloat16 [4, 4096, 768], P(None, 'seq'), may hold values from -6 to 6
Outputs:
- layer_out: bfloat16 [4, 4096, 768], P(None, 'seq')
- grad_tokens: float32 [4, 4096, 768], P(None, 'seq')
- grad_query_weight: float32 [768, 768], P('seq', 'tp')
- grad_query_bias: float32 [12, 64], P('tp', 'seq')
- grad_key_weight: float32 [768, 768], P('seq', 'tp')
- grad_value_weight: float32 [768, 768], P('seq', 'tp')
- grad_value_bias: float32 [12, 64], P('tp')
- grad_conv_weight: float32 [12, 33], P('tp')
- grad_output_weight: float32 [768, 768], P('tp', 'seq')
- grad_output_bias: float32 [768], replicated
- grad_first_gain: float32 [768], replicated
- grad_first_shift: float32 [768], replicated
- grad_up_weight: float32 [768, 3072], P('seq', 'tp')
- grad_up_bias: float32 [3072], P('tp')
- grad_down_weight: float32 [3072, 768], P('tp', 'seq')
- grad_down_bias: float32 [768], replicated
- grad_second_gain: float32 [768], replicated
- grad_second_shift: float32 [768], replicated
Inputs may be any that keep to these rules, and one draw needn't show every extreme that they name: `segment_sizes`: row by row, the sizes of the 64 consecutive landmark segments of each of up to 8 items packed in order; a row's sizes add up to 4096; each item holds a multiple of 512 tokens and each of its segments at least one; unused item places come last and hold zeros; for every g below 1, some row r + g is one single item.
All inputs are finite; a program needn't handle non-finite values.
Results may differ from a plain program's by a relative error of at most 0.023.
Values may be sent and summed in bfloat16 or wider, within the bound.
No kernel may reach another device: no remote copies, remote signals or barrier semaphores. Data moves between devices by JAX's collectives and lax.ppermute only.
A program may use at most 192 MiB of HBM per device.

v0:
```python
import functools

import jax
import jax.numpy as jnp
from jax import lax
from jax.experimental import pallas as pl
from jax.experimental.pallas import tpu as pltpu
from jax.sharding import PartitionSpec as P

HEAD_DIM = 64
TAPS = 33
SWEEPS = 6
SPAN = 4096
LANES = 128
STRIPE = 128
TILE = 256
VMEM_LIMIT = 44 << 20


highest = lax.Precision.HIGHEST
epsilon = 1e-05
very_negative = -1e30
f32 = jnp.float32
bf16 = jnp.bfloat16


def swap(value, axis, step):
    return lax.ppermute(value, axis, [(i, i ^ step) for i in range(lax.axis_size(axis))])


def dot(a, b):
    return jnp.dot(a, b, preferred_element_type=f32)


def outer(a, b):
    return lax.dot_general(a, b, (((0,), (0,)), ((), ())), preferred_element_type=f32)


def dot_t(a, b):
    return lax.dot_general(a, b, (((1,), (1,)), ((), ())), preferred_element_type=f32)


def after(value, *others):
    return lax.optimization_barrier((value,) + others)[0]


def scatter_start(blocks):
    got = swap((blocks[1], blocks[3]), "tp", 1)
    return [
        (mine.astype(f32) + far.astype(f32)).astype(bf16)
        for mine, far in zip((blocks[0], blocks[2]), got)
    ]


def scatter_far(blocks):
    far = swap(blocks[1], "tp", 2)
    return [(blocks[0].astype(f32) + far.astype(f32)).astype(bf16)]


def scatter_level(blocks, seq_index, size, last=False):
    bit = (seq_index // size) % 2
    views = [b.reshape(b.shape[0] // 2, 2, b.shape[1], b.shape[2]) for b in blocks]
    keep = [lax.dynamic_index_in_dim(v, bit, axis=1, keepdims=False) for v in views]
    send = [lax.dynamic_index_in_dim(v, 1 - bit, axis=1, keepdims=False) for v in views]
    got = swap(tuple(send), "seq", size)
    total = [k.astype(f32) + g.astype(f32) for k, g in zip(keep, got)]
    return total if last else [t.astype(bf16) for t in total]


def by_targets(blocks, count):
    return [b.reshape(count, b.shape[0] // count, b.shape[1]) for b in blocks]


def sum_merge(a, b, use):
    return a + jnp.where(use, b, 0.0)


def flag(flags_ref, row):
    return flags_ref[row : row + 1, 0:1] > 0.5


def plain_parts():
    return sum_merge, lambda value: value.astype(bf16), lambda message: message.astype(f32)


def soft_parts(heads):
    return (
        functools.partial(merge_states, heads=heads),
        functools.partial(state_message, heads=heads),
        functools.partial(message_state, heads=heads),
    )


def edges_after(parts, flags_ref, level, facing, outer_edge, got, got_outer):
    merge = parts[0]
    near = merge(outer_edge, got, flag(flags_ref, 4 * level + 1))
    away = merge(got_outer, facing, flag(flags_ref, 4 * level + 2))
    turn = flag(flags_ref, 4 * level + 3)
    return jnp.where(turn, near, away), jnp.where(turn, away, near)


def merge_first_kernel(parts, flags_ref, own_ref, got_ref, new_ref, message_ref):
    merge, encode, decode = parts
    own, got = own_ref[...], decode(got_ref[...])
    new_ref[...] = merge(own, got, flag(flags_ref, 0))
    facing, outer_edge = edges_after(parts, flags_ref, 0, own, own, got, got)
    message_ref[...] = jnp.concatenate((encode(facing), encode(outer_edge)), axis=0)


def merge_next_kernel(parts, flags_ref, own_ref, sent_ref, got_ref, new_ref, message_ref):
    merge, encode, decode = parts
    marks = own_ref.shape[0]
    got, got_outer = decode(got_ref[:marks]), decode(got_ref[marks:])
    new_ref[...] = merge(own_ref[...], got, flag(flags_ref, 4))
    facing, _ = edges_after(
        parts, flags_ref, 1, decode(sent_ref[:marks]), decode(sent_ref[marks:]), got, got_outer
    )
    message_ref[...] = encode(facing)


def exchange(parts, name, flags, own, message):
    marks, width = own.shape
    first = call(
        functools.partial(merge_first_kernel, parts),
        (((marks, width), f32), ((2 * marks, width), bf16)),
        name + "_first",
    )
    following = call(
        functools.partial(merge_next_kernel, parts),
        (((marks, width), f32), ((marks, width), bf16)),
        name + "_next",
    )
    own, sent = first(flags, own, swap(message, "seq", 1))
    own, message = following(flags, own, sent, swap(sent, "seq", 2))
    return own, swap(message, "seq", 4)


def sum_everywhere(value):
    for axis in ("tp", "seq"):
        size = 1
        while size < lax.axis_size(axis):
            value = value + swap(value, axis, size)
            size *= 2
    return value


def newton_inverse(kernel):
    size = kernel.shape[-1]
    column_sums = jnp.sum(kernel, axis=-2)
    bound = jnp.sqrt(jnp.sum(column_sums * column_sums, axis=-1))[..., None, None]
    identity = jnp.eye(size, dtype=kernel.dtype)
    inverse = jnp.swapaxes(kernel, -1, -2) / bound
    for sweep in range(SWEEPS):
        product = jnp.matmul(kernel, inverse, precision=highest)
        inner = 7.0 * identity - product
        inner = 15.0 * identity - jnp.matmul(product, inner, precision=highest)
        inner = 13.0 * identity - jnp.matmul(product, inner, precision=highest)
        inverse = 0.25 * jnp.matmul(inverse, inner, precision=highest)
    return inverse


WHOLE = pl.BlockSpec(memory_space=pltpu.VMEM)


def call(kernel, outs, name, scratch=(), limit=24 << 20, flops=0, moved=0, scalars=0):
    outs = tuple(jax.ShapeDtypeStruct(shape, dtype) for shape, dtype in outs)

    def run(*operands):
        return pl.pallas_call(
            kernel,
            out_shape=outs,
            in_specs=[pl.BlockSpec(memory_space=pltpu.SMEM)] * scalars
            + [WHOLE] * (len(operands) - scalars),
            out_specs=(WHOLE,) * len(outs),
            scratch_shapes=list(scratch),
            compiler_params=pltpu.CompilerParams(vmem_limit_bytes=limit),
            cost_estimate=pl.CostEstimate(flops=flops, bytes_accessed=moved, transcendentals=0),
            name=name,
        )(*operands)

    return run


def lane_ids(shape):
    return lax.broadcasted_iota(jnp.int32, shape, len(shape) - 1)


def row_ids(shape):
    return lax.broadcasted_iota(jnp.int32, shape, len(shape) - 2)


def spread_heads(block):
    heads = block.shape[1] // HEAD_DIM
    tall = jnp.concatenate([block] * heads, axis=0)
    same = row_ids(tall.shape) // HEAD_DIM == lane_ids(tall.shape) // HEAD_DIM
    return jnp.where(same, tall, jnp.zeros_like(tall))


def gather_heads(square):
    heads = square.shape[1] // HEAD_DIM
    result = jnp.zeros((HEAD_DIM, square.shape[1]), square.dtype)
    lane = lane_ids(result.shape) // HEAD_DIM
    for j in range(heads):
        result = jnp.where(lane == j, square[j * HEAD_DIM : (j + 1) * HEAD_DIM], result)
    return result


def two_parts(value):
    high = value.astype(bf16)
    return high, (value - high.astype(f32)).astype(bf16)


def dot_fine(a, b):
    a_high, a_low = two_parts(a)
    b_high, b_low = two_parts(b)
    return dot(a_high, b_high) + (dot(a_high, b_low) + dot(a_low, b_high))


def dot_fine_t(a, b):
    a_high, a_low = two_parts(a)
    b_high, b_low = two_parts(b)
    return dot_t(a_high, b_high) + (dot_t(a_high, b_low) + dot_t(a_low, b_high))


def outer_fine(a, b):
    a_high, a_low = two_parts(a)
    b_high, b_low = two_parts(b)
    return outer(a_high, b_high) + (outer(a_high, b_low) + outer(a_low, b_high))


def group_of(array, r, channels):
    return array[:, r * channels : (r + 1) * channels]


def layout_kernel(place_ref, sizes_ref, member_ref, turned_ref, count_ref, flags_ref):
    row, local = place_ref[0], place_ref[1]
    sizes = sizes_ref[row].astype(f32)
    items, marks = sizes.shape
    width = turned_ref.shape[1]
    devices = SPAN // width

    def pick(condition, value, axis):
        return jnp.sum(jnp.where(condition, value, 0.0), axis=axis, keepdims=True)

    totals = jnp.sum(sizes, axis=1, keepdims=True)
    small = (items, items)
    totals_row = pick(row_ids(small) == lane_ids(small), jnp.broadcast_to(totals, small), 0)
    ends = pick(lane_ids(small) <= row_ids(small), jnp.broadcast_to(totals_row, small), 1)
    wide = (items, LANES)
    below = jnp.broadcast_to(ends, wide) <= (width * lane_ids(wide)).astype(f32)
    item_of = jnp.sum(jnp.where(below, 1.0, 0.0), axis=0, keepdims=True)

    def item_at(index):
        return pick(lane_ids(item_of.shape) == index, item_of, 1)

    own = item_at(local)
    item_rows = row_ids((items, 1)).astype(f32)
    own_sizes = pick(row_ids(sizes.shape).astype(f32) == own, sizes, 0)
    item_start = pick(item_rows < own, totals, 0)
    square = (marks, marks)
    spread = jnp.broadcast_to(own_sizes, square)
    size_column = pick(row_ids(square) == lane_ids(square), spread, 1)
    end_column = pick(lane_ids(square) <= row_ids(square), spread, 1)
    end_row = pick(row_ids(square) <= lane_ids(square), jnp.broadcast_to(size_column, square), 0)
    first = (local * width).astype(f32) - item_start
    along = lane_ids(turned_ref.shape).astype(f32) + first
    inside = (along >= end_column - size_column) & (along < end_column)
    turned_ref[...] = jnp.where(inside, 1.0, 0.0).astype(bf16)
    down = row_ids(member_ref.shape).astype(f32) + first
    inside = (down >= end_row - own_sizes) & (down < end_row)
    member_ref[...] = jnp.where(inside, 1.0, 0.0).astype(bf16)
    count_ref[...] = jnp.broadcast_to(jnp.maximum(size_column, 1.0), count_ref.shape)

    def put(at, value):
        flags_ref[at : at + 1, :] = jnp.broadcast_to(jnp.where(value, 1.0, 0.0), (1, LANES))

    level, size = 0, 1
    while size < devices:
        start = local - local % size
        is_left = (local // size) % 2 == 0
        other = jnp.where(is_left, start + size, start - size)
        far_facing = item_at(jnp.where(is_left, other, other + size - 1))
        far_outer = item_at(jnp.where(is_left, other + size - 1, other))
        facing = item_at(jnp.where(is_left, start + size - 1, start))
        outer_edge = item_at(jnp.where(is_left, start, start + size - 1))
        next_left = (local // (2 * size)) % 2 == 0
        put(4 * level, own == far_facing)
        put(4 * level + 1, outer_edge == far_facing)
        put(4 * level + 2, far_outer == facing)
        turn = jnp.where(is_left != next_left, 1.0, 0.0)
        flags_ref[4 * level + 3 : 4 * level + 4, :] = jnp.full((1, LANES), turn, f32)
        level, size = level + 1, 2 * size
    before = jnp.where(local > 0, 1.0, 0.0) * jnp.where(item_at(local - 1) == own, 1.0, 0.0)
    behind = jnp.where(local < devices - 1, 1.0, 0.0) * jnp.where(
        item_at(local + 1) == own, 1.0, 0.0
    )
    flags_ref[12:13, :] = jnp.broadcast_to(before, (1, LANES))
    flags_ref[13:14, :] = jnp.broadcast_to(behind, (1, LANES))
    flags_ref[14:16, :] = jnp.zeros((2, LANES), f32)


def query_key_kernel(flat_ref, w0, w1, bias_ref, member_ref, query_ref, keys_ref, part_ref, message_ref):
    channels = query_ref.shape[2]
    scale = HEAD_DIM ** (-0.25)
    parts = []
    for r, w in enumerate((w0, w1)):
        query = dot_t(flat_ref[...], w[:channels]) + bias_ref[r : r + 1, :]
        query = (scale * query).astype(bf16)
        keys = (scale * dot_t(flat_ref[...], w[channels:])).astype(bf16)
        query_ref[r] = query
        keys_ref[r] = keys
        parts += [dot(member_ref[...], query), dot(member_ref[...], keys)]
    part = jnp.concatenate(parts, axis=1)
    part_ref[...] = part
    message_ref[...] = part.astype(bf16)


def land_kernel(flags_ref, count_ref, own0, got0, own1, got1, query_ref, keys_ref, kernel_ref):
    channels = own0.shape[1] // 4
    heads = channels // HEAD_DIM
    count = count_ref[:, 0:1]
    queries, keys = [], []
    for own, got in ((own0, got0), (own1, got1)):
        land = sum_merge(own[...], got[...].astype(f32), flag(flags_ref, 8)) / count
        for r in range(2):
            queries.append(group_of(land, 2 * r, channels).astype(bf16))
            keys.append(group_of(land, 2 * r + 1, channels).astype(bf16))
    lane = lane_ids(queries[0].shape) // HEAD_DIM
    for r in range(len(queries)):
        for j in range(heads):
            alone = jnp.where(lane == j, queries[r], jnp.zeros_like(queries[r]))
            scores = dot_t(alone, keys[r])
            powers = jnp.exp(scores - jnp.max(scores, axis=1, keepdims=True))
            kernel_ref[r * heads + j] = powers / jnp.sum(powers, axis=1, keepdims=True)
    query_ref[...] = jnp.concatenate(queries, axis=1)
    keys_ref[...] = jnp.concatenate(keys, axis=1)


def value_kernel(flat_ref, w0, w1, w2, w3, bias_ref, values_ref, head_ref, tail_ref):
    reach = head_ref.shape[0]
    heads, tails = [], []
    for r, w in enumerate((w0, w1, w2, w3)):
        values = (dot_t(flat_ref[...], w[...]) + bias_ref[r : r + 1, :]).astype(bf16)
        values_ref[r] = values
        heads.append(values[:reach])
        tails.append(values[values.shape[0] - reach :])
    head_ref[...] = jnp.concatenate(heads, axis=1)
    tail_ref[...] = jnp.concatenate(tails, axis=1)


def key_kernel(k0, k1, values_ref, land_query_ref, state_ref, message_ref):
    channels = values_ref.shape[2]
    heads = channels // HEAD_DIM
    mixed = []
    marks = land_query_ref.shape[0]
    stats = jnp.zeros((marks, LANES), f32)
    lane = lane_ids(stats.shape)
    groups = values_ref.shape[0]
    for r in range(groups):
        keys = (k0, k1)[r // 2][r % 2]
        scores = dot_t(spread_heads(group_of(land_query_ref[...], r, channels)), keys)
        top = jnp.max(scores, axis=1, keepdims=True).astype(bf16).astype(f32)
        powers = jnp.exp(scores - top)
        total = jnp.sum(powers, axis=1, keepdims=True)
        mixed.append(gather_heads(dot(powers.astype(bf16), values_ref[r])))
        for j in range(heads):
            h = r * heads + j
            at = slice(j * marks, (j + 1) * marks)
            stats = jnp.where(lane == h, top[at], stats)
            stats = jnp.where(lane == groups * heads + h, total[at], stats)
    state = jnp.concatenate(mixed + [stats], axis=1)
    state_ref[...] = state
    message_ref[...] = state_message(state, groups * heads)


def state_message(state, heads):
    width = state.shape[1] - LANES
    stats = state[:, width:]
    lane = lane_ids(stats.shape)
    high = stats.astype(bf16).astype(f32)
    low = pltpu.roll(stats - high, heads, 1)
    last = jnp.where(lane < 2 * heads, high, jnp.where(lane < 3 * heads, low, 0.0))
    return jnp.concatenate((state[:, :width], last), axis=1).astype(bf16)


def message_state(message, heads):
    message = message.astype(f32)
    width = message.shape[1] - LANES
    stats = message[:, width:]
    lane = lane_ids(stats.shape)
    low = pltpu.roll(stats, LANES - heads, 1)
    stats = stats + jnp.where((lane >= heads) & (lane < 2 * heads), low, 0.0)
    stats = jnp.where(lane < 2 * heads, stats, 0.0)
    return jnp.concatenate((message[:, :width], stats), axis=1)


def widen(stats, first, width):
    pieces = []
    rows = stats.shape[0]
    for pair in range(width // LANES):
        lane = lane_ids((rows, LANES))
        at = first + 2 * pair
        pieces.append(
            jnp.where(lane < HEAD_DIM, stats[:, at : at + 1], stats[:, at + 1 : at + 2])
        )
    return jnp.concatenate(pieces, axis=1)


def merge_states(a, b, use, heads):
    width = a.shape[1] - LANES
    stats_a, stats_b = a[:, width:], b[:, width:]
    lane = lane_ids(stats_a.shape)
    top = jnp.where(use, jnp.maximum(stats_a, stats_b), stats_a)
    is_top = lane < heads
    scale_a = jnp.exp(jnp.where(is_top, stats_a - top, 0.0))
    scale_b = jnp.where(use, jnp.exp(jnp.where(is_top & use, stats_b - top, 0.0)), 0.0)
    values = a[:, :width] * widen(scale_a, 0, width) + b[:, :width] * widen(scale_b, 0, width)
    total = stats_a * pltpu.roll(scale_a, heads, 1) + stats_b * pltpu.roll(scale_b, heads, 1)
    stats = jnp.where(is_top, top, jnp.where(lane < 2 * heads, total, 0.0))
    return jnp.concatenate((values, stats), axis=1)


def token_kernel(q0, q1, land_key_ref, weights_ref):
    groups, rows, width = weights_ref.shape
    channels = q0.shape[2]
    heads = channels // HEAD_DIM
    for r in range(groups):
        query = (q0, q1)[r // 2][r % 2]
        scores = dot_t(spread_heads(group_of(land_key_ref[...], r, channels)), query)
        scores = scores.reshape(heads, rows // heads, width)
        powers = jnp.exp(scores - jnp.max(scores, axis=1, keepdims=True))
        weights = powers / jnp.sum(powers, axis=1, keepdims=True)
        weights_ref[r] = weights.reshape(rows, width)


def toeplitz(taps_row, rows, width):
    wide = jnp.broadcast_to(taps_row, (rows, taps_row.shape[1]))
    return pltpu.roll(wide, 0, 1, stride=1, stride_axis=0)[:, :width]


def with_rim(cells, before, after, flags_ref):
    return jnp.concatenate(
        (
            jnp.where(flag(flags_ref, 12), before, jnp.zeros_like(before)),
            cells,
            jnp.where(flag(flags_ref, 13), after, jnp.zeros_like(after)),
        ),
        axis=0,
    )


def convolve(rim, filters):
    tall = jnp.concatenate(filters, axis=0)
    span = tall.shape[1]
    pieces = []
    for start in range(0, rim.shape[0] - (span - STRIPE), STRIPE):
        product = dot(tall, rim[start : start + span])
        lane = lane_ids((STRIPE, rim.shape[1])) // HEAD_DIM
        piece = product[:STRIPE]
        for j in range(1, len(filters)):
            piece = jnp.where(lane == j, product[j * STRIPE : (j + 1) * STRIPE], piece)
        pieces.append(piece)
    return jnp.concatenate(pieces, axis=0)


def context_kernel(own_ref, got_ref, inverse_ref, weights_ref, values_ref, before_ref, after_ref,
                   flags_ref, taps_ref, context_ref, mixed_ref, low_ref, stats_ref):
    groups, width, channels = values_ref.shape
    heads = channels // HEAD_DIM
    reach = before_ref.shape[0]
    merge, _, decode = soft_parts(groups * heads)
    state = merge(own_ref[...], decode(got_ref[...]), flag(flags_ref, 8))
    model = groups * channels
    stats_ref[...] = state[:, model:]
    mixed = state[:, :model] / widen(state[:, model:], groups * heads, model)
    mixed_ref[...] = mixed
    lows = []
    for r in range(groups):
        mixed_group = group_of(mixed, r, channels)
        lane = lane_ids(mixed_group.shape) // HEAD_DIM
        land = jnp.zeros(mixed_group.shape, f32)
        for j in range(heads):
            land = jnp.where(lane == j, dot_fine(inverse_ref[r * heads + j], mixed_group), land)
        low = land.astype(bf16)
        lows.append(low)
        nystrom = outer(weights_ref[r].astype(bf16), spread_heads(low))
        rim = with_rim(
            values_ref[r],
            group_of(before_ref[...], r, channels),
            group_of(after_ref[...], r, channels),
            flags_ref,
        )
        filters = [
            toeplitz(taps_ref[r * heads + j : r * heads + j + 1, :], STRIPE, STRIPE + 2 * reach)
            .astype(bf16)
            for j in range(heads)
        ]
        context_ref[r] = (nystrom + convolve(rim, filters)).astype(bf16)
    low_ref[...] = jnp.concatenate(lows, axis=1)


def token_back_kernel(back_ref, weights_ref, low_ref, q0, q1, land_key_ref, part_ref,
                      message_ref, part_key_ref, message_key_ref, direct_ref, head_ref, tail_ref):
    groups, width, channels = back_ref.shape
    heads = channels // HEAD_DIM
    reach = head_ref.shape[0]
    parts, key_parts = [], []
    for r in range(groups):
        back = back_ref[r]
        query = (q0, q1)[r // 2][r % 2]
        weights = weights_ref[r]
        parts.append(gather_heads(dot(weights.astype(bf16), back)))
        slope = dot_t(spread_heads(group_of(low_ref[...], r, channels)), back)
        product = (weights * slope).reshape(heads, -1, width)
        rows = jnp.sum(product, axis=1, keepdims=True)
        rows = jnp.broadcast_to(rows, product.shape).reshape(weights.shape)
        scores = (weights * (slope - rows)).astype(bf16)
        key_parts.append(gather_heads(dot(scores, query)))
        direct_ref[r] = outer(scores, spread_heads(group_of(land_key_ref[...], r, channels)))
    for pieces, whole_ref, low in ((parts, part_ref, message_ref), (key_parts, part_key_ref, message_key_ref)):
        whole = jnp.concatenate(pieces, axis=1)
        whole_ref[...] = whole
        low[...] = whole.astype(bf16)
    head_ref[...] = jnp.concatenate([back_ref[r, :reach] for r in range(groups)], axis=1)
    tail_ref[...] = jnp.concatenate([back_ref[r, width - reach :] for r in range(groups)], axis=1)


def conv_back_kernel(back_ref, before_ref, after_ref, values_ref, vbefore_ref, vafter_ref, flags_ref,
                     flipped_ref, conv_ref, taps_ref):
    groups, width, channels = back_ref.shape
    heads = channels // HEAD_DIM
    reach = before_ref.shape[0]
    span = STRIPE + 2 * reach
    order = row_ids((STRIPE, STRIPE)) + lane_ids((STRIPE, STRIPE)) == STRIPE - 1
    order = jnp.where(order, 1.0, 0.0).astype(bf16)
    lane = lane_ids((STRIPE, channels)) // HEAD_DIM
    for r in range(groups):
        rim = with_rim(
            back_ref[r],
            group_of(before_ref[...], r, channels),
            group_of(after_ref[...], r, channels),
            flags_ref,
        )
        filters = [
            toeplitz(flipped_ref[r * heads + j : r * heads + j + 1, :], STRIPE, span).astype(bf16)
            for j in range(heads)
        ]
        conv_ref[r] = convolve(rim, filters)
        value_rim = with_rim(
            values_ref[r],
            group_of(vbefore_ref[...], r, channels),
            group_of(vafter_ref[...], r, channels),
            flags_ref,
        )
        total = jnp.zeros((heads * STRIPE, span), f32)
        for start in range(0, width, STRIPE):
            turned = dot(order, back_ref[r, start : start + STRIPE])
            tall = [jnp.where(lane == j, turned, 0.0).astype(bf16) for j in range(heads)]
            total = total + dot_t(jnp.concatenate(tall, axis=0), value_rim[start : start + span])
        total = jnp.concatenate(
            (total, jnp.zeros((heads * STRIPE, 2 * LANES - span), f32)), axis=1
        )
        for j in range(heads):
            skewed = pltpu.roll(
                total[j * STRIPE : (j + 1) * STRIPE], 0, 1, stride=1, stride_axis=0
            )
            h = r * heads + j
            taps_ref[h : h + 1, :] = jnp.sum(skewed, axis=0, keepdims=True)


def seed_kernel(flags_ref, own_ref, got_ref, inverse_ref, mixed_ref, back_inverse_ref, back_mixed_ref):
    back = sum_merge(own_ref[...], got_ref[...].astype(f32), flag(flags_ref, 8))
    heads = inverse_ref.shape[0]
    pairs = []
    for pair in range(heads // 2):
        near = back[:, pair * LANES : (pair + 1) * LANES]
        mixed = mixed_ref[:, pair * LANES : (pair + 1) * LANES]
        lane = lane_ids(near.shape) // HEAD_DIM
        sums = jnp.zeros(near.shape, f32)
        for j in range(2):
            h = 2 * pair + j
            alone = jnp.where(lane == j, near, 0.0)
            back_inverse_ref[h] = dot_fine_t(alone, mixed)
            sums = sums + outer_fine(inverse_ref[h], alone)
        pairs.append(sums)
    back_mixed_ref[...] = jnp.concatenate(pairs, axis=1).astype(bf16)


def key_back_kernel(k0, k1, values_ref, land_query_ref, state_ref, mixed_ref, back_mixed_ref,
                    conv_ref, part_ref, message_ref, direct_ref, back_values_ref, bias_ref):
    groups, width, channels = values_ref.shape
    heads = channels // HEAD_DIM
    stats = state_ref[...]
    parts = []
    for r in range(groups):
        keys = (k0, k1)[r // 2][r % 2]
        land = spread_heads(group_of(land_query_ref[...], r, channels))
        scores = dot_t(land, keys)
        first = r * heads
        tops = jnp.concatenate([stats[:, first + j : first + j + 1] for j in range(heads)], axis=0)
        first += groups * heads
        totals = jnp.concatenate(
            [stats[:, first + j : first + j + 1] for j in range(heads)], axis=0
        )
        weights = jnp.exp(scores - tops) * (1.0 / totals)
        back_mixed = group_of(back_mixed_ref[...], r, channels)
        spread = spread_heads(back_mixed)
        dots = jnp.sum(
            spread_heads(group_of(mixed_ref[...], r, channels)) * spread.astype(f32),
            axis=1,
            keepdims=True,
        )
        slope = dot_t(spread, values_ref[r])
        back_scores = (weights * (slope - dots)).astype(bf16)
        parts.append(gather_heads(dot(back_scores, keys)))
        direct_ref[r] = outer(back_scores, land)
        back_values = (outer(weights.astype(bf16), spread) + conv_ref[r]).astype(bf16)
        back_values_ref[r] = back_values
        bias_ref[r : r + 1, :] = jnp.sum(back_values.astype(f32), axis=0, keepdims=True)
    part = jnp.concatenate(parts, axis=1)
    part_ref[...] = part
    message_ref[...] = part.astype(bf16)


def input_back_kernel(flags_ref, count_ref, flat_ref, query_direct_ref, key_direct_ref, back_values_ref,
                      query_own_ref, query_got_ref, key_own_ref, key_got_ref, kernel_ref,
                      back_kernel_ref, land_query_ref, land_key_ref, member_ref, back_input_ref,
                      w0, w1, w2, w3, v0, v1, v2, v3, grad_ref, bias_ref, g0, g1, g2, g3,
                      turned_ref):
    groups, width, channels = back_values_ref.shape
    heads = channels // HEAD_DIM
    scale = HEAD_DIM ** (-0.25)
    member = member_ref[...]
    count = count_ref[:, 0:1]
    sides = [
        sum_merge(own[...], got[...].astype(f32), flag(flags_ref, 8))
        for own, got in ((query_own_ref, query_got_ref), (key_own_ref, key_got_ref))
    ]
    total = back_input_ref[...]
    turned_ref[...] = flat_ref[...].T
    for r in range(groups):
        w, v = (w0, w1, w2, w3)[r], (v0, v1, v2, v3)[r]
        land_query = group_of(land_query_ref[...], r, channels)
        land_key = group_of(land_key_ref[...], r, channels)
        lane = lane_ids(land_query.shape) // HEAD_DIM
        query_side = group_of(sides[0], r, channels)
        key_side = group_of(sides[1], r, channels)
        for j in range(heads):
            kernel, back = kernel_ref[r * heads + j], back_kernel_ref[r * heads + j]
            scores = kernel * (back - jnp.sum(kernel * back, axis=1, keepdims=True))
            high, low = two_parts(scores)
            more = dot(high, land_key) + dot(low, land_key)
            query_side = query_side + jnp.where(lane == j, more, 0.0)
            more = outer(high, land_query) + outer(low, land_query)
            key_side = key_side + jnp.where(lane == j, more, 0.0)
        both = []
        for side, direct_ref in ((query_side, query_direct_ref), (key_side, key_direct_ref)):
            high, low = two_parts(side / count)
            both.append((direct_ref[r] + (dot(member, high) + dot(member, low))).astype(bf16))
        bias_ref[r : r + 1, :] = scale * jnp.sum(both[0].astype(f32), axis=0, keepdims=True)
        both = jnp.concatenate(both, axis=1)
        total = total + scale * dot(both, w[...]) + dot(back_values_ref[r], v[...])
        (g0, g1, g2, g3)[r][...] = (scale * dot(turned_ref[...], both)).astype(bf16)
    grad_ref[...] = total.astype(bf16)


def value_output_kernel(flat_ref, back_values_ref, back_attention_ref, context_ref, g0, g1, g2, g3):
    flat, back = flat_ref[...].T, back_attention_ref[...].T
    for r, g in enumerate((g0, g1, g2, g3)):
        g[...] = jnp.concatenate(
            (
                dot(back, context_ref[r]).astype(bf16),
                dot(flat, back_values_ref[r]).astype(bf16),
            ),
            axis=1,
        )


def place_kernel(rank_ref, r0, r1, r2, r3, out_ref):
    step = pl.program_id(0)
    for k, ref in enumerate((r0, r1, r2, r3)):

        @pl.when(step == k)
        def _():
            out_ref[0] = ref[...].astype(out_ref.dtype)


def place_rows(rank, blocks, dtype):
    width, model = blocks[0].shape
    return pl.pallas_call(
        place_kernel,
        out_shape=jax.ShapeDtypeStruct((len(blocks), width, model), dtype),
        grid_spec=pltpu.PrefetchScalarGridSpec(
            num_scalar_prefetch=1,
            grid=(len(blocks),),
            in_specs=[pl.BlockSpec((width, model), lambda i, rank: (0, 0))] * len(blocks),
            out_specs=pl.BlockSpec((1, width, model), lambda i, rank: (i ^ rank[0], 0, 0)),
        ),
        compiler_params=pltpu.CompilerParams(vmem_limit_bytes=24 << 20),
        name="place_rows",
    )(rank.reshape(1).astype(jnp.int32), *blocks)


def feed_kernel(
    flat_ref, context_ref, out0, out1, out2, out3, up0, up1, up2, up3, down0, down1, down2, down3,
    up_bias_ref, params_ref, cotangent_ref,
    layer_ref, back_input_ref, back_attention_ref, back_context_ref, active_ref, back_hidden_ref,
    first_low_ref, back_feed_ref, sums_ref, up_sums_ref,
    slope_ref, first_ref, total_ref,
):
    outs, ups, downs = (out0, out1, out2, out3), (up0, up1, up2, up3), (down0, down1, down2, down3)
    units = up0.shape[1]
    tile = TILE
    steps = units // tile
    output_bias, first_gain, first_shift, down_bias, second_gain, second_shift = [
        params_ref[k : k + 1, :] for k in range(6)
    ]

    def mean(value):
        return jnp.mean(value, axis=1, keepdims=True)

    attention = dot(context_ref[0], out0[...])
    for r in range(1, len(outs)):
        attention = attention + dot(context_ref[r], outs[r][...])
    value = flat_ref[...].astype(f32) + attention + output_bias
    centred = value - mean(value)
    first_inverse = lax.rsqrt(mean(centred * centred) + epsilon)
    first_normed = centred * first_inverse
    first_ref[...] = first_normed
    first_out = first_normed * first_gain + first_shift
    first_low_ref[...] = first_out.astype(bf16)
    total_ref[...] = first_out + down_bias
    for r in range(len(ups)):

        def forward(step, carry):
            at = pl.multiple_of(step * tile, tile)
            whole = pl.multiple_of(r * units + at, tile)
            hidden = dot(first_low_ref[...], ups[r][:, pl.ds(at, tile)])
            hidden = hidden + up_bias_ref[:, pl.ds(whole, tile)]
            cdf = 0.5 * (1.0 + lax.erf(hidden * 0.7071067811865476))
            slope_ref[:, pl.ds(whole, tile)] = cdf + hidden * (
                0.3989422804014327 * jnp.exp(-0.5 * hidden * hidden)
            )
            active = (hidden * cdf).astype(bf16)
            active_ref[:, pl.ds(whole, tile)] = active
            total_ref[...] += dot(active, downs[r][pl.ds(at, tile), :])
            return carry

        lax.fori_loop(0, steps, forward, 0)

    value = total_ref[...]
    centred = value - mean(value)
    second_inverse = lax.rsqrt(mean(centred * centred) + epsilon)
    normed = centred * second_inverse
    layer_ref[...] = (normed * second_gain + second_shift).astype(bf16)
    upstream = cotangent_ref[...].astype(f32)
    sums_ref[4:5, :] = jnp.sum(upstream * normed, axis=0, keepdims=True)
    sums_ref[5:6, :] = jnp.sum(upstream, axis=0, keepdims=True)
    scaled = upstream * second_gain
    back_second = (scaled - mean(scaled) - normed * mean(scaled * normed)) * second_inverse
    back_feed = back_second.astype(bf16)
    back_feed_ref[...] = back_feed
    sums_ref[3:4, :] = jnp.sum(back_feed.astype(f32), axis=0, keepdims=True)
    total_ref[...] = back_second
    for r in range(len(ups)):

        def backward(step, carry):
            at = pl.multiple_of(step * tile, tile)
            whole = pl.multiple_of(r * units + at, tile)
            back_active = dot_t(back_feed_ref[...], downs[r][pl.ds(at, tile), :])
            back_hidden = (back_active * slope_ref[:, pl.ds(whole, tile)]).astype(bf16)
            back_hidden_ref[:, pl.ds(whole, tile)] = back_hidden
            up_sums_ref[:, pl.ds(whole, tile)] = jnp.sum(
                back_hidden.astype(f32), axis=0, keepdims=True
            )
            total_ref[...] += dot_t(back_hidden, ups[r][:, pl.ds(at, tile)])
            return carry

        lax.fori_loop(0, steps, backward, 0)

    back_first = total_ref[...]
    first_normed = first_ref[...]
    sums_ref[1:2, :] = jnp.sum(back_first * first_normed, axis=0, keepdims=True)
    sums_ref[2:3, :] = jnp.sum(back_first, axis=0, keepdims=True)
    scaled = back_first * first_gain
    back_input = (scaled - mean(scaled) - first_normed * mean(scaled * first_normed)) * first_inverse
    back_input_ref[...] = back_input
    back_attention = back_input.astype(bf16)
    back_attention_ref[...] = back_attention
    sums_ref[0:1, :] = jnp.sum(back_attention.astype(f32), axis=0, keepdims=True)
    for r in range(len(outs)):
        back_context_ref[r] = dot_t(back_attention, outs[r][...]).astype(bf16)


def feed_layer(flat, context, outputs, ups, downs, up_bias, params, cotangent):
    width, model = flat.shape
    ranks, units = len(ups), ups[0].shape[1]
    channels = outputs[0].shape[0]
    shape = jax.ShapeDtypeStruct
    whole = pl.BlockSpec(memory_space=pltpu.VMEM)
    return pl.pallas_call(
        feed_kernel,
        out_shape=(
            shape((width, model), bf16),
            shape((width, model), f32),
            shape((width, model), bf16),
            shape((ranks, width, channels), bf16),
            shape((width, ranks * units), bf16),
            shape((width, ranks * units), bf16),
            shape((width, model), bf16),
            shape((width, model), bf16),
            shape((6, model), f32),
            shape((1, ranks * units), f32),
        ),
        in_specs=[whole] * 17,
        out_specs=(whole,) * 10,
        scratch_shapes=[
            pltpu.VMEM((width, ranks * units), f32),
            pltpu.VMEM((width, model), f32),
            pltpu.VMEM((width, model), f32),
        ],
        compiler_params=pltpu.CompilerParams(vmem_limit_bytes=VMEM_LIMIT),
        cost_estimate=pl.CostEstimate(
            flops=2 * width * model * (4 * ranks * units + 2 * ranks * channels),
            bytes_accessed=30 << 20,
            transcendentals=2 * width * ranks * units,
        ),
        name="feed_layer",
    )(flat, context, *outputs, *ups, *downs, up_bias, params, cotangent)


def per_device(
    tokens,
    query_weight,
    query_bias,
    key_weight,
    value_weight,
    value_bias,
    conv_weight,
    output_weight,
    output_bias,
    first_gain,
    first_shift,
    up_weight,
    up_bias,
    down_weight,
    down_bias,
    second_gain,
    second_shift,
    segment_sizes,
    cotangent,
):
    rows, width, model = tokens.shape
    channels = query_weight.shape[1]
    ranks = lax.axis_size("tp")
    own_heads = channels // HEAD_DIM
    heads = ranks * own_heads
    hidden_units = up_weight.shape[1]
    items = segment_sizes.shape[1]
    marks = segment_sizes.shape[2]
    reach = TAPS // 2
    device = lax.axis_index("seq")
    rank = lax.axis_index("tp")
    group = SPAN // width
    groups = segment_sizes.shape[0] // rows
    place = jnp.stack((rank * groups + device // group, device % group)).astype(jnp.int32)

    def by_rank(stacked):
        return jnp.take(stacked, jnp.arange(ranks) ^ rank, axis=0)

    half = ((2, width, channels), bf16)
    full = ((ranks, width, channels), bf16)
    full32 = ((ranks, width, channels), f32)
    edge = ((reach, model), bf16)
    marked = ((marks, model), f32)
    message = ((marks, model), bf16)
    tall = ((marks, LANES), f32)
    squares = ((heads, marks, marks), f32)

    small = jnp.concatenate(
        (
            query_bias.reshape(-1),
            value_bias.reshape(-1),
            conv_weight.reshape(-1),
            up_bias.reshape(-1),
        )
    )
    small_rows = -(-small.shape[0] // model)
    small_rows += -small_rows % 16
    small = jnp.pad(small, (0, small_rows * model - small.shape[0])).reshape(small_rows, model)
    query_key = jnp.concatenate((query_weight.T, key_weight.T), axis=0)
    value_turned = value_weight.T
    first_far = swap(query_key, "tp", 2)
    small_far = swap(small, "tp", 2)
    first_core = swap(query_key, "tp", 1)
    small_core = swap(small, "tp", 1)
    smalls = [s.reshape(-1).astype(f32) for s in (small, small_core, small_far, swap(small_far, "tp", 1))]
    member, member_turned, count, flags = call(
        layout_kernel,
        (((width, marks), bf16), ((marks, width), bf16), tall, ((16, LANES), f32)),
        "layout",
        scalars=1,
    )(place, segment_sizes)
    query_bias_all = jnp.stack([s[:channels] for s in smalls])
    value_bias_all = jnp.stack([s[channels : 2 * channels] for s in smalls])
    taps_all = jnp.concatenate(
        [s[2 * channels : 2 * channels + own_heads * TAPS].reshape(own_heads, TAPS) for s in smalls]
    )
    up_start = 2 * channels + own_heads * TAPS
    up_bias_all = jnp.concatenate([s[up_start : up_start + hidden_units] for s in smalls])
    taps_wide = jnp.pad(taps_all, ((0, 0), (0, 2 * LANES - TAPS)))
    taps_flipped = jnp.pad(taps_all[:, ::-1], ((0, 0), (0, 2 * LANES - TAPS)))
    flat = lax.dynamic_index_in_dim(tokens, rank, axis=0, keepdims=False)
    upstream = lax.dynamic_index_in_dim(cotangent, rank, axis=0, keepdims=False)

    def shards(own, far):
        return (own, swap(own, "tp", 1), far, swap(far, "tp", 1))

    query_key = (query_key, first_core, first_far, swap(first_far, "tp", 1))
    value_far = swap(after(value_turned, first_far), "tp", 2)
    output_far = swap(after(output_weight, value_far), "tp", 2)
    up_far = swap(after(up_weight, output_far), "tp", 2)
    down_far = swap(after(down_weight, up_far), "tp", 2)
    value_blocks = shards(value_turned, value_far)
    output_blocks = shards(output_weight, output_far)
    up_blocks = shards(up_weight, up_far)
    down_blocks = shards(down_weight, down_far)

    query, keys, sums = [], [], []
    for pair in range(2):
        q, k, part, sent = call(
            query_key_kernel, (half, half, marked, message), "query_key",
            flops=2 * width * model * 768,
        )(
            flat,
            query_key[2 * pair],
            query_key[2 * pair + 1],
            query_bias_all[2 * pair : 2 * pair + 2],
            member_turned,
        )
        query.append(q)
        keys.append(k)
        sums += exchange(plain_parts(), "land", flags, part, sent)
    land_query, land_key, kernel = call(land_kernel, (message, message, squares), "land")(
        flags, count, *sums
    )
    values, value_head, value_tail = call(
        value_kernel, (full, edge, edge), "values", flops=2 * width * model * 768
    )(flat, *value_blocks, value_bias_all)

    def neighbours(head, tail):
        count = lax.axis_size("seq")
        before = lax.ppermute(tail, "seq", [(i, i + 1) for i in range(count - 1)])
        behind = lax.ppermute(head, "seq", [(i + 1, i) for i in range(count - 1)])
        return before, behind

    value_before, value_after = neighbours(value_head, value_tail)
    state, sent = call(
        key_kernel,
        (((marks, model + LANES), f32), ((marks, model + LANES), bf16)),
        "key_softmax",
        flops=4 * width * 768 * 192,
    )(*keys, values, land_query)
    state, state_got = exchange(soft_parts(heads), "soft", flags, state, sent)
    (token_weights,) = call(
        token_kernel, (((ranks, own_heads * marks, width), f32),), "token_softmax",
        flops=2 * width * 768 * 192,
    )(*query, land_key)
    inverse, inverse_back = jax.vjp(newton_inverse, kernel)
    context, mixed, mixed_low, stats = call(
        context_kernel, (full, marked, message, tall), "context", flops=6 * width * 768 * 192,
    )(
        state, state_got, inverse, token_weights, values, value_before, value_after, flags,
        taps_wide,
    )

    params = jnp.stack(
        (output_bias, first_gain, first_shift, down_bias, second_gain, second_shift)
    ).astype(f32)
    (
        layer_out,
        back_input,
        back_attention,
        back_context,
        active,
        back_hidden,
        first_low,
        back_feed,
        norm_sums,
        up_sums,
    ) = feed_layer(
        flat, context, output_blocks, up_blocks, down_blocks, up_bias_all[None, :], params, upstream
    )

    layer_far = swap(layer_out, "tp", 2)
    part_back, sent_back, part_key, sent_key, query_direct, back_head, back_tail = call(
        token_back_kernel, (marked, message, marked, message, full32, edge, edge), "token_back",
        flops=8 * width * 768 * 192,
    )(back_context, token_weights, mixed_low, *query, land_key)
    back_own, back_got = exchange(plain_parts(), "back", flags, part_back, sent_back)
    key_own, key_got = exchange(plain_parts(), "back_key", flags, part_key, sent_key)
    back_before, back_after = neighbours(back_head, back_tail)
    conv_back, tap_rows = call(
        conv_back_kernel, (full32, ((heads, 2 * LANES), f32)), "conv_back",
        flops=6 * width * 768 * 192,
    )(
        back_context, back_before, back_after, values, value_before, value_after, flags,
        taps_flipped,
    )
    conv_part = tap_rows[:, STRIPE - 1 : STRIPE - 1 + TAPS]
    units_of = functools.partial(group_of, channels=hidden_units)
    positions = lax.axis_size("seq")
    sizes = [1 << level for level in range(positions.bit_length() - 1)]
    down = scatter_start([outer(back_feed, units_of(active, r)).astype(bf16) for r in range(ranks)])
    up = scatter_start(
        [outer(first_low, units_of(back_hidden, r)).astype(bf16) for r in range(ranks)]
    )
    down = by_targets(scatter_far(down), positions)
    up = by_targets(up, positions)
    for size in sizes:
        up = scatter_level(up, device, size)
    for size in sizes:
        down = scatter_level(down, device, size, size == sizes[-1])
    grad_up_weight = scatter_far(up)[0][0].astype(f32)
    grad_down_weight = down[0][0]
    grad_up_bias = [units_of(up_sums, r)[0] for r in range(ranks)]

    back_inverse, back_mixed = call(seed_kernel, (squares, message), "seed")(
        flags, back_own, back_got, inverse, mixed
    )
    part_query, sent_query, key_direct, back_values, value_bias_sums = call(
        key_back_kernel, (marked, message, full32, full, ((ranks, channels), f32)), "key_back",
        flops=10 * width * 768 * 192,
    )(*keys, values, land_query, stats, mixed, back_mixed, conv_back)
    query_own, query_got = exchange(plain_parts(), "back_query", flags, part_query, sent_query)
    (back_kernel,) = inverse_back(back_inverse)
    pairs = (((model, 2 * channels), bf16),) * ranks
    value_output = call(value_output_kernel, pairs, "value_output", flops=4 * width * model * model)(
        flat, back_values, back_attention, context
    )
    value_output = by_targets(scatter_far(scatter_start(value_output)), positions)
    for size in sizes:
        value_output = scatter_level(value_output, device, size, size == sizes[-1])
    grad_output_weight = value_output[0][0][:, :channels].T
    grad_value_weight = value_output[0][0][:, channels:]
    grad_row, query_bias_sums, *projection = call(
        input_back_kernel,
        (((width, model), bf16), ((ranks, channels), f32)) + pairs,
        "input_back",
        scratch=(pltpu.VMEM((model, width), bf16),),
        flops=2 * width * 768 * 768 * 6,
        limit=32 << 20,
    )(
        flags, count, flat, query_direct, key_direct, back_values, query_own, query_got, key_own,
        key_got, kernel, back_kernel, land_query, land_key, member, back_input, *query_key,
        *value_blocks,
    )
    projection = by_targets(scatter_start(projection), positions)
    for size in sizes:
        projection = scatter_level(projection, device, size)
    projection = scatter_far(projection)[0][0].astype(f32)
    grad_far = swap(grad_row, "tp", 2)
    grad_tokens = place_rows(rank, shards(grad_row, grad_far), f32)
    layer_rows = place_rows(rank, shards(layer_out, layer_far), bf16)

    ranked = jnp.stack(
        [
            jnp.concatenate(
                (
                    grad_up_bias[r],
                    value_bias_sums[r],
                    query_bias_sums[r],
                    conv_part[r * own_heads : (r + 1) * own_heads].reshape(-1),
                )
            )
            for r in range(ranks)
        ]
    )
    ranked = by_rank(ranked)
    ranked_size = ranked.size
    shared = [norm_sums[k] for k in range(6)]
    bundle = jnp.concatenate([ranked.reshape(-1)] + shared)
    bundle = jnp.pad(bundle, (0, -bundle.shape[0] % (8 * LANES))).reshape(-1, LANES)
    bundle = sum_everywhere(bundle).reshape(-1)
    own_ranked = lax.dynamic_index_in_dim(
        bundle[:ranked_size].reshape(ranks, -1), rank, axis=0, keepdims=False
    )
    grad_up_bias = own_ranked[:hidden_units]
    at = hidden_units
    grad_value_bias = own_ranked[at : at + channels].reshape(own_heads, HEAD_DIM)
    at += channels
    share = HEAD_DIM // lax.axis_size("seq")
    grad_query_bias = lax.dynamic_slice_in_dim(
        own_ranked[at : at + channels].reshape(own_heads, HEAD_DIM), device * share, share, axis=1
    )
    at += channels
    grad_conv_weight = own_ranked[at : at + own_heads * TAPS].reshape(own_heads, TAPS)
    shared = [
        bundle[ranked_size + k * model : ranked_size + (k + 1) * model] for k in range(len(shared))
    ]
    return (
        layer_rows,
        grad_tokens,
        projection[:, :channels],
        grad_query_bias,
        projection[:, channels:],
        grad_value_weight,
        grad_value_bias,
        grad_conv_weight,
        grad_output_weight,
        shared[0],
        shared[1],
        shared[2],
        grad_up_weight,
        grad_up_bias,
        grad_down_weight.T,
        shared[3],
        shared[4],
        shared[5],
    )


def solution(mesh):
    placed = (
        P(None, "seq", None),
        P(None, "tp"),
        P("tp", None),
        P(None, "tp"),
        P(None, "tp"),
        P("tp", None),
        P("tp", None),
        P("tp", None),
        P(),
        P(),
        P(),
        P(None, "tp"),
        P("tp"),
        P("tp", None),
        P(),
        P(),
        P(),
        P(),
        P(None, "seq", None),
    )
    return jax.shard_map(
        per_device,
        mesh=mesh,
        in_specs=placed,
        out_specs=(
            P(None, "seq", None),
            P(None, "seq", None),
            P("seq", "tp"),
            P("tp", "seq"),
            P("seq", "tp"),
            P("seq", "tp"),
            P("tp", None),
            P("tp", None),
            P("tp", "seq"),
            P(),
            P(),
            P(),
            P("seq", "tp"),
            P("tp"),
            P("tp", "seq"),
            P(),
            P(),
            P(),
        ),
        check_vma=False,
    )
```

profile of v0, /device:TPU:0, one launch (start us, length us, event | category | flops | bytes accessed | tf_op | source)
XLA Modules:
  0.0 466.1 jit_solution(3527138676140594449)
XLA Ops:
  4.0 3.0 collective-permute-start.4
  11.8 2.1 dynamic-slice_bitcast_fusion.cotangent_ref
  17.4 7.6 %collective-permute-done.2.w0.w2 = bf16[384,768]{1,0:T(8,128)(2,1)} collective-permute-done((bf16[384,768]{1,0:T(8,128)(2,1)}, bf16[384,768]{1,0:T(8,128)(2,1)}, u32[]{:S(2)}, u32[]{:S(2)}) %collective-permute-start.2) | collective-permute-done | bytes 589856 | tf_op jit(solution)/shard_map/ppermute | solution.py:28
  27.4 2.7 query_key.2
  31.9 2.7 query_key.3
  43.8 2.7 collective-permute-start.11
  46.6 3.3 collective-permute-done.13.got_ref
  54.2 2.2 values.1
  73.3 13.0 %collective-permute-done.24.up2 = bf16[768,768]{1,0:T(8,128)(2,1)} collective-permute-done((bf16[768,768]{1,0:T(8,128)(2,1)}, bf16[768,768]{1,0:T(8,128)(2,1)}, u32[]{:S(2)}, u32[]{:S(2)}) %collective-permute-start.24) | collective-permute-done | bytes 1179680 | tf_op jit(solution)/shard_map/ppermute | solution.py:28
  93.7 2.6 collective-permute-start.18
  96.4 17.3 %collective-permute-done.27.down2 = bf16[768,768]{1,0:T(8,128)(2,1)S(1)} collective-permute-done((bf16[768,768]{1,0:T(8,128)(2,1)S(1)}, bf16[768,768]{1,0:T(8,128)(2,1)S(1)}, u32[]{:S(2)}, u32[]{:S(2)}) %collective-permute-start.27) | collective-permute-done | bytes 1179680 | tf_op jit(solution)/shard_map/ppermute | solution.py:28
  117.8 5.7 %collective-permute-done.16.got_ref = bf16[128,896]{1,0:T(8,128)(2,1)S(1)} collective-permute-done((bf16[128,896]{1,0:T(8,128)(2,1)S(1)}, bf16[128,896]{1,0:T(8,128)(2,1)S(1)}, u32[]{:S(2)}, u32[]{:S(2)}) %collective-permute-start.16) | collective-permute-done | bytes 229408 | tf_op jit(solution)/shard_map/ppermute | solution.py:28
  126.6 2.6 collective-permute-done.19.after_ref.vafter_ref
  129.2 2.2 collective-permute-start.17
  132.8 3.9 collective-permute-done.17.got_ref
  137.3 2.1 context.1
  141.6 34.9 %feed_layer.1 = (bf16[512,768]{1,0:T(8,128)(2,1)S(1)}, f32[512,768]{1,0:T(8,128)}, bf16[512,768]{1,0:T(8,128)(2,1)S(1)}, bf16[4,512,192]{2,1,0:T(8,128)(2,1)S(1)...) custom-call(bf16[512,768]{1,0:T(8,128)(2,1)S(1)} %copy-done.22, ...), custom_call_target="tpu_custom_call" | custom-call | flops 10871635968 | bytes 31457280 | tf_op jit(solution)/shard_map/feed_layer/pallas_call | solution.py:801
  176.5 3.7 convolution_convert_fusion
  187.7 4.0 collective-permute-start.35
  193.5 2.7 collective-permute-start.32
  196.3 3.0 convolution_convert_fusion.6
  202.2 2.8 conv_back.1
  213.0 2.2 collective-permute-done.41.got_ref
  258.6 2.3 key_back.1
  261.4 4.2 collective-permute-done.37.got_ref
  266.9 5.6 %collective-permute-done.38.got_ref = bf16[128,768]{1,0:T(8,128)(2,1)S(1)} collective-permute-done((bf16[128,768]{1,0:T(8,128)(2,1)S(1)}, bf16[128,768]{1,0:T(8,128)(2,1)S(1)}, u32[]{:S(2)}, u32[]{:S(2)}) %collective-permute-start.38) | collective-permute-done | bytes 196640 | tf_op jit(solution)/shard_map/ppermute | solution.py:28
  273.5 5.6 %collective-permute-done.39.query_got_ref = bf16[64,768]{1,0:T(8,128)(2,1)S(1)} collective-permute-done((bf16[64,768]{1,0:T(8,128)(2,1)S(1)}, bf16[64,768]{1,0:T(8,128)(2,1)S(1)}, u32[]{:S(2)}, u32[]{:S(2)}) %collective-permute-start.39) | collective-permute-done | bytes 98336 | tf_op jit(solution)/shard_map/ppermute | solution.py:28
  279.2 9.5 %input_back.1 = (bf16[512,768]{1,0:T(8,128)(2,1)S(1)}, f32[4,192]{1,0:T(4,128)S(1)}, bf16[768,384]{1,0:T(8,128)(2,1)S(1)}, bf16[768,384]{1,0:T(8,128)(2,1)S(1)},...) custom-call(f32[16,128]{1,0:T(8,128)S(1)} %get-tuple-element.106.flags_ref, f32[64,128]{1,0:T(8,128)S(1)} %copy-done.44, ...), custom_call_target="tpu_custom_call" | custom-call | flops 3623878656 | tf_op jit(solution)/shard_map/input_back/pallas_call | solution.py:169
  293.6 3.1 convolution_convert_fusion.7
  311.9 2.4 collective-permute-done.59
  318.0 7.1 %collective-permute-done.30.r2 = bf16[512,768]{1,0:T(8,128)(2,1)S(1)} collective-permute-done((bf16[512,768]{1,0:T(8,128)(2,1)S(1)}, bf16[512,768]{1,0:T(8,128)(2,1)S(1)}, u32[]{:S(2)}, u32[]{:S(2)}) %collective-permute-start.30) | collective-permute-done | bytes 786464 | tf_op jit(solution)/shard_map/ppermute | solution.py:28
  339.6 2.4 place_rows.2
  343.4 5.4 %collective-permute-done.62 = bf16[768,384]{1,0:T(8,128)(2,1)S(1)} collective-permute-done((bf16[768,384]{1,0:T(8,128)(2,1)S(1)}, bf16[768,384]{1,0:T(8,128)(2,1)S(1)}, u32[]{:S(2)}, u32[]{:S(2)}) %collective-permute-start.62) | collective-permute-done | bytes 589856 | tf_op jit(solution)/shard_map/ppermute | solution.py:28
  350.5 12.7 %collective-permute-done.47 = bf16[4,96,384]{2,1,0:T(8,128)(2,1)S(1)} collective-permute-done((bf16[4,96,384]{2,1,0:T(8,128)(2,1)S(1)}, bf16[4,96,384]{2,1,0:T(8,128)(2,1)S(1)}, u32[]{:S(2)}, u32[]{:S(2)}) %collective-permute-start.47) | collective-permute-done | bytes 294944 | tf_op jit(solution)/shard_map/ppermute | solution.py:28
  364.8 6.3 %collective-permute-done.51 = bf16[4,96,384]{2,1,0:T(8,128)(2,1)S(1)} collective-permute-done((bf16[4,96,384]{2,1,0:T(8,128)(2,1)S(1)}, bf16[4,96,384]{2,1,0:T(8,128)(2,1)S(1)}, u32[]{:S(2)}, u32[]{:S(2)}) %collective-permute-start.51) | collective-permute-done | bytes 294944 | tf_op jit(solution)/shard_map/ppermute | solution.py:28
  373.5 13.9 %collective-permute-done.71 = bf16[4,96,768]{2,1,0:T(8,128)(2,1)S(1)} collective-permute-done((bf16[4,96,768]{2,1,0:T(8,128)(2,1)S(1)}, bf16[4,96,768]{2,1,0:T(8,128)(2,1)S(1)}, u32[]{:S(2)}, u32[]{:S(2)}) %collective-permute-start.71) | collective-permute-done | bytes 589856 | tf_op jit(solution)/shard_map/ppermute | solution.py:28
  389.3 3.2 collective-permute-done.48
  394.3 4.1 collective-permute-done.52
  401.6 4.8 %collective-permute-done.53 = bf16[1,96,384]{2,1,0:T(8,128)(2,1)S(1)} collective-permute-done((bf16[1,96,384]{2,1,0:T(8,128)(2,1)S(1)}, bf16[1,96,384]{2,1,0:T(8,128)(2,1)S(1)}, u32[]{:S(2)}, u32[]{:S(2)}) %collective-permute-start.53) | collective-permute-done | bytes 73760 | tf_op jit(solution)/shard_map/ppermute | solution.py:28
  407.7 3.1 collective-permute-done.54
  411.9 5.6 %collective-permute-done.64 = bf16[2,96,384]{2,1,0:T(8,128)(2,1)S(1)} collective-permute-done((bf16[2,96,384]{2,1,0:T(8,128)(2,1)S(1)}, bf16[2,96,384]{2,1,0:T(8,128)(2,1)S(1)}, u32[]{:S(2)}, u32[]{:S(2)}) %collective-permute-start.64) | collective-permute-done | bytes 147488 | tf_op jit(solution)/shard_map/ppermute | solution.py:28
  418.0 10.0 %collective-permute-done.68 = bf16[2,96,768]{2,1,0:T(8,128)(2,1)S(1)} collective-permute-done((bf16[2,96,768]{2,1,0:T(8,128)(2,1)S(1)}, bf16[2,96,768]{2,1,0:T(8,128)(2,1)S(1)}, u32[]{:S(2)}, u32[]{:S(2)}) %collective-permute-start.68) | collective-permute-done | bytes 294944 | tf_op jit(solution)/shard_map/ppermute | solution.py:28
  428.0 2.5 collective-permute-start.65
  432.5 5.3 %collective-permute-done.72 = bf16[2,96,768]{2,1,0:T(8,128)(2,1)S(1)} collective-permute-done((bf16[2,96,768]{2,1,0:T(8,128)(2,1)S(1)}, bf16[2,96,768]{2,1,0:T(8,128)(2,1)S(1)}, u32[]{:S(2)}, u32[]{:S(2)}) %collective-permute-start.72) | collective-permute-done | bytes 294944 | tf_op jit(solution)/shard_map/ppermute | solution.py:28
  439.3 2.9 collective-permute-start.73
  446.4 3.6 collective-permute-done.73
  451.1 2.9 collective-permute-done.79
  461.9 3.2 place_rows.3
  (685 shorter events, 201.5 us)
Async XLA Ops:
  4.0 13.3 %collective-permute-start.4 = (bf16[16,768]{1,0:T(8,128)(2,1)S(1)}, bf16[16,768]{1,0:T(8,128)(2,1)S(1)}, u32[]{:S(2)}, u32[]{:S(2)}) collective-permute-start(bf16[16,768]{1,0:T(8,128)(2,1)S(1)} %reshape.259), channel_id=1, source_target_pairs={{0,2},{1,3},{2,0},{3,1},{4,6},{5,7},{6,4},{7,5},{8,10},{9,11},{10,... | collective-permute-start | bytes 73736 | tf_op jit(solution)/shard_map/ppermute | solution.py:28
  7.0 10.3 %collective-permute-start.1 = (bf16[16,768]{1,0:T(8,128)(2,1)S(1)}, bf16[16,768]{1,0:T(8,128)(2,1)S(1)}, u32[]{:S(2)}, u32[]{:S(2)}) collective-permute-start(bf16[16,768]{1,0:T(8,128)(2,1)S(1)} %reshape.259), channel_id=1, source_target_pairs={{0,1},{1,0},{2,3},{3,2},{4,5},{5,4},{6,7},{7,6},{8,9},{9,8},{10,11... | collective-permute-start | bytes 73736 | tf_op jit(solution)/shard_map/ppermute | solution.py:28
  8.9 16.1 %collective-permute-start.2 = (bf16[384,768]{1,0:T(8,128)(2,1)}, bf16[384,768]{1,0:T(8,128)(2,1)}, u32[]{:S(2)}, u32[]{:S(2)}) collective-permute-start(bf16[384,768]{1,0:T(8,128)(2,1)} %pad_maximum_fusion.w0), channel_id=1, source_target_pairs={{0,2},{1,3},{2,0},{3,1},{4,6},{5,7},{6,4},{7,5},{8,10},{9,11},{10,... | collective-permute-start | bytes 1769480 | tf_op jit(solution)/shard_map/ppermute | solution.py:28
  9.0 18.4 %collective-permute-start = (bf16[384,768]{1,0:T(8,128)(2,1)}, bf16[384,768]{1,0:T(8,128)(2,1)}, u32[]{:S(2)}, u32[]{:S(2)}) collective-permute-start(bf16[384,768]{1,0:T(8,128)(2,1)} %pad_maximum_fusion.w0), channel_id=1, source_target_pairs={{0,1},{1,0},{2,3},{3,2},{4,5},{5,4},{6,7},{7,6},{8,9},{9,8},{10,11... | collective-permute-start | bytes 1769480 | tf_op jit(solution)/shard_map/ppermute | solution.py:28
  9.4 42.9 %collective-permute-start.6 = (bf16[192,768]{1,0:T(8,128)(2,1)}, bf16[192,768]{1,0:T(8,128)(2,1)}, u32[]{:S(2)}, u32[]{:S(2)}) collective-permute-start(bf16[192,768]{1,0:T(8,128)(2,1)} %bitcast.10.w0.v0), channel_id=1, source_target_pairs={{0,1},{1,0},{2,3},{3,2},{4,5},{5,4},{6,7},{7,6},{8,9},{9,8},{10,11... | collective-permute-start | bytes 884744 | tf_op jit(solution)/shard_map/ppermute | solution.py:28
  27.1 11.6 %collective-permute-start.7 = (bf16[192,768]{1,0:T(8,128)(2,1)}, bf16[192,768]{1,0:T(8,128)(2,1)}, u32[]{:S(2)}, u32[]{:S(2)}) collective-permute-start(bf16[192,768]{1,0:T(8,128)(2,1)} %bitcast.10.w0.v0), channel_id=1, source_target_pairs={{0,2},{1,3},{2,0},{3,1},{4,6},{5,7},{6,4},{7,5},{8,10},{9,11},{10,... | collective-permute-start | bytes 884744 | tf_op jit(solution)/shard_map/ppermute | solution.py:28
  38.7 13.5 %collective-permute-start.21 = (bf16[192,768]{1,0:T(8,128)(2,1)}, bf16[192,768]{1,0:T(8,128)(2,1)S(1)}, u32[]{:S(2)}, u32[]{:S(2)}) collective-permute-start(bf16[192,768]{1,0:T(8,128)(2,1)} %out0.1), channel_id=1, source_target_pairs={{0,2},{1,3},{2,0},{3,1},{4,6},{5,7},{6,4},{7,5},{8,10},{9,11},{10,... | collective-permute-start | bytes 884744 | tf_op jit(solution)/shard_map/ppermute | solution.py:28
  40.2 12.6 %collective-permute-start.8 = (bf16[192,768]{1,0:T(8,128)(2,1)}, bf16[192,768]{1,0:T(8,128)(2,1)S(1)}, u32[]{:S(2)}, u32[]{:S(2)}) collective-permute-start(bf16[192,768]{1,0:T(8,128)(2,1)} %collective-permute-done.7.w2.v2), channel_id=1, source_target_pairs={{0,1},{1,0},{2,3},{3,2},{4,5},{5,4},{6,7},{7,6},{8,9},{9,8},{10,11... | collective-permute-start | bytes 884744 | tf_op jit(solution)/shard_map/ppermute | solution.py:28
  40.3 9.5 %collective-permute-start.13 = (bf16[128,768]{1,0:T(8,128)(2,1)S(1)}, bf16[128,768]{1,0:T(8,128)(2,1)S(1)}, u32[]{:S(2)}, u32[]{:S(2)}) collective-permute-start(bf16[128,768]{1,0:T(8,128)(2,1)S(1)} %get-tuple-element.122.sent_ref), channel_id=1, source_target_pairs={{0,8},{4,12},{8,0},{12,4},{16,24},{20,28},{24,16},{28,20},{1,9},{5... | collective-permute-start | bytes 589832 | tf_op jit(solution)/shard_map/ppermute | solution.py:28
  43.8 13.9 %collective-permute-start.11 = (bf16[64,768]{1,0:T(8,128)(2,1)}, bf16[64,768]{1,0:T(8,128)(2,1)S(1)}, u32[]{:S(2)}, u32[]{:S(2)}) collective-permute-start(bf16[64,768]{1,0:T(8,128)(2,1)} %get-tuple-element.118), channel_id=1, source_target_pairs={{0,16},{4,20},{8,24},{12,28},{16,0},{20,4},{24,8},{28,12},{1,17},{... | collective-permute-start | bytes 294920 | tf_op jit(solution)/shard_map/ppermute | solution.py:28
  52.2 87.8 %collective-permute-start.23 = (bf16[768,768]{1,0:T(8,128)(2,1)}, bf16[768,768]{1,0:T(8,128)(2,1)}, u32[]{:S(2)}, u32[]{:S(2)}) collective-permute-start(bf16[768,768]{1,0:T(8,128)(2,1)} %up0.1), channel_id=1, source_target_pairs={{0,1},{1,0},{2,3},{3,2},{4,5},{5,4},{6,7},{7,6},{8,9},{9,8},{10,11... | collective-permute-start | bytes 3538952 | tf_op jit(solution)/shard_map/ppermute | solution.py:28
  52.3 41.3 %collective-permute-start.20 = (bf16[192,768]{1,0:T(8,128)(2,1)}, bf16[192,768]{1,0:T(8,128)(2,1)}, u32[]{:S(2)}, u32[]{:S(2)}) collective-permute-start(bf16[192,768]{1,0:T(8,128)(2,1)} %out0.1), channel_id=1, source_target_pairs={{0,1},{1,0},{2,3},{3,2},{4,5},{5,4},{6,7},{7,6},{8,9},{9,8},{10,11... | collective-permute-start | bytes 884744 | tf_op jit(solution)/shard_map/ppermute | solution.py:28
  53.0 87.1 %collective-permute-start.26 = (bf16[768,768]{1,0:T(8,128)(2,1)}, bf16[768,768]{1,0:T(8,128)(2,1)}, u32[]{:S(2)}, u32[]{:S(2)}) collective-permute-start(bf16[768,768]{1,0:T(8,128)(2,1)} %down0.1), channel_id=1, source_target_pairs={{0,1},{1,0},{2,3},{3,2},{4,5},{5,4},{6,7},{7,6},{8,9},{9,8},{10,11... | collective-permute-start | bytes 3538952 | tf_op jit(solution)/shard_map/ppermute | solution.py:28
  57.7 28.6 %collective-permute-start.24 = (bf16[768,768]{1,0:T(8,128)(2,1)}, bf16[768,768]{1,0:T(8,128)(2,1)}, u32[]{:S(2)}, u32[]{:S(2)}) collective-permute-start(bf16[768,768]{1,0:T(8,128)(2,1)} %up0.1), channel_id=1, source_target_pairs={{0,2},{1,3},{2,0},{3,1},{4,6},{5,7},{6,4},{7,5},{8,10},{9,11},{10,... | collective-permute-start | bytes 3538952 | tf_op jit(solution)/shard_map/ppermute | solution.py:28
  86.2 27.4 %collective-permute-start.27 = (bf16[768,768]{1,0:T(8,128)(2,1)S(1)}, bf16[768,768]{1,0:T(8,128)(2,1)S(1)}, u32[]{:S(2)}, u32[]{:S(2)}) collective-permute-start(bf16[768,768]{1,0:T(8,128)(2,1)S(1)} %copy-done.152), channel_id=1, source_target_pairs={{0,2},{1,3},{2,0},{3,1},{4,6},{5,7},{6,4},{7,5},{8,10},{9,11},{10,... | collective-permute-start | bytes 3538952 | tf_op jit(solution)/shard_map/ppermute | solution.py:28
  93.7 21.5 %collective-permute-start.18 = (bf16[16,768]{1,0:T(8,128)(2,1)S(1)}, bf16[16,768]{1,0:T(8,128)(2,1)S(1)}, u32[]{:S(2)}, u32[]{:S(2)}) collective-permute-start(bf16[16,768]{1,0:T(8,128)(2,1)S(1)} %copy-done.69), channel_id=1, source_target_pairs={{0,4},{4,8},{8,12},{12,16},{16,20},{20,24},{24,28},{1,5},{5,9},{9,... | collective-permute-start | bytes 73736 | tf_op jit(solution)/shard_map/ppermute | solution.py:953
  96.4 43.7 %collective-permute-start.25 = (bf16[768,768]{1,0:T(8,128)(2,1)}, bf16[768,768]{1,0:T(8,128)(2,1)S(1)}, u32[]{:S(2)}, u32[]{:S(2)}) collective-permute-start(bf16[768,768]{1,0:T(8,128)(2,1)} %collective-permute-done.24.up2), channel_id=1, source_target_pairs={{0,1},{1,0},{2,3},{3,2},{4,5},{5,4},{6,7},{7,6},{8,9},{9,8},{10,11... | collective-permute-start | bytes 3538952 | tf_op jit(solution)/shard_map/ppermute | solution.py:28
  113.7 26.5 %collective-permute-start.28 = (bf16[768,768]{1,0:T(8,128)(2,1)S(1)}, bf16[768,768]{1,0:T(8,128)(2,1)S(1)}, u32[]{:S(2)}, u32[]{:S(2)}) collective-permute-start(bf16[768,768]{1,0:T(8,128)(2,1)S(1)} %collective-permute-done.27.down2), channel_id=1, source_target_pairs={{0,1},{1,0},{2,3},{3,2},{4,5},{5,4},{6,7},{7,6},{8,9},{9,8},{10,11... | collective-permute-start | bytes 3538952 | tf_op jit(solution)/shard_map/ppermute | solution.py:28
  187.7 14.4 %collective-permute-start.35 = (bf16[16,768]{1,0:T(8,128)(2,1)S(1)}, bf16[16,768]{1,0:T(8,128)(2,1)S(1)}, u32[]{:S(2)}, u32[]{:S(2)}) collective-permute-start(bf16[16,768]{1,0:T(8,128)(2,1)S(1)} %get-tuple-element.155), channel_id=1, source_target_pairs={{0,4},{4,8},{8,12},{12,16},{16,20},{20,24},{24,28},{1,5},{5,9},{9,... | collective-permute-start | bytes 73736 | tf_op jit(solution)/shard_map/ppermute | solution.py:953
  191.7 10.4 %collective-permute-start.36 = (bf16[16,768]{1,0:T(8,128)(2,1)S(1)}, bf16[16,768]{1,0:T(8,128)(2,1)S(1)}, u32[]{:S(2)}, u32[]{:S(2)}) collective-permute-start(bf16[16,768]{1,0:T(8,128)(2,1)S(1)} %get-tuple-element.156), channel_id=1, source_target_pairs={{4,0},{8,4},{12,8},{16,12},{20,16},{24,20},{28,24},{5,1},{9,5},{13... | collective-permute-start | bytes 73736 | tf_op jit(solution)/shard_map/ppermute | solution.py:954
  196.2 10.2 %collective-permute-start.40 = (bf16[64,768]{1,0:T(8,128)(2,1)S(1)}, bf16[64,768]{1,0:T(8,128)(2,1)S(1)}, u32[]{:S(2)}, u32[]{:S(2)}) collective-permute-start(bf16[64,768]{1,0:T(8,128)(2,1)S(1)} %get-tuple-element.167), channel_id=1, source_target_pairs={{0,4},{4,0},{8,12},{12,8},{16,20},{20,16},{24,28},{28,24},{1,5},{5... | collective-permute-start | bytes 294920 | tf_op jit(solution)/shard_map/ppermute | solution.py:28
  208.5 10.0 %collective-permute-start.34 = (bf16[64,768]{1,0:T(8,128)(2,1)}, bf16[64,768]{1,0:T(8,128)(2,1)S(1)}, u32[]{:S(2)}, u32[]{:S(2)}) collective-permute-start(bf16[64,768]{1,0:T(8,128)(2,1)} %get-tuple-element.153), channel_id=1, source_target_pairs={{0,16},{4,20},{8,24},{12,28},{16,0},{20,4},{24,8},{28,12},{1,17},{... | collective-permute-start | bytes 294920 | tf_op jit(solution)/shard_map/ppermute | solution.py:28
  217.3 56.1 %collective-permute-start.42 = (bf16[64,768]{1,0:T(8,128)(2,1)S(1)}, bf16[64,768]{1,0:T(8,128)(2,1)S(1)}, u32[]{:S(2)}, u32[]{:S(2)}) collective-permute-start(bf16[64,768]{1,0:T(8,128)(2,1)S(1)} %get-tuple-element.171), channel_id=1, source_target_pairs={{0,16},{4,20},{8,24},{12,28},{16,0},{20,4},{24,8},{28,12},{1,17},{... | collective-permute-start | bytes 294920 | tf_op jit(solution)/shard_map/ppermute | solution.py:28
  303.3 21.9 %collective-permute-start.76 = (bf16[768,768]{1,0:T(8,128)(2,1)}, bf16[768,768]{1,0:T(8,128)(2,1)}, u32[]{:S(2)}, u32[]{:S(2)}) collective-permute-start(bf16[768,768]{1,0:T(8,128)(2,1)} %convolution_convert_fusion), channel_id=1, source_target_pairs={{0,1},{1,0},{2,3},{3,2},{4,5},{5,4},{6,7},{7,6},{8,9},{9,8},{10,11... | collective-permute-start | bytes 3538952 | tf_op jit(solution)/shard_map/ppermute | solution.py:28
  306.8 18.4 %collective-permute-start.30 = (bf16[512,768]{1,0:T(8,128)(2,1)S(1)}, bf16[512,768]{1,0:T(8,128)(2,1)S(1)}, u32[]{:S(2)}, u32[]{:S(2)}) collective-permute-start(bf16[512,768]{1,0:T(8,128)(2,1)S(1)} %copy-done.9), channel_id=1, source_target_pairs={{0,2},{1,3},{2,0},{3,1},{4,6},{5,7},{6,4},{7,5},{8,10},{9,11},{10,... | collective-permute-start | bytes 2359304 | tf_op jit(solution)/shard_map/ppermute | solution.py:28
  308.0 27.5 %collective-permute-start.29 = (bf16[512,768]{1,0:T(8,128)(2,1)S(1)}, bf16[512,768]{1,0:T(8,128)(2,1)S(1)}, u32[]{:S(2)}, u32[]{:S(2)}) collective-permute-start(bf16[512,768]{1,0:T(8,128)(2,1)S(1)} %copy-done.9), channel_id=1, source_target_pairs={{0,1},{1,0},{2,3},{3,2},{4,5},{5,4},{6,7},{7,6},{8,9},{9,8},{10,11... | collective-permute-start | bytes 2359304 | tf_op jit(solution)/shard_map/ppermute | solution.py:28
  308.9 18.7 %collective-permute-start.66 = (bf16[768,768]{1,0:T(8,128)(2,1)}, bf16[768,768]{1,0:T(8,128)(2,1)}, u32[]{:S(2)}, u32[]{:S(2)}) collective-permute-start(bf16[768,768]{1,0:T(8,128)(2,1)} %convolution_convert_fusion.6), channel_id=1, source_target_pairs={{0,1},{1,0},{2,3},{3,2},{4,5},{5,4},{6,7},{7,6},{8,9},{9,8},{10,11... | collective-permute-start | bytes 3538952 | tf_op jit(solution)/shard_map/ppermute | solution.py:28
  314.4 15.1 %collective-permute-start.70 = (bf16[768,768]{1,0:T(8,128)(2,1)}, bf16[768,768]{1,0:T(8,128)(2,1)}, u32[]{:S(2)}, u32[]{:S(2)}) collective-permute-start(bf16[768,768]{1,0:T(8,128)(2,1)} %convolution_convert_fusion.4), channel_id=1, source_target_pairs={{0,1},{1,0},{2,3},{3,2},{4,5},{5,4},{6,7},{7,6},{8,9},{9,8},{10,11... | collective-permute-start | bytes 3538952 | tf_op jit(solution)/shard_map/ppermute | solution.py:28
  325.2 16.7 %collective-permute-start.60 = (bf16[768,384]{1,0:T(8,128)(2,1)}, bf16[768,384]{1,0:T(8,128)(2,1)S(1)}, u32[]{:S(2)}, u32[]{:S(2)}) collective-permute-start(bf16[768,384]{1,0:T(8,128)(2,1)} %copy-done.59), channel_id=1, source_target_pairs={{0,1},{1,0},{2,3},{3,2},{4,5},{5,4},{6,7},{7,6},{8,9},{9,8},{10,11... | collective-permute-start | bytes 1769480 | tf_op jit(solution)/shard_map/ppermute | solution.py:28
  325.2 12.0 %collective-permute-start.31 = (bf16[512,768]{1,0:T(8,128)(2,1)S(1)}, bf16[512,768]{1,0:T(8,128)(2,1)S(1)}, u32[]{:S(2)}, u32[]{:S(2)}) collective-permute-start(bf16[512,768]{1,0:T(8,128)(2,1)S(1)} %collective-permute-done.30.r2), channel_id=1, source_target_pairs={{0,1},{1,0},{2,3},{3,2},{4,5},{5,4},{6,7},{7,6},{8,9},{9,8},{10,11... | collective-permute-start | bytes 2359304 | tf_op jit(solution)/shard_map/ppermute | solution.py:28
  332.6 16.2 %collective-permute-start.62 = (bf16[768,384]{1,0:T(8,128)(2,1)S(1)}, bf16[768,384]{1,0:T(8,128)(2,1)S(1)}, u32[]{:S(2)}, u32[]{:S(2)}) collective-permute-start(bf16[768,384]{1,0:T(8,128)(2,1)S(1)} %copy-done.131), channel_id=1, source_target_pairs={{0,2},{1,3},{2,0},{3,1},{4,6},{5,7},{6,4},{7,5},{8,10},{9,11},{10,... | collective-permute-start | bytes 1769480 | tf_op jit(solution)/shard_map/ppermute | solution.py:28
  335.1 92.9 %collective-permute-start.75 = (bf16[768,768]{1,0:T(8,128)(2,1)S(1)}, bf16[768,768]{1,0:T(8,128)(2,1)S(1)}, u32[]{:S(2)}, u32[]{:S(2)}) collective-permute-start(bf16[768,768]{1,0:T(8,128)(2,1)S(1)} %copy-done.153), channel_id=1, source_target_pairs={{0,1},{1,0},{2,3},{3,2},{4,5},{5,4},{6,7},{7,6},{8,9},{9,8},{10,11... | collective-permute-start | bytes 3538952 | tf_op jit(solution)/shard_map/ppermute | solution.py:28
  336.4 70.8 %collective-permute-start.44 = (bf16[512,768]{1,0:T(8,128)(2,1)S(1)}, bf16[512,768]{1,0:T(8,128)(2,1)S(1)}, u32[]{:S(2)}, u32[]{:S(2)}) collective-permute-start(bf16[512,768]{1,0:T(8,128)(2,1)S(1)} %get-tuple-element.175.r0), channel_id=1, source_target_pairs={{0,2},{1,3},{2,0},{3,1},{4,6},{5,7},{6,4},{7,5},{8,10},{9,11},{10,... | collective-permute-start | bytes 2359304 | tf_op jit(solution)/shard_map/ppermute | solution.py:28
  337.2 93.3 %collective-permute-start.77 = (bf16[768,768]{1,0:T(8,128)(2,1)S(1)}, bf16[768,768]{1,0:T(8,128)(2,1)S(1)}, u32[]{:S(2)}, u32[]{:S(2)}) collective-permute-start(bf16[768,768]{1,0:T(8,128)(2,1)S(1)} %add_convert_fusion.1), channel_id=1, source_target_pairs={{0,2},{1,3},{2,0},{3,1},{4,6},{5,7},{6,4},{7,5},{8,10},{9,11},{10,... | collective-permute-start | bytes 3538952 | tf_op jit(solution)/shard_map/ppermute | solution.py:28
  341.9 30.7 %collective-permute-start.67 = (bf16[4,96,768]{2,1,0:T(8,128)(2,1)S(1)}, bf16[4,96,768]{2,1,0:T(8,128)(2,1)S(1)}, u32[]{:S(2)}, u32[]{:S(2)}) collective-permute-start(bf16[4,96,768]{2,1,0:T(8,128)(2,1)S(1)} %dynamic-slice_bitcast_fusion.4), channel_id=1, source_target_pairs={{0,4},{4,0},{8,12},{12,8},{16,20},{20,16},{24,28},{28,24},{1,5},{5... | collective-permute-start | bytes 1769480 | tf_op jit(solution)/shard_map/ppermute | solution.py:28
  348.8 14.5 %collective-permute-start.47 = (bf16[4,96,384]{2,1,0:T(8,128)(2,1)S(1)}, bf16[4,96,384]{2,1,0:T(8,128)(2,1)S(1)}, u32[]{:S(2)}, u32[]{:S(2)}) collective-permute-start(bf16[4,96,384]{2,1,0:T(8,128)(2,1)S(1)} %dynamic-slice_bitcast_fusion.10), channel_id=1, source_target_pairs={{0,4},{4,0},{8,12},{12,8},{16,20},{20,16},{24,28},{28,24},{1,5},{5... | collective-permute-start | bytes 884744 | tf_op jit(solution)/shard_map/ppermute | solution.py:28
  371.1 16.3 %collective-permute-start.71 = (bf16[4,96,768]{2,1,0:T(8,128)(2,1)S(1)}, bf16[4,96,768]{2,1,0:T(8,128)(2,1)S(1)}, u32[]{:S(2)}, u32[]{:S(2)}) collective-permute-start(bf16[4,96,768]{2,1,0:T(8,128)(2,1)S(1)} %dynamic-slice_bitcast_fusion.3), channel_id=1, source_target_pairs={{0,4},{4,0},{8,12},{12,8},{16,20},{20,16},{24,28},{28,24},{1,5},{5... | collective-permute-start | bytes 1769480 | tf_op jit(solution)/shard_map/ppermute | solution.py:28
  372.7 27.6 %collective-permute-start.63 = (bf16[4,96,384]{2,1,0:T(8,128)(2,1)S(1)}, bf16[4,96,384]{2,1,0:T(8,128)(2,1)S(1)}, u32[]{:S(2)}, u32[]{:S(2)}) collective-permute-start(bf16[4,96,384]{2,1,0:T(8,128)(2,1)S(1)} %dynamic-slice_bitcast_fusion.8), channel_id=1, source_target_pairs={{0,4},{4,0},{8,12},{12,8},{16,20},{20,16},{24,28},{28,24},{1,5},{5... | collective-permute-start | bytes 884744 | tf_op jit(solution)/shard_map/ppermute | solution.py:28
  407.2 50.7 %collective-permute-start.43 = (bf16[512,768]{1,0:T(8,128)(2,1)S(1)}, bf16[512,768]{1,0:T(8,128)(2,1)S(1)}, u32[]{:S(2)}, u32[]{:S(2)}) collective-permute-start(bf16[512,768]{1,0:T(8,128)(2,1)S(1)} %get-tuple-element.175.r0), channel_id=1, source_target_pairs={{0,1},{1,0},{2,3},{3,2},{4,5},{5,4},{6,7},{7,6},{8,9},{9,8},{10,11... | collective-permute-start | bytes 2359304 | tf_op jit(solution)/shard_map/ppermute | solution.py:28
  407.3 51.5 %collective-permute-start.45 = (bf16[512,768]{1,0:T(8,128)(2,1)S(1)}, bf16[512,768]{1,0:T(8,128)(2,1)S(1)}, u32[]{:S(2)}, u32[]{:S(2)}) collective-permute-start(bf16[512,768]{1,0:T(8,128)(2,1)S(1)} %collective-permute-done.44.r2), channel_id=1, source_target_pairs={{0,1},{1,0},{2,3},{3,2},{4,5},{5,4},{6,7},{7,6},{8,9},{9,8},{10,11... | collective-permute-start | bytes 2359304 | tf_op jit(solution)/shard_map/ppermute | solution.py:28
  417.6 10.3 %collective-permute-start.68 = (bf16[2,96,768]{2,1,0:T(8,128)(2,1)S(1)}, bf16[2,96,768]{2,1,0:T(8,128)(2,1)S(1)}, u32[]{:S(2)}, u32[]{:S(2)}) collective-permute-start(bf16[2,96,768]{2,1,0:T(8,128)(2,1)S(1)} %dynamic-slice_bitcast_fusion.7), channel_id=1, source_target_pairs={{0,8},{4,12},{8,0},{12,4},{16,24},{20,28},{24,16},{28,20},{1,9},{5... | collective-permute-start | bytes 884744 | tf_op jit(solution)/shard_map/ppermute | solution.py:28
  427.9 9.9 %collective-permute-start.72 = (bf16[2,96,768]{2,1,0:T(8,128)(2,1)S(1)}, bf16[2,96,768]{2,1,0:T(8,128)(2,1)S(1)}, u32[]{:S(2)}, u32[]{:S(2)}) collective-permute-start(bf16[2,96,768]{2,1,0:T(8,128)(2,1)S(1)} %dynamic-slice_bitcast_fusion.6), channel_id=1, source_target_pairs={{0,8},{4,12},{8,0},{12,4},{16,24},{20,28},{24,16},{28,20},{1,9},{5... | collective-permute-start | bytes 884744 | tf_op jit(solution)/shard_map/ppermute | solution.py:28
  428.0 11.3 %collective-permute-start.65 = (bf16[1,96,384]{2,1,0:T(8,128)(2,1)S(1)}, bf16[1,96,384]{2,1,0:T(8,128)(2,1)S(1)}, u32[]{:S(2)}, u32[]{:S(2)}) collective-permute-start(bf16[1,96,384]{2,1,0:T(8,128)(2,1)S(1)} %constant_dynamic-slice_fusion.3), channel_id=1, source_target_pairs={{0,16},{4,20},{8,24},{12,28},{16,0},{20,4},{24,8},{28,12},{1,17},{... | collective-permute-start | bytes 221192 | tf_op jit(solution)/shard_map/ppermute | solution.py:28
  431.1 11.2 %collective-permute-start.78 = (bf16[4,96,768]{2,1,0:T(8,128)(2,1)S(1)}, bf16[4,96,768]{2,1,0:T(8,128)(2,1)S(1)}, u32[]{:S(2)}, u32[]{:S(2)}) collective-permute-start(bf16[4,96,768]{2,1,0:T(8,128)(2,1)S(1)} %dynamic-slice_bitcast_fusion.2), channel_id=1, source_target_pairs={{0,4},{4,0},{8,12},{12,8},{16,20},{20,16},{24,28},{28,24},{1,5},{5... | collective-permute-start | bytes 1769480 | tf_op jit(solution)/shard_map/ppermute | solution.py:28
  437.8 17.4 %collective-permute-start.69 = (bf16[1,96,768]{2,1,0:T(8,128)(2,1)}, bf16[1,96,768]{2,1,0:T(8,128)(2,1)}, u32[]{:S(2)}, u32[]{:S(2)}) collective-permute-start(bf16[1,96,768]{2,1,0:T(8,128)(2,1)} %constant_dynamic-slice_fusion.2), channel_id=1, source_target_pairs={{0,16},{4,20},{8,24},{12,28},{16,0},{20,4},{24,8},{28,12},{1,17},{... | collective-permute-start | bytes 442376 | tf_op jit(solution)/shard_map/ppermute | solution.py:28
  439.3 10.7 %collective-permute-start.73 = (bf16[1,96,768]{2,1,0:T(8,128)(2,1)}, bf16[1,96,768]{2,1,0:T(8,128)(2,1)}, u32[]{:S(2)}, u32[]{:S(2)}) collective-permute-start(bf16[1,96,768]{2,1,0:T(8,128)(2,1)} %constant_dynamic-slice_fusion.1), channel_id=1, source_target_pairs={{0,16},{4,20},{8,24},{12,28},{16,0},{20,4},{24,8},{28,12},{1,17},{... | collective-permute-start | bytes 442376 | tf_op jit(solution)/shard_map/ppermute | solution.py:28
  444.9 9.1 %collective-permute-start.79 = (bf16[2,96,768]{2,1,0:T(8,128)(2,1)}, bf16[2,96,768]{2,1,0:T(8,128)(2,1)}, u32[]{:S(2)}, u32[]{:S(2)}) collective-permute-start(bf16[2,96,768]{2,1,0:T(8,128)(2,1)} %dynamic-slice_bitcast_fusion.5), channel_id=1, source_target_pairs={{0,8},{4,12},{8,0},{12,4},{16,24},{20,28},{24,16},{28,20},{1,9},{5... | collective-permute-start | bytes 884744 | tf_op jit(solution)/shard_map/ppermute | solution.py:28
  455.2 9.9 %collective-permute-start.80 = (bf16[1,96,768]{2,1,0:T(8,128)(2,1)S(1)}, bf16[1,96,768]{2,1,0:T(8,128)(2,1)S(1)}, u32[]{:S(2)}, u32[]{:S(2)}) collective-permute-start(bf16[1,96,768]{2,1,0:T(8,128)(2,1)S(1)} %constant_dynamic-slice_fusion), channel_id=1, source_target_pairs={{0,16},{4,20},{8,24},{12,28},{16,0},{20,4},{24,8},{28,12},{1,17},{... | collective-permute-start | bytes 442376 | tf_op jit(solution)/shard_map/ppermute | solution.py:28
  (194 other events, 1390.6 us)
where the time goes:
time: 476 us; the launch traced here: 466 us
  waiting for transfers between devices  169 us (36%)
  Pallas kernels  79.7 us (17%)
  starting transfers between devices  74.6 us (16%)
  matrix products  71.4 us (15%)
  local copies, waits for them, and re-layouts  47.8 us (10%)
  other arithmetic  20.3 us (4%)
    ppermute x77, waiting for transfers between devices, swap(): lax.ppermute(value, axis, [(i, i ^ step) for i in range(lax.axis_size(axi...  166 us
    ppermute x77, starting transfers between devices, swap(): lax.ppermute(value, axis, [(i, i ^ step) for i in range(lax.axis_size(axi...  64.9 us
    pallas_call x26, Pallas kernels, run(): pl.pallas_call(kernel, out_shape=outs, in_specs=[pl.BlockSpec(memory_spac...  39.3 us
    pallas_call x1, Pallas kernels, feed_layer(): pl.pallas_call(feed_kernel, out_shape=(shape((width, model), bf16), shape...  34.9 us
    unnamed x323, local copies, waits for them, and re-layouts  27.3 us
    dot_general x8, matrix products, outer(): lax.dot_general(a, b, (((0,), (0,)), ((), ())), preferred_element_type=f32)  19.1 us
    dot_general x18, matrix products, newton_inverse(): inner = 15.0 * identity - jnp.matmul(product, inner, precision=highest)  13.8 us
    dot_general x18, matrix products, newton_inverse(): product = jnp.matmul(kernel, inverse, precision=highest)  12.9 us
  transfers between devices with their start and end apart: 81, of which 34 were waited for; matrix products, arithmetic and copies ran while one was open for 21% of the time, Pallas kernels for 7%

commit v1 on v0

--- a/solution.py
+++ b/solution.py
@@ -17,7 +17,6 @@
 VMEM_LIMIT = 44 << 20
 
 
-highest = lax.Precision.HIGHEST
 epsilon = 1e-05
 very_negative = -1e30
 f32 = jnp.float32
@@ -118,7 +117,7 @@
     message_ref[...] = encode(facing)
 
 
-def exchange(parts, name, flags, own, message):
+def exchange(parts, name, flags, own, message, waits=((), ())):
     marks, width = own.shape
     first = call(
         functools.partial(merge_first_kernel, parts),
@@ -130,8 +129,8 @@
         (((marks, width), f32), ((marks, width), bf16)),
         name + "_next",
     )
-    own, sent = first(flags, own, swap(message, "seq", 1))
-    own, message = following(flags, own, sent, swap(sent, "seq", 2))
+    own, sent = first(flags, after(own, *waits[0]), swap(message, "seq", 1))
+    own, message = following(flags, after(own, *waits[1]), sent, swap(sent, "seq", 2))
     return own, swap(message, "seq", 4)
 
 
@@ -144,25 +143,14 @@
     return value
 
 
-def newton_inverse(kernel):
-    size = kernel.shape[-1]
-    column_sums = jnp.sum(kernel, axis=-2)
-    bound = jnp.sqrt(jnp.sum(column_sums * column_sums, axis=-1))[..., None, None]
-    identity = jnp.eye(size, dtype=kernel.dtype)
-    inverse = jnp.swapaxes(kernel, -1, -2) / bound
-    for sweep in range(SWEEPS):
-        product = jnp.matmul(kernel, inverse, precision=highest)
-        inner = 7.0 * identity - product
-        inner = 15.0 * identity - jnp.matmul(product, inner, precision=highest)
-        inner = 13.0 * identity - jnp.matmul(product, inner, precision=highest)
-        inverse = 0.25 * jnp.matmul(inverse, inner, precision=highest)
-    return inverse
-
-
 WHOLE = pl.BlockSpec(memory_space=pltpu.VMEM)
 
 
-def call(kernel, outs, name, scratch=(), limit=24 << 20, flops=0, moved=0, scalars=0):
+def cost(us):
+    return pl.CostEstimate(flops=0, bytes_accessed=int(us * 3.3e6), transcendentals=0)
+
+
+def call(kernel, outs, name, scratch=(), limit=24 << 20, us=1.0, scalars=0):
     outs = tuple(jax.ShapeDtypeStruct(shape, dtype) for shape, dtype in outs)
 
     def run(*operands):
@@ -174,7 +162,7 @@
             out_specs=(WHOLE,) * len(outs),
             scratch_shapes=list(scratch),
             compiler_params=pltpu.CompilerParams(vmem_limit_bytes=limit),
-            cost_estimate=pl.CostEstimate(flops=flops, bytes_accessed=moved, transcendentals=0),
+            cost_estimate=cost(us),
             name=name,
         )(*operands)
 
@@ -210,22 +198,142 @@
     return high, (value - high.astype(f32)).astype(bf16)
 
 
-def dot_fine(a, b):
+def first_half(shape):
+    return lane_ids(shape) < HEAD_DIM
+
+
+def pair_spread(pair):
+    near = first_half(pair.shape)
+    zero = jnp.zeros_like(pair)
+    return jnp.concatenate((jnp.where(near, pair, zero), jnp.where(near, zero, pair)), axis=0)
+
+
+def pair_gather(square):
+    top, bottom = square[:HEAD_DIM], square[HEAD_DIM:]
+    return jnp.where(first_half(top.shape), top, bottom)
+
+
+def fine(product, a, b, turn=lambda value: value):
     a_high, a_low = two_parts(a)
-    b_high, b_low = two_parts(b)
-    return dot(a_high, b_high) + (dot(a_high, b_low) + dot(a_low, b_high))
-
-
-def dot_fine_t(a, b):
-    a_high, a_low = two_parts(a)
-    b_high, b_low = two_parts(b)
-    return dot_t(a_high, b_high) + (dot_t(a_high, b_low) + dot_t(a_low, b_high))
-
-
-def outer_fine(a, b):
-    a_high, a_low = two_parts(a)
-    b_high, b_low = two_parts(b)
-    return outer(a_high, b_high) + (outer(a_high, b_low) + outer(a_low, b_high))
+    b_high, b_low = [turn(part) for part in two_parts(b)]
+    return product(a_high, b_high) + (product(a_high, b_low) + product(a_low, b_high))
+
+
+def pair_mul(a, b):
+    return fine(dot, a, b, pair_spread)
+
+
+def pair_mul_t(a, b):
+    return fine(dot_t, a, b, pair_spread)
+
+
+def pair_t_mul(a, b):
+    return pair_gather(fine(outer, a, b))
+
+
+def pair_sums(value, reduce=jnp.sum, neutral=0.0):
+    near = first_half(value.shape)
+    left = reduce(jnp.where(near, value, neutral), axis=1, keepdims=True)
+    right = reduce(jnp.where(near, neutral, value), axis=1, keepdims=True)
+    return jnp.where(near, left, right)
+
+
+def pair_of(array, pair):
+    return array[:, pair * LANES : (pair + 1) * LANES]
+
+
+def pair_turned(value):
+    tall = value.T
+    return jnp.concatenate((tall[:HEAD_DIM], tall[HEAD_DIM:]), axis=1)
+
+
+def start_bound(kernel):
+    column_sums = jnp.sum(kernel, axis=0, keepdims=True)
+    return column_sums, jnp.sqrt(pair_sums(column_sums * column_sums))
+
+
+def pair_identity():
+    shape = (HEAD_DIM, LANES)
+    return jnp.where(row_ids(shape) == lane_ids(shape) % HEAD_DIM, 1.0, 0.0)
+
+
+def newton_first_kernel(kernel_ref, inverse_ref, saved_ref):
+    inverses = []
+    for p in range(kernel_ref.shape[0]):
+        kernel = kernel_ref[p]
+        inverses.append(pair_turned(kernel) / start_bound(kernel)[1])
+    newton_sweeps(kernel_ref, inverses, inverse_ref, saved_ref)
+
+
+def newton_next_kernel(kernel_ref, last_ref, inverse_ref, saved_ref):
+    inverses = [last_ref[p] for p in range(kernel_ref.shape[0])]
+    newton_sweeps(kernel_ref, inverses, inverse_ref, saved_ref)
+
+
+def newton_sweeps(kernel_ref, inverses, inverse_ref, saved_ref):
+    pairs = range(kernel_ref.shape[0])
+    identity = pair_identity()
+    for sweep in range(saved_ref.shape[0]):
+        products = [pair_mul(kernel_ref[p], inverses[p]) for p in pairs]
+        inner = [15.0 * identity - pair_mul(products[p], 7.0 * identity - products[p]) for p in pairs]
+        last = [13.0 * identity - pair_mul(products[p], inner[p]) for p in pairs]
+        for p in pairs:
+            saved_ref[sweep, 0, p] = inverses[p]
+            saved_ref[sweep, 1, p] = products[p]
+            saved_ref[sweep, 2, p] = inner[p]
+            saved_ref[sweep, 3, p] = last[p]
+        inverses = [0.25 * pair_mul(inverses[p], last[p]) for p in pairs]
+    for p in pairs:
+        inverse_ref[p] = inverses[p]
+
+
+def newton_back_kernel(kernel_ref, saved_ref, inverse_in, kernel_in, inverse_out, kernel_out):
+    pairs = range(kernel_ref.shape[0])
+    identity = pair_identity()
+    back = [inverse_in[p] for p in pairs]
+    total = [kernel_in[p] for p in pairs]
+    for sweep in reversed(range(saved_ref.shape[0])):
+        inverse = [saved_ref[sweep, 0, p] for p in pairs]
+        product = [saved_ref[sweep, 1, p] for p in pairs]
+        third = [0.25 * pair_t_mul(inverse[p], back[p]) for p in pairs]
+        second = [-pair_t_mul(product[p], third[p]) for p in pairs]
+        first = [-pair_t_mul(product[p], second[p]) for p in pairs]
+        slope = [
+            -(
+                pair_mul_t(third[p], saved_ref[sweep, 2, p])
+                + pair_mul_t(second[p], 7.0 * identity - product[p])
+                + first[p]
+            )
+            for p in pairs
+        ]
+        back = [
+            0.25 * pair_mul_t(back[p], saved_ref[sweep, 3, p])
+            + pair_t_mul(kernel_ref[p], slope[p])
+            for p in pairs
+        ]
+        total = [total[p] + pair_mul_t(slope[p], inverse[p]) for p in pairs]
+    for p in pairs:
+        inverse_out[p] = back[p]
+        kernel_out[p] = total[p]
+
+
+def land_back_kernel(kernel_ref, back_start_ref, back_kernel_ref, land_query_ref, land_key_ref,
+                     query_ref, key_ref):
+    queries, keys = [], []
+    for p in range(kernel_ref.shape[0]):
+        kernel, start = kernel_ref[p], pair_turned(back_start_ref[p])
+        column_sums, bound = start_bound(kernel)
+        both = jnp.sum(start * kernel, axis=0, keepdims=True)
+        back_bound = -pair_sums(both) / (bound * bound)
+        back = back_kernel_ref[p] + start / bound + back_bound * column_sums / bound
+        scores = kernel * (back - pair_sums(kernel * back))
+        land_query, land_key = pair_of(land_query_ref[...], p), pair_of(land_key_ref[...], p)
+        high, low = two_parts(scores)
+        spread = pair_spread(land_key)
+        queries.append(dot(high, spread) + dot(low, spread))
+        keys.append(pair_gather(outer(high, land_query) + outer(low, land_query)))
+    query_ref[...] = jnp.concatenate(queries, axis=1)
+    key_ref[...] = jnp.concatenate(keys, axis=1)
 
 
 def group_of(array, r, channels):
@@ -299,14 +407,14 @@
     flags_ref[14:16, :] = jnp.zeros((2, LANES), f32)
 
 
-def query_key_kernel(flat_ref, w0, w1, bias_ref, member_ref, query_ref, keys_ref, part_ref, message_ref):
+def query_key_kernel(flat_ref, q0, k0, q1, k1, bias_ref, member_ref, query_ref, keys_ref, part_ref, message_ref):
     channels = query_ref.shape[2]
     scale = HEAD_DIM ** (-0.25)
     parts = []
-    for r, w in enumerate((w0, w1)):
-        query = dot_t(flat_ref[...], w[:channels]) + bias_ref[r : r + 1, :]
+    for r, (q, k) in enumerate(((q0, k0), (q1, k1))):
+        query = dot_t(flat_ref[...], q[...]) + bias_ref[r : r + 1, :]
         query = (scale * query).astype(bf16)
-        keys = (scale * dot_t(flat_ref[...], w[channels:])).astype(bf16)
+        keys = (scale * dot_t(flat_ref[...], k[...])).astype(bf16)
         query_ref[r] = query
         keys_ref[r] = keys
         parts += [dot(member_ref[...], query), dot(member_ref[...], keys)]
@@ -317,7 +425,6 @@
 
 def land_kernel(flags_ref, count_ref, own0, got0, own1, got1, query_ref, keys_ref, kernel_ref):
     channels = own0.shape[1] // 4
-    heads = channels // HEAD_DIM
     count = count_ref[:, 0:1]
     queries, keys = [], []
     for own, got in ((own0, got0), (own1, got1)):
@@ -325,15 +432,13 @@
         for r in range(2):
             queries.append(group_of(land, 2 * r, channels).astype(bf16))
             keys.append(group_of(land, 2 * r + 1, channels).astype(bf16))
-    lane = lane_ids(queries[0].shape) // HEAD_DIM
-    for r in range(len(queries)):
-        for j in range(heads):
-            alone = jnp.where(lane == j, queries[r], jnp.zeros_like(queries[r]))
-            scores = dot_t(alone, keys[r])
-            powers = jnp.exp(scores - jnp.max(scores, axis=1, keepdims=True))
-            kernel_ref[r * heads + j] = powers / jnp.sum(powers, axis=1, keepdims=True)
-    query_ref[...] = jnp.concatenate(queries, axis=1)
-    keys_ref[...] = jnp.concatenate(keys, axis=1)
+    land_query, land_key = jnp.concatenate(queries, axis=1), jnp.concatenate(keys, axis=1)
+    query_ref[...] = land_query
+    keys_ref[...] = land_key
+    for p in range(kernel_ref.shape[0]):
+        scores = dot_t(pair_of(land_query, p), pair_spread(pair_of(land_key, p)))
+        powers = jnp.exp(scores - pair_sums(scores, jnp.max, very_negative))
+        kernel_ref[p] = powers / pair_sums(powers)
 
 
 def value_kernel(flat_ref, w0, w1, w2, w3, bias_ref, values_ref, head_ref, tail_ref):
@@ -474,16 +579,18 @@
     stats_ref[...] = state[:, model:]
     mixed = state[:, :model] / widen(state[:, model:], groups * heads, model)
     mixed_ref[...] = mixed
-    lows = []
+    low = jnp.concatenate(
+        [
+            pair_mul(inverse_ref[p], pair_of(mixed, p)).astype(bf16)
+            for p in range(inverse_ref.shape[0])
+        ],
+        axis=1,
+    )
+    low_ref[...] = low
     for r in range(groups):
-        mixed_group = group_of(mixed, r, channels)
-        lane = lane_ids(mixed_group.shape) // HEAD_DIM
-        land = jnp.zeros(mixed_group.shape, f32)
-        for j in range(heads):
-            land = jnp.where(lane == j, dot_fine(inverse_ref[r * heads + j], mixed_group), land)
-        low = land.astype(bf16)
-        lows.append(low)
-        nystrom = outer(weights_ref[r].astype(bf16), spread_heads(low))
+        nystrom = outer(
+            weights_ref[r].astype(bf16), spread_heads(group_of(low, r, channels))
+        )
         rim = with_rim(
             values_ref[r],
             group_of(before_ref[...], r, channels),
@@ -496,7 +603,6 @@
             for j in range(heads)
         ]
         context_ref[r] = (nystrom + convolve(rim, filters)).astype(bf16)
-    low_ref[...] = jnp.concatenate(lows, axis=1)
 
 
 def token_back_kernel(back_ref, weights_ref, low_ref, q0, q1, land_key_ref, part_ref,
@@ -570,19 +676,11 @@
 
 def seed_kernel(flags_ref, own_ref, got_ref, inverse_ref, mixed_ref, back_inverse_ref, back_mixed_ref):
     back = sum_merge(own_ref[...], got_ref[...].astype(f32), flag(flags_ref, 8))
-    heads = inverse_ref.shape[0]
     pairs = []
-    for pair in range(heads // 2):
-        near = back[:, pair * LANES : (pair + 1) * LANES]
-        mixed = mixed_ref[:, pair * LANES : (pair + 1) * LANES]
-        lane = lane_ids(near.shape) // HEAD_DIM
-        sums = jnp.zeros(near.shape, f32)
-        for j in range(2):
-            h = 2 * pair + j
-            alone = jnp.where(lane == j, near, 0.0)
-            back_inverse_ref[h] = dot_fine_t(alone, mixed)
-            sums = sums + outer_fine(inverse_ref[h], alone)
-        pairs.append(sums)
+    for p in range(inverse_ref.shape[0]):
+        near = pair_of(back, p)
+        back_inverse_ref[p] = pair_mul_t(near, pair_of(mixed_ref[...], p))
+        pairs.append(pair_t_mul(inverse_ref[p], near))
     back_mixed_ref[...] = jnp.concatenate(pairs, axis=1).astype(bf16)
 
 
@@ -623,44 +721,36 @@
 
 
 def input_back_kernel(flags_ref, count_ref, flat_ref, query_direct_ref, key_direct_ref, back_values_ref,
-                      query_own_ref, query_got_ref, key_own_ref, key_got_ref, kernel_ref,
-                      back_kernel_ref, land_query_ref, land_key_ref, member_ref, back_input_ref,
-                      w0, w1, w2, w3, v0, v1, v2, v3, grad_ref, bias_ref, g0, g1, g2, g3,
-                      turned_ref):
+                      query_own_ref, query_got_ref, query_more_ref, key_own_ref, key_got_ref,
+                      key_more_ref, member_ref, back_input_ref, q0, q1, q2, q3, k0, k1, k2, k3, v0,
+                      v1, v2, v3, grad_ref, bias_ref, g0, g1, g2, g3, turned_ref):
     groups, width, channels = back_values_ref.shape
-    heads = channels // HEAD_DIM
     scale = HEAD_DIM ** (-0.25)
     member = member_ref[...]
     count = count_ref[:, 0:1]
     sides = [
-        sum_merge(own[...], got[...].astype(f32), flag(flags_ref, 8))
-        for own, got in ((query_own_ref, query_got_ref), (key_own_ref, key_got_ref))
+        two_parts(
+            (sum_merge(own[...], got[...].astype(f32), flag(flags_ref, 8)) + more[...]) / count
+        )
+        for own, got, more in (
+            (query_own_ref, query_got_ref, query_more_ref),
+            (key_own_ref, key_got_ref, key_more_ref),
+        )
     ]
     total = back_input_ref[...]
     turned_ref[...] = flat_ref[...].T
     for r in range(groups):
-        w, v = (w0, w1, w2, w3)[r], (v0, v1, v2, v3)[r]
-        land_query = group_of(land_query_ref[...], r, channels)
-        land_key = group_of(land_key_ref[...], r, channels)
-        lane = lane_ids(land_query.shape) // HEAD_DIM
-        query_side = group_of(sides[0], r, channels)
-        key_side = group_of(sides[1], r, channels)
-        for j in range(heads):
-            kernel, back = kernel_ref[r * heads + j], back_kernel_ref[r * heads + j]
-            scores = kernel * (back - jnp.sum(kernel * back, axis=1, keepdims=True))
-            high, low = two_parts(scores)
-            more = dot(high, land_key) + dot(low, land_key)
-            query_side = query_side + jnp.where(lane == j, more, 0.0)
-            more = outer(high, land_query) + outer(low, land_query)
-            key_side = key_side + jnp.where(lane == j, more, 0.0)
+        q, k, v = (q0, q1, q2, q3)[r], (k0, k1, k2, k3)[r], (v0, v1, v2, v3)[r]
         both = []
-        for side, direct_ref in ((query_side, query_direct_ref), (key_side, key_direct_ref)):
-            high, low = two_parts(side / count)
-            both.append((direct_ref[r] + (dot(member, high) + dot(member, low))).astype(bf16))
+        for (high, low), direct_ref in zip(sides, (query_direct_ref, key_direct_ref)):
+            far = dot(member, group_of(high, r, channels)) + dot(member, group_of(low, r, channels))
+            both.append((direct_ref[r] + far).astype(bf16))
         bias_ref[r : r + 1, :] = scale * jnp.sum(both[0].astype(f32), axis=0, keepdims=True)
-        both = jnp.concatenate(both, axis=1)
-        total = total + scale * dot(both, w[...]) + dot(back_values_ref[r], v[...])
-        (g0, g1, g2, g3)[r][...] = (scale * dot(turned_ref[...], both)).astype(bf16)
+        total = total + scale * (dot(both[0], q[...]) + dot(both[1], k[...]))
+        total = total + dot(back_values_ref[r], v[...])
+        (g0, g1, g2, g3)[r][...] = jnp.concatenate(
+            [(scale * dot(turned_ref[...], side)).astype(bf16) for side in both], axis=1
+        )
     grad_ref[...] = total.astype(bf16)
 
 
@@ -697,6 +787,7 @@
             out_specs=pl.BlockSpec((1, width, model), lambda i, rank: (i ^ rank[0], 0, 0)),
         ),
         compiler_params=pltpu.CompilerParams(vmem_limit_bytes=24 << 20),
+        cost_estimate=cost(2.5),
         name="place_rows",
     )(rank.reshape(1).astype(jnp.int32), *blocks)
 
@@ -820,11 +911,7 @@
             pltpu.VMEM((width, model), f32),
         ],
         compiler_params=pltpu.CompilerParams(vmem_limit_bytes=VMEM_LIMIT),
-        cost_estimate=pl.CostEstimate(
-            flops=2 * width * model * (4 * ranks * units + 2 * ranks * channels),
-            bytes_accessed=30 << 20,
-            transcendentals=2 * width * ranks * units,
-        ),
+        cost_estimate=cost(35.0),
         name="feed_layer",
     )(flat, context, *outputs, *ups, *downs, up_bias, params, cotangent)
 
@@ -875,7 +962,9 @@
     marked = ((marks, model), f32)
     message = ((marks, model), bf16)
     tall = ((marks, LANES), f32)
-    squares = ((heads, marks, marks), f32)
+    squares = ((heads // 2, marks, LANES), f32)
+    half_sweeps = SWEEPS // 2
+    saved = ((half_sweeps, 4, heads // 2, marks, LANES), f32)
 
     small = jnp.concatenate(
         (
@@ -888,11 +977,10 @@
     small_rows = -(-small.shape[0] // model)
     small_rows += -small_rows % 16
     small = jnp.pad(small, (0, small_rows * model - small.shape[0])).reshape(small_rows, model)
-    query_key = jnp.concatenate((query_weight.T, key_weight.T), axis=0)
-    value_turned = value_weight.T
-    first_far = swap(query_key, "tp", 2)
+    turned = [w.T for w in (query_weight, key_weight, value_weight)]
+    query_far, key_far = swap((turned[0], turned[1]), "tp", 2)
+    query_core, key_core = swap((turned[0], turned[1]), "tp", 1)
     small_far = swap(small, "tp", 2)
-    first_core = swap(query_key, "tp", 1)
     small_core = swap(small, "tp", 1)
     smalls = [s.reshape(-1).astype(f32) for s in (small, small_core, small_far, swap(small_far, "tp", 1))]
     member, member_turned, count, flags = call(
@@ -916,12 +1004,13 @@
     def shards(own, far):
         return (own, swap(own, "tp", 1), far, swap(far, "tp", 1))
 
-    query_key = (query_key, first_core, first_far, swap(first_far, "tp", 1))
-    value_far = swap(after(value_turned, first_far), "tp", 2)
+    query_blocks = (turned[0], query_core, query_far, swap(query_far, "tp", 1))
+    key_blocks = (turned[1], key_core, key_far, swap(key_far, "tp", 1))
+    value_far = swap(after(turned[2], key_far), "tp", 2)
     output_far = swap(after(output_weight, value_far), "tp", 2)
     up_far = swap(after(up_weight, output_far), "tp", 2)
     down_far = swap(after(down_weight, up_far), "tp", 2)
-    value_blocks = shards(value_turned, value_far)
+    value_blocks = shards(turned[2], value_far)
     output_blocks = shards(output_weight, output_far)
     up_blocks = shards(up_weight, up_far)
     down_blocks = shards(down_weight, down_far)
@@ -929,12 +1018,13 @@
     query, keys, sums = [], [], []
     for pair in range(2):
         q, k, part, sent = call(
-            query_key_kernel, (half, half, marked, message), "query_key",
-            flops=2 * width * model * 768,
+            query_key_kernel, (half, half, marked, message), "query_key", us=2.5,
         )(
             flat,
-            query_key[2 * pair],
-            query_key[2 * pair + 1],
+            query_blocks[2 * pair],
+            key_blocks[2 * pair],
+            query_blocks[2 * pair + 1],
+            key_blocks[2 * pair + 1],
             query_bias_all[2 * pair : 2 * pair + 2],
             member_turned,
         )
@@ -945,7 +1035,7 @@
         flags, count, *sums
     )
     values, value_head, value_tail = call(
-        value_kernel, (full, edge, edge), "values", flops=2 * width * model * 768
+        value_kernel, (full, edge, edge), "values", us=2.0
     )(flat, *value_blocks, value_bias_all)
 
     def neighbours(head, tail):
@@ -959,18 +1049,20 @@
         key_kernel,
         (((marks, model + LANES), f32), ((marks, model + LANES), bf16)),
         "key_softmax",
-        flops=4 * width * 768 * 192,
-    )(*keys, values, land_query)
+        us=1.4,
+    )(*keys, values, after(land_query, up_far))
     state, state_got = exchange(soft_parts(heads), "soft", flags, state, sent)
     (token_weights,) = call(
-        token_kernel, (((ranks, own_heads * marks, width), f32),), "token_softmax",
-        flops=2 * width * 768 * 192,
+        token_kernel, (((ranks, own_heads * marks, width), f32),), "token_softmax", us=0.8,
     )(*query, land_key)
-    inverse, inverse_back = jax.vjp(newton_inverse, kernel)
+    inverse, saved_first = call(newton_first_kernel, (squares, saved), "newton_first", us=6.0)(kernel)
+    inverse, saved_last = call(newton_next_kernel, (squares, saved), "newton_next", us=6.0)(
+        kernel, inverse
+    )
     context, mixed, mixed_low, stats = call(
-        context_kernel, (full, marked, message, tall), "context", flops=6 * width * 768 * 192,
+        context_kernel, (full, marked, message, tall), "context", us=2.0,
     )(
-        state, state_got, inverse, token_weights, values, value_before, value_after, flags,
+        after(state, down_far), state_got, inverse, token_weights, values, value_before, value_after, flags,
         taps_wide,
     )
 
@@ -993,68 +1085,77 @@
     )
 
     layer_far = swap(layer_out, "tp", 2)
+    units_of = functools.partial(group_of, channels=hidden_units)
+    positions = lax.axis_size("seq")
+    sizes = [1 << level for level in range(positions.bit_length() - 1)]
+    down = [outer(back_feed, units_of(active, r)).astype(bf16) for r in range(ranks)]
     part_back, sent_back, part_key, sent_key, query_direct, back_head, back_tail = call(
         token_back_kernel, (marked, message, marked, message, full32, edge, edge), "token_back",
-        flops=8 * width * 768 * 192,
-    )(back_context, token_weights, mixed_low, *query, land_key)
-    back_own, back_got = exchange(plain_parts(), "back", flags, part_back, sent_back)
+        us=1.8,
+    )(after(back_context, *down), token_weights, mixed_low, *query, land_key)
+    down = scatter_start(down)
+    up = [outer(first_low, units_of(back_hidden, r)).astype(bf16) for r in range(ranks)]
+    back_own, back_got = exchange(
+        plain_parts(), "back", flags, part_back, sent_back, (up[:2], up[2:] + down)
+    )
     key_own, key_got = exchange(plain_parts(), "back_key", flags, part_key, sent_key)
     back_before, back_after = neighbours(back_head, back_tail)
     conv_back, tap_rows = call(
-        conv_back_kernel, (full32, ((heads, 2 * LANES), f32)), "conv_back",
-        flops=6 * width * 768 * 192,
+        conv_back_kernel, (full32, ((heads, 2 * LANES), f32)), "conv_back", us=2.8
     )(
         back_context, back_before, back_after, values, value_before, value_after, flags,
         taps_flipped,
     )
     conv_part = tap_rows[:, STRIPE - 1 : STRIPE - 1 + TAPS]
-    units_of = functools.partial(group_of, channels=hidden_units)
-    positions = lax.axis_size("seq")
-    sizes = [1 << level for level in range(positions.bit_length() - 1)]
-    down = scatter_start([outer(back_feed, units_of(active, r)).astype(bf16) for r in range(ranks)])
-    up = scatter_start(
-        [outer(first_low, units_of(back_hidden, r)).astype(bf16) for r in range(ranks)]
-    )
-    down = by_targets(scatter_far(down), positions)
-    up = by_targets(up, positions)
-    for size in sizes:
+    up = scatter_start(up)
+    back_inverse, back_mixed = call(seed_kernel, (squares, message), "seed")(
+        flags, after(back_own, conv_back, layer_far, *up), back_got, inverse, mixed
+    )
+    down = by_targets(scatter_far([down[0], after(down[1], layer_far)]), positions)
+    up = scatter_level(by_targets(up, positions), device, 1)
+    part_query, sent_query, key_direct, back_values, value_bias_sums = call(
+        key_back_kernel, (marked, message, full32, full, ((ranks, channels), f32)), "key_back",
+        us=2.4,
+    )(*keys, values, land_query, stats, mixed, back_mixed, conv_back)
+    newton_back = call(newton_back_kernel, (squares, squares), "newton_back", us=10.0)
+    back_middle = newton_back(kernel, saved_last, back_inverse, jnp.zeros(*squares))
+    pairs = (((model, 2 * channels), bf16),) * ranks
+    value_output = call(value_output_kernel, pairs, "value_output", us=2.0)(
+        flat, back_values, back_attention, context
+    )
+    query_own, query_got = exchange(
+        plain_parts(), "back_query", flags, part_query, sent_query,
+        (list(back_middle), list(value_output)),
+    )
+    back_start, back_kernel = newton_back(kernel, saved_first, *back_middle)
+    query_more, key_more = call(land_back_kernel, (marked, marked), "land_back")(
+        kernel, back_start, back_kernel, land_query, land_key
+    )
+    value_output = scatter_start(value_output)
+    grad_row, query_bias_sums, *projection = call(
+        input_back_kernel,
+        (((width, model), bf16), ((ranks, channels), f32)) + pairs,
+        "input_back",
+        scratch=(pltpu.VMEM((model, width), bf16),),
+        us=7.0,
+        limit=32 << 20,
+    )(
+        flags, count, flat, query_direct, key_direct, back_values,
+        after(query_own, *down, *up, *value_output), query_got, query_more, key_own, key_got,
+        key_more, member, back_input, *query_blocks, *key_blocks, *value_blocks,
+    )
+    for size in sizes[1:]:
         up = scatter_level(up, device, size)
     for size in sizes:
         down = scatter_level(down, device, size, size == sizes[-1])
     grad_up_weight = scatter_far(up)[0][0].astype(f32)
     grad_down_weight = down[0][0]
     grad_up_bias = [units_of(up_sums, r)[0] for r in range(ranks)]
-
-    back_inverse, back_mixed = call(seed_kernel, (squares, message), "seed")(
-        flags, back_own, back_got, inverse, mixed
-    )
-    part_query, sent_query, key_direct, back_values, value_bias_sums = call(
-        key_back_kernel, (marked, message, full32, full, ((ranks, channels), f32)), "key_back",
-        flops=10 * width * 768 * 192,
-    )(*keys, values, land_query, stats, mixed, back_mixed, conv_back)
-    query_own, query_got = exchange(plain_parts(), "back_query", flags, part_query, sent_query)
-    (back_kernel,) = inverse_back(back_inverse)
-    pairs = (((model, 2 * channels), bf16),) * ranks
-    value_output = call(value_output_kernel, pairs, "value_output", flops=4 * width * model * model)(
-        flat, back_values, back_attention, context
-    )
-    value_output = by_targets(scatter_far(scatter_start(value_output)), positions)
+    value_output = by_targets(scatter_far(value_output), positions)
     for size in sizes:
         value_output = scatter_level(value_output, device, size, size == sizes[-1])
     grad_output_weight = value_output[0][0][:, :channels].T
     grad_value_weight = value_output[0][0][:, channels:]
-    grad_row, query_bias_sums, *projection = call(
-        input_back_kernel,
-        (((width, model), bf16), ((ranks, channels), f32)) + pairs,
-        "input_back",
-        scratch=(pltpu.VMEM((model, width), bf16),),
-        flops=2 * width * 768 * 768 * 6,
-        limit=32 << 20,
-    )(
-        flags, count, flat, query_direct, key_direct, back_values, query_own, query_got, key_own,
-        key_got, kernel, back_kernel, land_query, land_key, member, back_input, *query_key,
-        *value_blocks,
-    )
     projection = by_targets(scatter_start(projection), positions)
     for size in sizes:
         projection = scatter_level(projection, device, size)

time: 476 us -> 426 us (0.89)
  matrix products: 71.4 us -> 10.3 us
  waiting for transfers between devices: 169 us -> 138 us
  local copies, waits for them, and re-layouts: 47.8 us -> 74.1 us
  Pallas kernels: 79.7 us -> 98 us
    dot_general x72 -> x0, matrix products: 52.3 us -> none  [the longest x18 13.8 us: newton_inverse(): inner = 15.0 * identity - jnp.matmul(product, inner, precision=highest)]
    ppermute x77 -> x80, waiting for transfers between devices: 166 us -> 135 us  [swap(): lax.ppermute(value, axis, [(i, i ^ step) for i in range(lax.axis_size(axi...]
    pallas_call x26 -> x31, Pallas kernels: 39.3 us -> 54.9 us  [run(): pl.pallas_call(kernel, out_shape=outs, in_specs=[pl.BlockSpec(memory_spac...]
    dot_general x8, matrix products: 19.1 us -> 10.3 us  [outer(): lax.dot_general(a, b, (((0,), (0,)), ((), ())), preferred_element_type=f32)]
    unnamed x323 -> x245, local copies, waits for them, and re-layouts: 27.3 us -> 33.5 us
    another operation x7, local copies, waits for them, and re-layouts: 0.07 us -> 5.74 us  [per_device(): jnp.stack((output_bias, first_gain, first_shift, down_bias, second_gain,...]
    slice x4, local copies, waits for them, and re-layouts: 0.29 us -> 5.44 us  [per_device(): s[up_start:up_start + hidden_units]]
    ppermute x77 -> x80, starting transfers between devices: 64.9 us -> 62.3 us  [swap(): lax.ppermute(value, axis, [(i, i ^ step) for i in range(lax.axis_size(axi...]
  transfers between devices with their start and end apart: 81 -> 84, of which waited for: 34 -> 36; matrix products, arithmetic and copies ran while one was open for 21% -> 16% of each run, Pallas kernels for 7% -> 14%
where the time goes in v1:
time: 426 us; the launch traced here: 418 us
  waiting for transfers between devices  138 us (32%)
  Pallas kernels  98 us (23%)
  local copies, waits for them, and re-layouts  74.1 us (17%)
  starting transfers between devices  72 us (17%)
  other arithmetic  21.9 us (5%)
  matrix products  10.3 us (2%)
    ppermute x80, waiting for transfers between devices, swap(): lax.ppermute(value, axis, [(i, i ^ step) for i in range(lax.axis_size(axi...  135 us
    ppermute x80, starting transfers between devices, swap(): lax.ppermute(value, axis, [(i, i ^ step) for i in range(lax.axis_size(axi...  62.3 us
    pallas_call x31, Pallas kernels, run(): pl.pallas_call(kernel, out_shape=outs, in_specs=[pl.BlockSpec(memory_spac...  54.9 us
    pallas_call x1, Pallas kernels, feed_layer(): pl.pallas_call(feed_kernel, out_shape=(shape((width, model), bf16), shape...  36.1 us
    unnamed x245, local copies, waits for them, and re-layouts  33.5 us
    dot_general x8, matrix products, outer(): lax.dot_general(a, b, (((0,), (0,)), ((), ())), preferred_element_type=f32)  10.3 us
  transfers between devices with their start and end apart: 84, of which 36 were waited for; matrix products, arithmetic and copies ran while one was open for 16% of the time, Pallas kernels for 14%

profile of v1, /device:TPU:0, one launch (start us, length us, event | category | flops | bytes accessed | tf_op | source)
XLA Modules:
  0.0 417.7 jit_solution(18349453536471068306)
XLA Ops:
  0.7 3.0 collective-permute-start.4
  3.7 7.3 %collective-permute-done.4.k0.k2 = bf16[192,768]{1,0:T(8,128)(2,1)} collective-permute-done((bf16[192,768]{1,0:T(8,128)(2,1)}, bf16[192,768]{1,0:T(8,128)(2,1)}, u32[]{:S(2)}, u32[]{:S(2)}) %collective-permute-start.4) | collective-permute-done | bytes 294944 | tf_op jit(solution)/shard_map/ppermute | solution.py:27
  12.8 6.8 %collective-permute-done.10.w2.v2 = bf16[192,768]{1,0:T(8,128)(2,1)} collective-permute-done((bf16[192,768]{1,0:T(8,128)(2,1)}, bf16[192,768]{1,0:T(8,128)(2,1)}, u32[]{:S(2)}, u32[]{:S(2)}) %collective-permute-start.10) | collective-permute-done | bytes 294944 | tf_op jit(solution)/shard_map/ppermute | solution.py:27
  21.0 6.2 %collective-permute-done.18.out2 = bf16[192,768]{1,0:T(8,128)(2,1)} collective-permute-done((bf16[192,768]{1,0:T(8,128)(2,1)}, bf16[192,768]{1,0:T(8,128)(2,1)}, u32[]{:S(2)}, u32[]{:S(2)}) %collective-permute-start.18) | collective-permute-done | bytes 294944 | tf_op jit(solution)/shard_map/ppermute | solution.py:27
  35.6 18.4 %collective-permute-done.7 = bf16[16,768]{1,0:T(8,128)(2,1)S(1)} collective-permute-done((bf16[16,768]{1,0:T(8,128)(2,1)S(1)}, bf16[16,768]{1,0:T(8,128)(2,1)S(1)}, u32[]{:S(2)}, u32[]{:S(2)}) %collective-permute-start.7) | collective-permute-done | bytes 24608 | tf_op jit(solution)/shard_map/ppermute | solution.py:27
  57.5 4.4 %collective-permute-done.3.q0.q2 = bf16[192,768]{1,0:T(8,128)(2,1)S(1)} collective-permute-done((bf16[192,768]{1,0:T(8,128)(2,1)S(1)}, bf16[192,768]{1,0:T(8,128)(2,1)S(1)}, u32[]{:S(2)}, u32[]{:S(2)}) %collective-permute-start.3) | collective-permute-done | bytes 294944 | tf_op jit(solution)/shard_map/ppermute | solution.py:27
  64.1 2.5 query_key.2
  68.2 2.5 query_key.3
  73.8 2.6 collective-permute-done.15.got_ref
  78.2 2.5 collective-permute-done.13.got_ref
  82.7 3.0 collective-permute-done.16.got_ref
  87.3 2.4 collective-permute-done.14.got0
  90.2 2.3 collective-permute-done.17.got1
  93.1 2.5 values.1
  99.8 3.7 collective-permute-done.20.got_ref
  103.5 3.2 collective-permute-start.24
  124.8 3.2 collective-permute-start.23
  145.4 2.5 newton_first.1
  149.4 2.3 newton_next.1
  155.0 3.0 context.1
  159.4 36.1 %feed_layer.1 = (bf16[512,768]{1,0:T(8,128)(2,1)S(1)}, f32[512,768]{1,0:T(8,128)}, bf16[512,768]{1,0:T(8,128)(2,1)S(1)}, bf16[4,512,192]{2,1,0:T(8,128)(2,1)S(1)...) custom-call(bf16[512,768]{1,0:T(8,128)(2,1)S(1)} %copy-done.3, ...), custom_call_target="tpu_custom_call" | custom-call | bytes 115500000 | tf_op jit(solution)/shard_map/feed_layer/pallas_call | solution.py:892
  195.6 3.6 convolution_convert_fusion.7
  202.7 2.6 collective-permute-start.33
  207.4 3.5 collective-permute-start.39
  216.3 3.4 collective-permute-done.40.after_ref
  219.8 2.7 collective-permute-start.51
  223.1 3.6 conv_back.1
  249.5 3.8 place_rows.2
  255.0 5.3 %collective-permute-done.46 = bf16[4,96,768]{2,1,0:T(8,128)(2,1)} collective-permute-done((bf16[4,96,768]{2,1,0:T(8,128)(2,1)}, bf16[4,96,768]{2,1,0:T(8,128)(2,1)}, u32[]{:S(2)}, u32[]{:S(2)}) %collective-permute-start.46) | collective-permute-done | bytes 589856 | tf_op jit(solution)/shard_map/ppermute | solution.py:27
  262.0 7.0 %collective-permute-done.77 = bf16[2,96,768]{2,1,0:T(8,128)(2,1)S(1)} collective-permute-done((bf16[2,96,768]{2,1,0:T(8,128)(2,1)S(1)}, bf16[2,96,768]{2,1,0:T(8,128)(2,1)S(1)}, u32[]{:S(2)}, u32[]{:S(2)}) %collective-permute-start.77) | collective-permute-done | bytes 294944 | tf_op jit(solution)/shard_map/ppermute | solution.py:27
  269.5 2.3 add_convert_fusion
  275.0 8.2 %collective-permute-done.43.got_ref = bf16[64,768]{1,0:T(8,128)(2,1)S(1)} collective-permute-done((bf16[64,768]{1,0:T(8,128)(2,1)S(1)}, bf16[64,768]{1,0:T(8,128)(2,1)S(1)}, u32[]{:S(2)}, u32[]{:S(2)}) %collective-permute-start.43) | collective-permute-done | bytes 98336 | tf_op jit(solution)/shard_map/ppermute | solution.py:27
  291.8 6.6 %newton_back.2 = (f32[6,64,128]{2,1,0:T(8,128)S(1)}, f32[6,64,128]{2,1,0:T(8,128)S(1)}) custom-call(f32[6,64,128]{2,1,0:T(8,128)S(1)} %get-tuple-element.157.kernel_ref, f32[3,4,6,64,128]{4,3,2,1,0:T(8,128)S(1)} %copy-done.8, f32[6,64,128]{2,1,0:T(8,128)S(1)} %get-tuple-element.194.inverse_in, f32[6,64,128]{2,1,0:T(8,128)S(1)} %broadcast_in_dim.17.kernel_in), custom_call_target="tpu_custom_call" | custom-call | bytes 33000000 | tf_op jit(solution)/shard_map/newton_back/pallas_call | solution.py:157
  298.6 6.9 %newton_back.3 = (f32[6,64,128]{2,1,0:T(8,128)S(1)}, f32[6,64,128]{2,1,0:T(8,128)S(1)}) custom-call(f32[6,64,128]{2,1,0:T(8,128)S(1)} %get-tuple-element.157.kernel_ref, f32[3,4,6,64,128]{4,3,2,1,0:T(8,128)S(1)} %copy-done.6, f32[6,64,128]{2,1,0:T(8,128)S(1)} %get-tuple-element.195.inverse_in, f32[6,64,128]{2,1,0:T(8,128)S(1)} %get-tuple-element.196.kernel_in), custom_call_target="tpu_custom_call" | custom-call | bytes 33000000 | tf_op jit(solution)/shard_map/newton_back/pallas_call | solution.py:157
  307.7 6.4 %collective-permute-done.45.got_ref = bf16[128,768]{1,0:T(8,128)(2,1)S(1)} collective-permute-done((bf16[128,768]{1,0:T(8,128)(2,1)S(1)}, bf16[128,768]{1,0:T(8,128)(2,1)S(1)}, u32[]{:S(2)}, u32[]{:S(2)}) %collective-permute-start.45) | collective-permute-done | bytes 196640 | tf_op jit(solution)/shard_map/ppermute | solution.py:27
  316.2 2.4 collective-permute-start.50
  318.6 4.9 %collective-permute-done.71 = bf16[768,384]{1,0:T(8,128)(2,1)S(1)} collective-permute-done((bf16[768,384]{1,0:T(8,128)(2,1)S(1)}, bf16[768,384]{1,0:T(8,128)(2,1)S(1)}, u32[]{:S(2)}, u32[]{:S(2)}) %collective-permute-start.71) | collective-permute-done | bytes 589856 | tf_op jit(solution)/shard_map/ppermute | solution.py:27
  328.1 7.2 %input_back.1 = (bf16[512,768]{1,0:T(8,128)(2,1)S(1)}, f32[4,192]{1,0:T(4,128)S(1)}, bf16[768,384]{1,0:T(8,128)(2,1)S(1)}, bf16[768,384]{1,0:T(8,128)(2,1)}, bf1...) custom-call(f32[16,128]{1,0:T(8,128)S(1)} %get-tuple-element.126.flags_ref, ...), custom_call_target="tpu_custom_call" | custom-call | bytes 23100000 | tf_op jit(solution)/shard_map/input_back/pallas_call | solution.py:157
  339.4 3.6 collective-permute-done.67
  352.4 4.2 %collective-permute-done.70 = f32[80,128]{1,0:T(8,128)S(1)} collective-permute-done((f32[80,128]{1,0:T(8,128)S(1)}, f32[80,128]{1,0:T(8,128)S(1)}, u32[]{:S(2)}, u32[]{:S(2)}) %collective-permute-start.70) | collective-permute-done | bytes 40992 | tf_op jit(solution)/shard_map/ppermute | solution.py:27
  367.6 4.4 %collective-permute-done.73 = bf16[2,96,384]{2,1,0:T(8,128)(2,1)S(1)} collective-permute-done((bf16[2,96,384]{2,1,0:T(8,128)(2,1)S(1)}, bf16[2,96,384]{2,1,0:T(8,128)(2,1)S(1)}, u32[]{:S(2)}, u32[]{:S(2)}) %collective-permute-start.73) | collective-permute-done | bytes 147488 | tf_op jit(solution)/shard_map/ppermute | solution.py:27
  373.0 4.8 %collective-permute-done.74 = bf16[1,96,384]{2,1,0:T(8,128)(2,1)S(1)} collective-permute-done((bf16[1,96,384]{2,1,0:T(8,128)(2,1)S(1)}, bf16[1,96,384]{2,1,0:T(8,128)(2,1)S(1)}, u32[]{:S(2)}, u32[]{:S(2)}) %collective-permute-start.74) | collective-permute-done | bytes 73760 | tf_op jit(solution)/shard_map/ppermute | solution.py:27
  382.5 6.1 %collective-permute-done.62 = bf16[4,96,384]{2,1,0:T(8,128)(2,1)S(1)} collective-permute-done((bf16[4,96,384]{2,1,0:T(8,128)(2,1)S(1)}, bf16[4,96,384]{2,1,0:T(8,128)(2,1)S(1)}, u32[]{:S(2)}, u32[]{:S(2)}) %collective-permute-start.62) | collective-permute-done | bytes 294944 | tf_op jit(solution)/shard_map/ppermute | solution.py:27
  388.8 3.0 collective-permute-done.58
  391.9 3.0 collective-permute-done.63
  398.1 2.7 collective-permute-done.64
  403.0 2.4 collective-permute-done.65
  413.4 3.2 place_rows.3
  (538 shorter events, 176.6 us)
Async XLA Ops:
  0.7 10.4 %collective-permute-start.4 = (bf16[192,768]{1,0:T(8,128)(2,1)}, bf16[192,768]{1,0:T(8,128)(2,1)}, u32[]{:S(2)}, u32[]{:S(2)}) collective-permute-start(bf16[192,768]{1,0:T(8,128)(2,1)} %bitcast.155), channel_id=1, source_target_pairs={{0,2},{1,3},{2,0},{3,1},{4,6},{5,7},{6,4},{7,5},{8,10},{9,11},{10,... | collective-permute-start | bytes 884744 | tf_op jit(solution)/shard_map/ppermute | solution.py:27
  27.2 28.8 %collective-permute-start.19 = (bf16[768,768]{1,0:T(8,128)(2,1)}, bf16[768,768]{1,0:T(8,128)(2,1)}, u32[]{:S(2)}, u32[]{:S(2)}) collective-permute-start(bf16[768,768]{1,0:T(8,128)(2,1)} %up0.1), channel_id=1, source_target_pairs={{0,2},{1,3},{2,0},{3,1},{4,6},{5,7},{6,4},{7,5},{8,10},{9,11},{10,... | collective-permute-start | bytes 3538952 | tf_op jit(solution)/shard_map/ppermute | solution.py:27
  28.3 33.7 %collective-permute-start.1 = (bf16[192,768]{1,0:T(8,128)(2,1)}, bf16[192,768]{1,0:T(8,128)(2,1)}, u32[]{:S(2)}, u32[]{:S(2)}) collective-permute-start(bf16[192,768]{1,0:T(8,128)(2,1)} %bitcast.156), channel_id=1, source_target_pairs={{0,1},{1,0},{2,3},{3,2},{4,5},{5,4},{6,7},{7,6},{8,9},{9,8},{10,11... | collective-permute-start | bytes 884744 | tf_op jit(solution)/shard_map/ppermute | solution.py:27
  31.4 23.7 %collective-permute-start.2 = (bf16[16,768]{1,0:T(8,128)(2,1)S(1)}, bf16[16,768]{1,0:T(8,128)(2,1)}, u32[]{:S(2)}, u32[]{:S(2)}) collective-permute-start(bf16[16,768]{1,0:T(8,128)(2,1)S(1)} %reshape.229), channel_id=1, source_target_pairs={{0,1},{1,0},{2,3},{3,2},{4,5},{5,4},{6,7},{7,6},{8,9},{9,8},{10,11... | collective-permute-start | bytes 73736 | tf_op jit(solution)/shard_map/ppermute | solution.py:27
  31.9 22.0 %collective-permute-start.7 = (bf16[16,768]{1,0:T(8,128)(2,1)S(1)}, bf16[16,768]{1,0:T(8,128)(2,1)S(1)}, u32[]{:S(2)}, u32[]{:S(2)}) collective-permute-start(bf16[16,768]{1,0:T(8,128)(2,1)S(1)} %reshape.229), channel_id=1, source_target_pairs={{0,2},{1,3},{2,0},{3,1},{4,6},{5,7},{6,4},{7,5},{8,10},{9,11},{10,... | collective-permute-start | bytes 73736 | tf_op jit(solution)/shard_map/ppermute | solution.py:27
  32.9 29.1 %collective-permute-start = (bf16[192,768]{1,0:T(8,128)(2,1)}, bf16[192,768]{1,0:T(8,128)(2,1)}, u32[]{:S(2)}, u32[]{:S(2)}) collective-permute-start(bf16[192,768]{1,0:T(8,128)(2,1)} %bitcast.151), channel_id=1, source_target_pairs={{0,1},{1,0},{2,3},{3,2},{4,5},{5,4},{6,7},{7,6},{8,9},{9,8},{10,11... | collective-permute-start | bytes 884744 | tf_op jit(solution)/shard_map/ppermute | solution.py:27
  56.0 36.6 %collective-permute-start.22 = (bf16[768,768]{1,0:T(8,128)(2,1)}, bf16[768,768]{1,0:T(8,128)(2,1)}, u32[]{:S(2)}, u32[]{:S(2)}) collective-permute-start(bf16[768,768]{1,0:T(8,128)(2,1)} %down0.1), channel_id=1, source_target_pairs={{0,2},{1,3},{2,0},{3,1},{4,6},{5,7},{6,4},{7,5},{8,10},{9,11},{10,... | collective-permute-start | bytes 3538952 | tf_op jit(solution)/shard_map/ppermute | solution.py:27
  57.2 11.0 %collective-permute-start.6 = (bf16[192,768]{1,0:T(8,128)(2,1)}, bf16[192,768]{1,0:T(8,128)(2,1)S(1)}, u32[]{:S(2)}, u32[]{:S(2)}) collective-permute-start(bf16[192,768]{1,0:T(8,128)(2,1)} %collective-permute-done.4.k0.k2), channel_id=1, source_target_pairs={{0,1},{1,0},{2,3},{3,2},{4,5},{5,4},{6,7},{7,6},{8,9},{9,8},{10,11... | collective-permute-start | bytes 884744 | tf_op jit(solution)/shard_map/ppermute | solution.py:27
  72.8 14.4 %collective-permute-start.9 = (bf16[192,768]{1,0:T(8,128)(2,1)S(1)}, bf16[192,768]{1,0:T(8,128)(2,1)S(1)}, u32[]{:S(2)}, u32[]{:S(2)}) collective-permute-start(bf16[192,768]{1,0:T(8,128)(2,1)S(1)} %bitcast.160), channel_id=1, source_target_pairs={{0,1},{1,0},{2,3},{3,2},{4,5},{5,4},{6,7},{7,6},{8,9},{9,8},{10,11... | collective-permute-start | bytes 884744 | tf_op jit(solution)/shard_map/ppermute | solution.py:27
  78.1 11.6 %collective-permute-start.11 = (bf16[192,768]{1,0:T(8,128)(2,1)}, bf16[192,768]{1,0:T(8,128)(2,1)S(1)}, u32[]{:S(2)}, u32[]{:S(2)}) collective-permute-start(bf16[192,768]{1,0:T(8,128)(2,1)} %collective-permute-done.10.w2.v2), channel_id=1, source_target_pairs={{0,1},{1,0},{2,3},{3,2},{4,5},{5,4},{6,7},{7,6},{8,9},{9,8},{10,11... | collective-permute-start | bytes 884744 | tf_op jit(solution)/shard_map/ppermute | solution.py:27
  87.2 10.5 %collective-permute-start.26 = (bf16[192,768]{1,0:T(8,128)(2,1)S(1)}, bf16[192,768]{1,0:T(8,128)(2,1)S(1)}, u32[]{:S(2)}, u32[]{:S(2)}) collective-permute-start(bf16[192,768]{1,0:T(8,128)(2,1)S(1)} %copy-done.62), channel_id=1, source_target_pairs={{0,1},{1,0},{2,3},{3,2},{4,5},{5,4},{6,7},{7,6},{8,9},{9,8},{10,11... | collective-permute-start | bytes 884744 | tf_op jit(solution)/shard_map/ppermute | solution.py:27
  89.7 69.6 %collective-permute-start.28 = (bf16[768,768]{1,0:T(8,128)(2,1)}, bf16[768,768]{1,0:T(8,128)(2,1)}, u32[]{:S(2)}, u32[]{:S(2)}) collective-permute-start(bf16[768,768]{1,0:T(8,128)(2,1)} %up0.1), channel_id=1, source_target_pairs={{0,1},{1,0},{2,3},{3,2},{4,5},{5,4},{6,7},{7,6},{8,9},{9,8},{10,11... | collective-permute-start | bytes 3538952 | tf_op jit(solution)/shard_map/ppermute | solution.py:27
  89.7 69.6 %collective-permute-start.30 = (bf16[768,768]{1,0:T(8,128)(2,1)}, bf16[768,768]{1,0:T(8,128)(2,1)}, u32[]{:S(2)}, u32[]{:S(2)}) collective-permute-start(bf16[768,768]{1,0:T(8,128)(2,1)} %down0.1), channel_id=1, source_target_pairs={{0,1},{1,0},{2,3},{3,2},{4,5},{5,4},{6,7},{7,6},{8,9},{9,8},{10,11... | collective-permute-start | bytes 3538952 | tf_op jit(solution)/shard_map/ppermute | solution.py:27
  92.6 66.8 %collective-permute-start.29 = (bf16[768,768]{1,0:T(8,128)(2,1)}, bf16[768,768]{1,0:T(8,128)(2,1)}, u32[]{:S(2)}, u32[]{:S(2)}) collective-permute-start(bf16[768,768]{1,0:T(8,128)(2,1)} %collective-permute-done.19.up2), channel_id=1, source_target_pairs={{0,1},{1,0},{2,3},{3,2},{4,5},{5,4},{6,7},{7,6},{8,9},{9,8},{10,11... | collective-permute-start | bytes 3538952 | tf_op jit(solution)/shard_map/ppermute | solution.py:27
  92.6 66.8 %collective-permute-start.31 = (bf16[768,768]{1,0:T(8,128)(2,1)}, bf16[768,768]{1,0:T(8,128)(2,1)}, u32[]{:S(2)}, u32[]{:S(2)}) collective-permute-start(bf16[768,768]{1,0:T(8,128)(2,1)} %collective-permute-done.22.down2), channel_id=1, source_target_pairs={{0,1},{1,0},{2,3},{3,2},{4,5},{5,4},{6,7},{7,6},{8,9},{9,8},{10,11... | collective-permute-start | bytes 3538952 | tf_op jit(solution)/shard_map/ppermute | solution.py:27
  124.8 11.5 %collective-permute-start.23 = (bf16[64,896]{1,0:T(8,128)(2,1)}, bf16[64,896]{1,0:T(8,128)(2,1)}, u32[]{:S(2)}, u32[]{:S(2)}) collective-permute-start(bf16[64,896]{1,0:T(8,128)(2,1)} %get-tuple-element.156), channel_id=1, source_target_pairs={{0,16},{4,20},{8,24},{12,28},{16,0},{20,4},{24,8},{28,12},{1,17},{... | collective-permute-start | bytes 344072 | tf_op jit(solution)/shard_map/ppermute | solution.py:27
  136.3 23.0 %collective-permute-start.27 = (bf16[192,768]{1,0:T(8,128)(2,1)}, bf16[192,768]{1,0:T(8,128)(2,1)}, u32[]{:S(2)}, u32[]{:S(2)}) collective-permute-start(bf16[192,768]{1,0:T(8,128)(2,1)} %collective-permute-done.18.out2), channel_id=1, source_target_pairs={{0,1},{1,0},{2,3},{3,2},{4,5},{5,4},{6,7},{7,6},{8,9},{9,8},{10,11... | collective-permute-start | bytes 884744 | tf_op jit(solution)/shard_map/ppermute | solution.py:27
  202.7 25.9 %collective-permute-start.33 = (bf16[512,768]{1,0:T(8,128)(2,1)S(1)}, bf16[512,768]{1,0:T(8,128)(2,1)}, u32[]{:S(2)}, u32[]{:S(2)}) collective-permute-start(bf16[512,768]{1,0:T(8,128)(2,1)S(1)} %get-tuple-element.166.r0), channel_id=1, source_target_pairs={{0,2},{1,3},{2,0},{3,1},{4,6},{5,7},{6,4},{7,5},{8,10},{9,11},{10,... | collective-permute-start | bytes 2359304 | tf_op jit(solution)/shard_map/ppermute | solution.py:27
  205.3 21.6 %collective-permute-start.37 = (bf16[768,768]{1,0:T(8,128)(2,1)S(1)}, bf16[768,768]{1,0:T(8,128)(2,1)S(1)}, u32[]{:S(2)}, u32[]{:S(2)}) collective-permute-start(bf16[768,768]{1,0:T(8,128)(2,1)S(1)} %convolution_convert_fusion.4), channel_id=1, source_target_pairs={{0,1},{1,0},{2,3},{3,2},{4,5},{5,4},{6,7},{7,6},{8,9},{9,8},{10,11... | collective-permute-start | bytes 3538952 | tf_op jit(solution)/shard_map/ppermute | solution.py:27
  211.8 18.6 %collective-permute-start.42 = (bf16[768,768]{1,0:T(8,128)(2,1)S(1)}, bf16[768,768]{1,0:T(8,128)(2,1)S(1)}, u32[]{:S(2)}, u32[]{:S(2)}) collective-permute-start(bf16[768,768]{1,0:T(8,128)(2,1)S(1)} %convolution_convert_fusion), channel_id=1, source_target_pairs={{0,1},{1,0},{2,3},{3,2},{4,5},{5,4},{6,7},{7,6},{8,9},{9,8},{10,11... | collective-permute-start | bytes 3538952 | tf_op jit(solution)/shard_map/ppermute | solution.py:27
  212.7 19.0 %collective-permute-start.41 = (bf16[768,768]{1,0:T(8,128)(2,1)S(1)}, bf16[768,768]{1,0:T(8,128)(2,1)S(1)}, u32[]{:S(2)}, u32[]{:S(2)}) collective-permute-start(bf16[768,768]{1,0:T(8,128)(2,1)S(1)} %convolution_convert_fusion.2), channel_id=1, source_target_pairs={{0,1},{1,0},{2,3},{3,2},{4,5},{5,4},{6,7},{7,6},{8,9},{9,8},{10,11... | collective-permute-start | bytes 3538952 | tf_op jit(solution)/shard_map/ppermute | solution.py:27
  226.7 10.1 %collective-permute-start.32 = (bf16[512,768]{1,0:T(8,128)(2,1)S(1)}, bf16[512,768]{1,0:T(8,128)(2,1)S(1)}, u32[]{:S(2)}, u32[]{:S(2)}) collective-permute-start(bf16[512,768]{1,0:T(8,128)(2,1)S(1)} %get-tuple-element.166.r0), channel_id=1, source_target_pairs={{0,1},{1,0},{2,3},{3,2},{4,5},{5,4},{6,7},{7,6},{8,9},{9,8},{10,11... | collective-permute-start | bytes 2359304 | tf_op jit(solution)/shard_map/ppermute | solution.py:27
  230.4 16.5 %collective-permute-start.34 = (bf16[512,768]{1,0:T(8,128)(2,1)}, bf16[512,768]{1,0:T(8,128)(2,1)}, u32[]{:S(2)}, u32[]{:S(2)}) collective-permute-start(bf16[512,768]{1,0:T(8,128)(2,1)} %collective-permute-done.33.r2), channel_id=1, source_target_pairs={{0,1},{1,0},{2,3},{3,2},{4,5},{5,4},{6,7},{7,6},{8,9},{9,8},{10,11... | collective-permute-start | bytes 2359304 | tf_op jit(solution)/shard_map/ppermute | solution.py:27
  231.6 21.7 %collective-permute-start.47 = (bf16[4,96,768]{2,1,0:T(8,128)(2,1)}, bf16[4,96,768]{2,1,0:T(8,128)(2,1)}, u32[]{:S(2)}, u32[]{:S(2)}) collective-permute-start(bf16[4,96,768]{2,1,0:T(8,128)(2,1)} %dynamic-slice_bitcast_fusion.3), channel_id=1, source_target_pairs={{0,4},{4,0},{8,12},{12,8},{16,20},{20,16},{24,28},{28,24},{1,5},{5... | collective-permute-start | bytes 1769480 | tf_op jit(solution)/shard_map/ppermute | solution.py:27
  235.1 34.4 %collective-permute-start.36 = (bf16[768,768]{1,0:T(8,128)(2,1)}, bf16[768,768]{1,0:T(8,128)(2,1)}, u32[]{:S(2)}, u32[]{:S(2)}) collective-permute-start(bf16[768,768]{1,0:T(8,128)(2,1)} %convolution_convert_fusion.6), channel_id=1, source_target_pairs={{0,1},{1,0},{2,3},{3,2},{4,5},{5,4},{6,7},{7,6},{8,9},{9,8},{10,11... | collective-permute-start | bytes 3538952 | tf_op jit(solution)/shard_map/ppermute | solution.py:27
  236.5 33.0 %collective-permute-start.80 = (bf16[768,768]{1,0:T(8,128)(2,1)}, bf16[768,768]{1,0:T(8,128)(2,1)}, u32[]{:S(2)}, u32[]{:S(2)}) collective-permute-start(bf16[768,768]{1,0:T(8,128)(2,1)} %add_convert_fusion.3), channel_id=1, source_target_pairs={{0,2},{1,3},{2,0},{3,1},{4,6},{5,7},{6,4},{7,5},{8,10},{9,11},{10,... | collective-permute-start | bytes 3538952 | tf_op jit(solution)/shard_map/ppermute | solution.py:27
  237.7 22.6 %collective-permute-start.46 = (bf16[4,96,768]{2,1,0:T(8,128)(2,1)}, bf16[4,96,768]{2,1,0:T(8,128)(2,1)}, u32[]{:S(2)}, u32[]{:S(2)}) collective-permute-start(bf16[4,96,768]{2,1,0:T(8,128)(2,1)} %dynamic-slice_bitcast_fusion.4), channel_id=1, source_target_pairs={{0,4},{4,0},{8,12},{12,8},{16,20},{20,16},{24,28},{28,24},{1,5},{5... | collective-permute-start | bytes 1769480 | tf_op jit(solution)/shard_map/ppermute | solution.py:27
  246.8 25.0 %collective-permute-start.38 = (bf16[128,768]{1,0:T(8,128)(2,1)S(1)}, bf16[128,768]{1,0:T(8,128)(2,1)S(1)}, u32[]{:S(2)}, u32[]{:S(2)}) collective-permute-start(bf16[128,768]{1,0:T(8,128)(2,1)S(1)} %get-tuple-element.182.sent_ref), channel_id=1, source_target_pairs={{0,8},{4,12},{8,0},{12,4},{16,24},{20,28},{24,16},{28,20},{1,9},{5... | collective-permute-start | bytes 589832 | tf_op jit(solution)/shard_map/ppermute | solution.py:27
  253.3 73.2 %collective-permute-start.53 = (bf16[64,768]{1,0:T(8,128)(2,1)S(1)}, bf16[64,768]{1,0:T(8,128)(2,1)S(1)}, u32[]{:S(2)}, u32[]{:S(2)}) collective-permute-start(bf16[64,768]{1,0:T(8,128)(2,1)S(1)} %get-tuple-element.219), channel_id=1, source_target_pairs={{0,16},{4,20},{8,24},{12,28},{16,0},{20,4},{24,8},{28,12},{1,17},{... | collective-permute-start | bytes 294920 | tf_op jit(solution)/shard_map/ppermute | solution.py:27
  269.0 19.1 %collective-permute-start.75 = (bf16[2,96,768]{2,1,0:T(8,128)(2,1)S(1)}, bf16[2,96,768]{2,1,0:T(8,128)(2,1)S(1)}, u32[]{:S(2)}, u32[]{:S(2)}) collective-permute-start(bf16[2,96,768]{2,1,0:T(8,128)(2,1)S(1)} %dynamic-slice_bitcast_fusion.7), channel_id=1, source_target_pairs={{0,8},{4,12},{8,0},{12,4},{16,24},{20,28},{24,16},{28,20},{1,9},{5... | collective-permute-start | bytes 884744 | tf_op jit(solution)/shard_map/ppermute | solution.py:27
  272.0 11.3 %collective-permute-start.43 = (bf16[64,768]{1,0:T(8,128)(2,1)S(1)}, bf16[64,768]{1,0:T(8,128)(2,1)S(1)}, u32[]{:S(2)}, u32[]{:S(2)}) collective-permute-start(bf16[64,768]{1,0:T(8,128)(2,1)S(1)} %get-tuple-element.188), channel_id=1, source_target_pairs={{0,16},{4,20},{8,24},{12,28},{16,0},{20,4},{24,8},{28,12},{1,17},{... | collective-permute-start | bytes 294920 | tf_op jit(solution)/shard_map/ppermute | solution.py:27
  273.6 17.5 %collective-permute-start.78 = (bf16[1,96,768]{2,1,0:T(8,128)(2,1)S(1)}, bf16[1,96,768]{2,1,0:T(8,128)(2,1)S(1)}, u32[]{:S(2)}, u32[]{:S(2)}) collective-permute-start(bf16[1,96,768]{2,1,0:T(8,128)(2,1)S(1)} %constant_dynamic-slice_fusion.1), channel_id=1, source_target_pairs={{0,16},{4,20},{8,24},{12,28},{16,0},{20,4},{24,8},{28,12},{1,17},{... | collective-permute-start | bytes 442376 | tf_op jit(solution)/shard_map/ppermute | solution.py:27
  288.0 19.0 %collective-permute-start.49 = (bf16[768,384]{1,0:T(8,128)(2,1)S(1)}, bf16[768,384]{1,0:T(8,128)(2,1)S(1)}, u32[]{:S(2)}, u32[]{:S(2)}) collective-permute-start(bf16[768,384]{1,0:T(8,128)(2,1)S(1)} %get-tuple-element.204), channel_id=1, source_target_pairs={{0,1},{1,0},{2,3},{3,2},{4,5},{5,4},{6,7},{7,6},{8,9},{9,8},{10,11... | collective-permute-start | bytes 1769480 | tf_op jit(solution)/shard_map/ppermute | solution.py:27
  289.0 25.8 %collective-permute-start.81 = (bf16[4,96,768]{2,1,0:T(8,128)(2,1)S(1)}, bf16[4,96,768]{2,1,0:T(8,128)(2,1)S(1)}, u32[]{:S(2)}, u32[]{:S(2)}) collective-permute-start(bf16[4,96,768]{2,1,0:T(8,128)(2,1)S(1)} %dynamic-slice_bitcast_fusion.2), channel_id=1, source_target_pairs={{0,4},{4,0},{8,12},{12,8},{16,20},{20,16},{24,28},{28,24},{1,5},{5... | collective-permute-start | bytes 1769480 | tf_op jit(solution)/shard_map/ppermute | solution.py:27
  290.7 16.2 %collective-permute-start.44 = (bf16[64,768]{1,0:T(8,128)(2,1)S(1)}, bf16[64,768]{1,0:T(8,128)(2,1)S(1)}, u32[]{:S(2)}, u32[]{:S(2)}) collective-permute-start(bf16[64,768]{1,0:T(8,128)(2,1)S(1)} %get-tuple-element.198), channel_id=1, source_target_pairs={{0,4},{4,0},{8,12},{12,8},{16,20},{20,16},{24,28},{28,24},{1,5},{5... | collective-permute-start | bytes 294920 | tf_op jit(solution)/shard_map/ppermute | solution.py:27
  298.4 17.7 %collective-permute-start.48 = (bf16[768,384]{1,0:T(8,128)(2,1)S(1)}, bf16[768,384]{1,0:T(8,128)(2,1)S(1)}, u32[]{:S(2)}, u32[]{:S(2)}) collective-permute-start(bf16[768,384]{1,0:T(8,128)(2,1)S(1)} %get-tuple-element.202), channel_id=1, source_target_pairs={{0,1},{1,0},{2,3},{3,2},{4,5},{5,4},{6,7},{7,6},{8,9},{9,8},{10,11... | collective-permute-start | bytes 1769480 | tf_op jit(solution)/shard_map/ppermute | solution.py:27
  307.2 16.2 %collective-permute-start.71 = (bf16[768,384]{1,0:T(8,128)(2,1)S(1)}, bf16[768,384]{1,0:T(8,128)(2,1)S(1)}, u32[]{:S(2)}, u32[]{:S(2)}) collective-permute-start(bf16[768,384]{1,0:T(8,128)(2,1)S(1)} %add_convert_fusion.8), channel_id=1, source_target_pairs={{0,2},{1,3},{2,0},{3,1},{4,6},{5,7},{6,4},{7,5},{8,10},{9,11},{10,... | collective-permute-start | bytes 1769480 | tf_op jit(solution)/shard_map/ppermute | solution.py:27
  314.1 30.6 %collective-permute-start.76 = (bf16[1,96,768]{2,1,0:T(8,128)(2,1)}, bf16[1,96,768]{2,1,0:T(8,128)(2,1)}, u32[]{:S(2)}, u32[]{:S(2)}) collective-permute-start(bf16[1,96,768]{2,1,0:T(8,128)(2,1)} %constant_dynamic-slice_fusion.2), channel_id=1, source_target_pairs={{0,16},{4,20},{8,24},{12,28},{16,0},{20,4},{24,8},{28,12},{1,17},{... | collective-permute-start | bytes 442376 | tf_op jit(solution)/shard_map/ppermute | solution.py:27
  314.8 29.9 %collective-permute-start.79 = (bf16[1,96,768]{2,1,0:T(8,128)(2,1)}, bf16[1,96,768]{2,1,0:T(8,128)(2,1)S(1)}, u32[]{:S(2)}, u32[]{:S(2)}) collective-permute-start(bf16[1,96,768]{2,1,0:T(8,128)(2,1)} %add_convert_fusion.11), channel_id=1, source_target_pairs={{0,2},{1,3},{2,0},{3,1},{4,6},{5,7},{6,4},{7,5},{8,10},{9,11},{10,... | collective-permute-start | bytes 442376 | tf_op jit(solution)/shard_map/ppermute | solution.py:27
  316.2 11.7 %collective-permute-start.50 = (bf16[64,768]{1,0:T(8,128)(2,1)S(1)}, bf16[64,768]{1,0:T(8,128)(2,1)S(1)}, u32[]{:S(2)}, u32[]{:S(2)}) collective-permute-start(bf16[64,768]{1,0:T(8,128)(2,1)S(1)} %get-tuple-element.209), channel_id=1, source_target_pairs={{0,16},{4,20},{8,24},{12,28},{16,0},{20,4},{24,8},{28,12},{1,17},{... | collective-permute-start | bytes 294920 | tf_op jit(solution)/shard_map/ppermute | solution.py:27
  323.5 14.2 %collective-permute-start.82 = (bf16[2,96,768]{2,1,0:T(8,128)(2,1)}, bf16[2,96,768]{2,1,0:T(8,128)(2,1)}, u32[]{:S(2)}, u32[]{:S(2)}) collective-permute-start(bf16[2,96,768]{2,1,0:T(8,128)(2,1)} %dynamic-slice_bitcast_fusion.5), channel_id=1, source_target_pairs={{0,8},{4,12},{8,0},{12,4},{16,24},{20,28},{24,16},{28,20},{1,9},{5... | collective-permute-start | bytes 884744 | tf_op jit(solution)/shard_map/ppermute | solution.py:27
  349.3 57.8 %collective-permute-start.54 = (bf16[512,768]{1,0:T(8,128)(2,1)S(1)}, bf16[512,768]{1,0:T(8,128)(2,1)S(1)}, u32[]{:S(2)}, u32[]{:S(2)}) collective-permute-start(bf16[512,768]{1,0:T(8,128)(2,1)S(1)} %get-tuple-element.223.r0), channel_id=1, source_target_pairs={{0,1},{1,0},{2,3},{3,2},{4,5},{5,4},{6,7},{7,6},{8,9},{9,8},{10,11... | collective-permute-start | bytes 2359304 | tf_op jit(solution)/shard_map/ppermute | solution.py:27
  349.3 33.2 %collective-permute-start.55 = (bf16[512,768]{1,0:T(8,128)(2,1)S(1)}, bf16[512,768]{1,0:T(8,128)(2,1)S(1)}, u32[]{:S(2)}, u32[]{:S(2)}) collective-permute-start(bf16[512,768]{1,0:T(8,128)(2,1)S(1)} %get-tuple-element.223.r0), channel_id=1, source_target_pairs={{0,2},{1,3},{2,0},{3,1},{4,6},{5,7},{6,4},{7,5},{8,10},{9,11},{10,... | collective-permute-start | bytes 2359304 | tf_op jit(solution)/shard_map/ppermute | solution.py:27
  351.0 26.8 %collective-permute-start.61 = (bf16[768,384]{1,0:T(8,128)(2,1)}, bf16[768,384]{1,0:T(8,128)(2,1)}, u32[]{:S(2)}, u32[]{:S(2)}) collective-permute-start(bf16[768,384]{1,0:T(8,128)(2,1)} %copy-done.90), channel_id=1, source_target_pairs={{0,1},{1,0},{2,3},{3,2},{4,5},{5,4},{6,7},{7,6},{8,9},{9,8},{10,11... | collective-permute-start | bytes 1769480 | tf_op jit(solution)/shard_map/ppermute | solution.py:27
  351.2 29.5 %collective-permute-start.57 = (bf16[768,384]{1,0:T(8,128)(2,1)}, bf16[768,384]{1,0:T(8,128)(2,1)}, u32[]{:S(2)}, u32[]{:S(2)}) collective-permute-start(bf16[768,384]{1,0:T(8,128)(2,1)} %get-tuple-element.225), channel_id=1, source_target_pairs={{0,1},{1,0},{2,3},{3,2},{4,5},{5,4},{6,7},{7,6},{8,9},{9,8},{10,11... | collective-permute-start | bytes 1769480 | tf_op jit(solution)/shard_map/ppermute | solution.py:27
  379.1 9.5 %collective-permute-start.62 = (bf16[4,96,384]{2,1,0:T(8,128)(2,1)S(1)}, bf16[4,96,384]{2,1,0:T(8,128)(2,1)S(1)}, u32[]{:S(2)}, u32[]{:S(2)}) collective-permute-start(bf16[4,96,384]{2,1,0:T(8,128)(2,1)S(1)} %dynamic-slice_bitcast_fusion.9), channel_id=1, source_target_pairs={{0,4},{4,0},{8,12},{12,8},{16,20},{20,16},{24,28},{28,24},{1,5},{5... | collective-permute-start | bytes 884744 | tf_op jit(solution)/shard_map/ppermute | solution.py:27
  382.0 9.7 %collective-permute-start.58 = (bf16[4,96,384]{2,1,0:T(8,128)(2,1)S(1)}, bf16[4,96,384]{2,1,0:T(8,128)(2,1)S(1)}, u32[]{:S(2)}, u32[]{:S(2)}) collective-permute-start(bf16[4,96,384]{2,1,0:T(8,128)(2,1)S(1)} %dynamic-slice_bitcast_fusion.10), channel_id=1, source_target_pairs={{0,4},{4,0},{8,12},{12,8},{16,20},{20,16},{24,28},{28,24},{1,5},{5... | collective-permute-start | bytes 884744 | tf_op jit(solution)/shard_map/ppermute | solution.py:27
  382.5 25.5 %collective-permute-start.56 = (bf16[512,768]{1,0:T(8,128)(2,1)S(1)}, bf16[512,768]{1,0:T(8,128)(2,1)S(1)}, u32[]{:S(2)}, u32[]{:S(2)}) collective-permute-start(bf16[512,768]{1,0:T(8,128)(2,1)S(1)} %collective-permute-done.55.r2), channel_id=1, source_target_pairs={{0,1},{1,0},{2,3},{3,2},{4,5},{5,4},{6,7},{7,6},{8,9},{9,8},{10,11... | collective-permute-start | bytes 2359304 | tf_op jit(solution)/shard_map/ppermute | solution.py:27
  (158 other events, 1299.6 us)

commit v2 on v1

--- a/solution.py
+++ b/solution.py
@@ -13,8 +13,7 @@
 SPAN = 4096
 LANES = 128
 STRIPE = 128
-TILE = 256
-VMEM_LIMIT = 44 << 20
+VMEM_LIMIT = 28 << 20
 
 
 epsilon = 1e-05
@@ -43,31 +42,35 @@
     return lax.optimization_barrier((value,) + others)[0]
 
 
-def scatter_start(blocks):
-    got = swap((blocks[1], blocks[3]), "tp", 1)
-    return [
-        (mine.astype(f32) + far.astype(f32)).astype(bf16)
-        for mine, far in zip((blocks[0], blocks[2]), got)
-    ]
-
-
-def scatter_far(blocks):
-    far = swap(blocks[1], "tp", 2)
-    return [(blocks[0].astype(f32) + far.astype(f32)).astype(bf16)]
-
-
-def scatter_level(blocks, seq_index, size, last=False):
-    bit = (seq_index // size) % 2
-    views = [b.reshape(b.shape[0] // 2, 2, b.shape[1], b.shape[2]) for b in blocks]
-    keep = [lax.dynamic_index_in_dim(v, bit, axis=1, keepdims=False) for v in views]
-    send = [lax.dynamic_index_in_dim(v, 1 - bit, axis=1, keepdims=False) for v in views]
-    got = swap(tuple(send), "seq", size)
-    total = [k.astype(f32) + g.astype(f32) for k, g in zip(keep, got)]
-    return total if last else [t.astype(bf16) for t in total]
-
-
-def by_targets(blocks, count):
-    return [b.reshape(count, b.shape[0] // count, b.shape[1]) for b in blocks]
+class Scatter:
+    def __init__(self, name, mine, theirs, bits, hops):
+        self.name, self.bits, self.hops = name, bits, list(hops)
+        self.keep, self.send, self.way = mine, theirs, ("tp", 1)
+
+    def hop(self, other=None):
+        operands = [self.keep, swap(self.send, *self.way)]
+        tiles, rows, columns = self.keep.shape
+        if other is not None:
+            operands += [other.keep, swap(other.send, *other.way)]
+            columns += other.keep.shape[2]
+        if not self.hops:
+            kernel, outs = last_tile_kernel, (((tiles, rows, columns), f32),)
+        else:
+            following = self.hops.pop(0)
+            far = following == "far"
+            self.way = ("tp", 2) if far else ("seq", 1 << following)
+            kernel = functools.partial(route_kernel, None if far else following)
+            outs = (((tiles // 2, rows, columns), bf16),) * 2
+        size = tiles * rows * columns * 2
+        result = call(
+            kernel, outs, self.name + "_route", scalars=1, us=0.5 + size / 1.2e6, limit=16 << 20
+        )(self.bits, *operands)
+        self.keep = result[0]
+        self.send = result[-1]
+        return result
+
+    def wait_for(self, *others):
+        self.send = after(self.send, *others)
 
 
 def sum_merge(a, b, use):
@@ -117,7 +120,7 @@
     message_ref[...] = encode(facing)
 
 
-def exchange(parts, name, flags, own, message, waits=((), ())):
+def exchange(parts, name, flags, own, message, waits=((), ()), marks_of=None):
     marks, width = own.shape
     first = call(
         functools.partial(merge_first_kernel, parts),
@@ -130,7 +133,10 @@
         name + "_next",
     )
     own, sent = first(flags, after(own, *waits[0]), swap(message, "seq", 1))
+    first_own = own
     own, message = following(flags, after(own, *waits[1]), sent, swap(sent, "seq", 2))
+    if marks_of is not None:
+        marks_of += [first_own, own]
     return own, swap(message, "seq", 4)
 
 
@@ -150,7 +156,7 @@
     return pl.CostEstimate(flops=0, bytes_accessed=int(us * 3.3e6), transcendentals=0)
 
 
-def call(kernel, outs, name, scratch=(), limit=24 << 20, us=1.0, scalars=0):
+def call(kernel, outs, name, scratch=(), limit=12 << 20, us=1.0, scalars=0):
     outs = tuple(jax.ShapeDtypeStruct(shape, dtype) for shape, dtype in outs)
 
     def run(*operands):
@@ -407,12 +413,12 @@
     flags_ref[14:16, :] = jnp.zeros((2, LANES), f32)
 
 
-def query_key_kernel(flat_ref, q0, k0, q1, k1, bias_ref, member_ref, query_ref, keys_ref, part_ref, message_ref):
+def query_key_kernel(flat_ref, q0, k0, q1, k1, s0, s1, member_ref, query_ref, keys_ref, part_ref, message_ref):
     channels = query_ref.shape[2]
     scale = HEAD_DIM ** (-0.25)
     parts = []
-    for r, (q, k) in enumerate(((q0, k0), (q1, k1))):
-        query = dot_t(flat_ref[...], q[...]) + bias_ref[r : r + 1, :]
+    for r, (q, k, small) in enumerate(((q0, k0, s0), (q1, k1, s1))):
+        query = dot_t(flat_ref[...], q[...]) + small_row(small, 0, channels)
         query = (scale * query).astype(bf16)
         keys = (scale * dot_t(flat_ref[...], k[...])).astype(bf16)
         query_ref[r] = query
@@ -421,6 +427,93 @@
     part = jnp.concatenate(parts, axis=1)
     part_ref[...] = part
     message_ref[...] = part.astype(bf16)
+
+
+def route_kernel(level, bits_ref, *refs):
+    keep_out, send_out = refs[-2:]
+    half = keep_out.shape[0]
+
+    def total(i):
+        sums = [
+            (refs[k][i].astype(f32) + refs[k + 1][i].astype(f32)).astype(bf16)
+            for k in range(0, len(refs) - 2, 2)
+        ]
+        return jnp.concatenate(sums, axis=1) if len(sums) > 1 else sums[0]
+
+    for i in range(half):
+        if level is None:
+            keep, send = i, half + i
+        else:
+            bit = bits_ref[level]
+            keep, send = 2 * i + bit, 2 * i + 1 - bit
+        keep_out[i] = total(keep)
+        send_out[i] = total(send)
+
+
+def last_tile_kernel(bits_ref, keep_ref, got_ref, out_ref):
+    for i in range(out_ref.shape[0]):
+        out_ref[i] = keep_ref[i].astype(f32) + got_ref[i].astype(f32)
+
+
+def put_tiles(product, r, mine_ref, theirs_ref):
+    ref = theirs_ref if r % 2 else mine_ref
+    places = ref.shape[0] // 2
+    rows = product.shape[0] // places
+    first = places if r >= 2 else 0
+    for place in range(places):
+        ref[first + place, :rows] = product[place * rows : (place + 1) * rows].astype(bf16)
+
+
+def weight_gradient_kernel(side_ref, units_ref, mine_ref, theirs_ref, turned_ref):
+    turned_ref[...] = side_ref[...].T
+    columns = mine_ref.shape[2]
+    for r in range(units_ref.shape[1] // columns):
+        product = dot(turned_ref[...], units_ref[:, r * columns : (r + 1) * columns])
+        put_tiles(product, r, mine_ref, theirs_ref)
+
+
+def small_kernel(query_ref, value_ref, taps_ref, flipped_ref, up_ref, out_ref):
+    columns = out_ref.shape[1]
+
+    def row(pieces):
+        width = sum(piece.shape[1] for piece in pieces)
+        return jnp.concatenate(pieces + [jnp.zeros((1, columns - width), f32)], axis=1)
+
+    heads = range(query_ref.shape[0])
+    rows = []
+    for ref in (query_ref, value_ref):
+        value = ref[...].astype(f32)
+        rows.append(row([value[j : j + 1] for j in heads]))
+    for ref in (taps_ref, flipped_ref):
+        value = ref[...].astype(f32)
+        rows += [row([value[j : j + 1]]) for j in heads]
+    rows.append(up_ref[...].astype(f32).reshape(1, columns))
+    rows.append(jnp.zeros((out_ref.shape[0] - len(rows), columns), f32))
+    out_ref[...] = jnp.concatenate(rows, axis=0).astype(bf16)
+
+
+def small_row(ref, at, width):
+    return ref[:, :width].astype(f32)[at : at + 1]
+
+
+def bundle_kernel(rank_ref, up_ref, value_ref, taps_ref, norm_ref, out_ref):
+    ranks, channels = value_ref.shape
+    columns = out_ref.shape[1]
+    heads = taps_ref.shape[0] // ranks
+    for r in range(ranks):
+        at = 4 * (r ^ rank_ref[0])
+        value = value_ref[r : r + 1, :]
+        rows = (
+            up_ref[:, r * columns : (r + 1) * columns],
+            jnp.concatenate((value, jnp.zeros((1, columns - channels), f32)), axis=1),
+            jnp.concatenate([taps_ref[r * heads + j : r * heads + j + 1] for j in range(heads)], axis=1),
+        )
+        for k, row in enumerate(rows):
+            out_ref[pl.ds(at + k, 1), :] = row
+        out_ref[pl.ds(at + 3, 1), :] = jnp.zeros((1, columns), f32)
+    norms = norm_ref.shape[0]
+    out_ref[4 * ranks : 4 * ranks + norms, :] = norm_ref[...]
+    out_ref[4 * ranks + norms :, :] = jnp.zeros((out_ref.shape[0] - 4 * ranks - norms, columns), f32)
 
 
 def land_kernel(flags_ref, count_ref, own0, got0, own1, got1, query_ref, keys_ref, kernel_ref):
@@ -441,11 +534,12 @@
         kernel_ref[p] = powers / pair_sums(powers)
 
 
-def value_kernel(flat_ref, w0, w1, w2, w3, bias_ref, values_ref, head_ref, tail_ref):
+def value_kernel(flat_ref, w0, w1, w2, w3, s0, s1, s2, s3, values_ref, head_ref, tail_ref):
     reach = head_ref.shape[0]
     heads, tails = [], []
-    for r, w in enumerate((w0, w1, w2, w3)):
-        values = (dot_t(flat_ref[...], w[...]) + bias_ref[r : r + 1, :]).astype(bf16)
+    channels = values_ref.shape[2]
+    for r, (w, small) in enumerate(((w0, s0), (w1, s1), (w2, s2), (w3, s3))):
+        values = (dot_t(flat_ref[...], w[...]) + small_row(small, 1, channels)).astype(bf16)
         values_ref[r] = values
         heads.append(values[:reach])
         tails.append(values[values.shape[0] - reach :])
@@ -569,7 +663,7 @@
 
 
 def context_kernel(own_ref, got_ref, inverse_ref, weights_ref, values_ref, before_ref, after_ref,
-                   flags_ref, taps_ref, context_ref, mixed_ref, low_ref, stats_ref):
+                   flags_ref, s0, s1, s2, s3, context_ref, mixed_ref, low_ref, stats_ref):
     groups, width, channels = values_ref.shape
     heads = channels // HEAD_DIM
     reach = before_ref.shape[0]
@@ -598,8 +692,9 @@
             flags_ref,
         )
         filters = [
-            toeplitz(taps_ref[r * heads + j : r * heads + j + 1, :], STRIPE, STRIPE + 2 * reach)
-            .astype(bf16)
+            toeplitz(
+                small_row((s0, s1, s2, s3)[r], 2 + j, 2 * LANES), STRIPE, STRIPE + 2 * reach
+            ).astype(bf16)
             for j in range(heads)
         ]
         context_ref[r] = (nystrom + convolve(rim, filters)).astype(bf16)
@@ -632,7 +727,7 @@
 
 
 def conv_back_kernel(back_ref, before_ref, after_ref, values_ref, vbefore_ref, vafter_ref, flags_ref,
-                     flipped_ref, conv_ref, taps_ref):
+                     s0, s1, s2, s3, conv_ref, taps_ref):
     groups, width, channels = back_ref.shape
     heads = channels // HEAD_DIM
     reach = before_ref.shape[0]
@@ -648,7 +743,9 @@
             flags_ref,
         )
         filters = [
-            toeplitz(flipped_ref[r * heads + j : r * heads + j + 1, :], STRIPE, span).astype(bf16)
+            toeplitz(
+                small_row((s0, s1, s2, s3)[r], 2 + heads + j, 2 * LANES), STRIPE, span
+            ).astype(bf16)
             for j in range(heads)
         ]
         conv_ref[r] = convolve(rim, filters)
@@ -723,8 +820,9 @@
 def input_back_kernel(flags_ref, count_ref, flat_ref, query_direct_ref, key_direct_ref, back_values_ref,
                       query_own_ref, query_got_ref, query_more_ref, key_own_ref, key_got_ref,
                       key_more_ref, member_ref, back_input_ref, q0, q1, q2, q3, k0, k1, k2, k3, v0,
-                      v1, v2, v3, grad_ref, bias_ref, g0, g1, g2, g3, turned_ref):
+                      v1, v2, v3, grad_ref, mine_ref, theirs_ref, turned_ref, both_ref, weight_ref):
     groups, width, channels = back_values_ref.shape
+    model = flat_ref.shape[1]
     scale = HEAD_DIM ** (-0.25)
     member = member_ref[...]
     count = count_ref[:, 0:1]
@@ -737,33 +835,37 @@
             (key_own_ref, key_got_ref, key_more_ref),
         )
     ]
-    total = back_input_ref[...]
     turned_ref[...] = flat_ref[...].T
     for r in range(groups):
-        q, k, v = (q0, q1, q2, q3)[r], (k0, k1, k2, k3)[r], (v0, v1, v2, v3)[r]
+        q, k = (q0, q1, q2, q3)[r], (k0, k1, k2, k3)[r]
         both = []
         for (high, low), direct_ref in zip(sides, (query_direct_ref, key_direct_ref)):
             far = dot(member, group_of(high, r, channels)) + dot(member, group_of(low, r, channels))
             both.append((direct_ref[r] + far).astype(bf16))
-        bias_ref[r : r + 1, :] = scale * jnp.sum(both[0].astype(f32), axis=0, keepdims=True)
-        total = total + scale * (dot(both[0], q[...]) + dot(both[1], k[...]))
-        total = total + dot(back_values_ref[r], v[...])
-        (g0, g1, g2, g3)[r][...] = jnp.concatenate(
-            [(scale * dot(turned_ref[...], side)).astype(bf16) for side in both], axis=1
-        )
-    grad_ref[...] = total.astype(bf16)
-
-
-def value_output_kernel(flat_ref, back_values_ref, back_attention_ref, context_ref, g0, g1, g2, g3):
+        bias = scale * jnp.sum(both[0].astype(f32), axis=0, keepdims=True)
+        bias = jnp.concatenate((bias, jnp.zeros_like(bias)), axis=1)
+        at = slice(2 * r * channels, 2 * (r + 1) * channels)
+        both_ref[:, at] = jnp.concatenate(both, axis=1)
+        weight_ref[at, :] = jnp.concatenate((q[...], k[...]), axis=0)
+        put_tiles(scale * dot(turned_ref[...], both_ref[:, at]), r, mine_ref, theirs_ref)
+        ref = theirs_ref if r % 2 else mine_ref
+        places = ref.shape[0] // 2
+        more = ref.shape[1] - model // places
+        for place in range(places):
+            ref[(places if r >= 2 else 0) + place, model // places :] = jnp.broadcast_to(
+                bias, (more, bias.shape[1])
+            ).astype(bf16)
+    total = back_input_ref[...] + scale * dot(both_ref[...], weight_ref[...])
+    values = jnp.concatenate([back_values_ref[r] for r in range(groups)], axis=1)
+    weights = jnp.concatenate([v[...] for v in (v0, v1, v2, v3)], axis=0)
+    grad_ref[...] = (total + dot(values, weights)).astype(bf16)
+
+
+def value_output_kernel(flat_ref, back_values_ref, back_attention_ref, context_ref, mine_ref, theirs_ref):
     flat, back = flat_ref[...].T, back_attention_ref[...].T
-    for r, g in enumerate((g0, g1, g2, g3)):
-        g[...] = jnp.concatenate(
-            (
-                dot(back, context_ref[r]).astype(bf16),
-                dot(flat, back_values_ref[r]).astype(bf16),
-            ),
-            axis=1,
-        )
+    for r in range(context_ref.shape[0]):
+        product = (dot(back, context_ref[r]), dot(flat, back_values_ref[r]))
+        put_tiles(jnp.concatenate(product, axis=1), r, mine_ref, theirs_ref)
 
 
 def place_kernel(rank_ref, r0, r1, r2, r3, out_ref):
@@ -794,17 +896,15 @@
 
 def feed_kernel(
     flat_ref, context_ref, out0, out1, out2, out3, up0, up1, up2, up3, down0, down1, down2, down3,
-    up_bias_ref, params_ref, cotangent_ref,
+    s0, s1, s2, s3, p0, p1, p2, p3, p4, p5, cotangent_ref,
     layer_ref, back_input_ref, back_attention_ref, back_context_ref, active_ref, back_hidden_ref,
     first_low_ref, back_feed_ref, sums_ref, up_sums_ref,
     slope_ref, first_ref, total_ref,
 ):
     outs, ups, downs = (out0, out1, out2, out3), (up0, up1, up2, up3), (down0, down1, down2, down3)
     units = up0.shape[1]
-    tile = TILE
-    steps = units // tile
     output_bias, first_gain, first_shift, down_bias, second_gain, second_shift = [
-        params_ref[k : k + 1, :] for k in range(6)
+        p[...].astype(f32).reshape(1, flat_ref.shape[1]) for p in (p0, p1, p2, p3, p4, p5)
     ]
 
     def mean(value):
@@ -822,22 +922,13 @@
     first_low_ref[...] = first_out.astype(bf16)
     total_ref[...] = first_out + down_bias
     for r in range(len(ups)):
-
-        def forward(step, carry):
-            at = pl.multiple_of(step * tile, tile)
-            whole = pl.multiple_of(r * units + at, tile)
-            hidden = dot(first_low_ref[...], ups[r][:, pl.ds(at, tile)])
-            hidden = hidden + up_bias_ref[:, pl.ds(whole, tile)]
-            cdf = 0.5 * (1.0 + lax.erf(hidden * 0.7071067811865476))
-            slope_ref[:, pl.ds(whole, tile)] = cdf + hidden * (
-                0.3989422804014327 * jnp.exp(-0.5 * hidden * hidden)
-            )
-            active = (hidden * cdf).astype(bf16)
-            active_ref[:, pl.ds(whole, tile)] = active
-            total_ref[...] += dot(active, downs[r][pl.ds(at, tile), :])
-            return carry
-
-        lax.fori_loop(0, steps, forward, 0)
+        at = slice(r * units, (r + 1) * units)
+        hidden = dot(first_low_ref[...], ups[r][...]) + small_row((s0, s1, s2, s3)[r], 8, units)
+        cdf = 0.5 * (1.0 + lax.erf(hidden * 0.7071067811865476))
+        slope_ref[:, at] = cdf + hidden * (0.3989422804014327 * jnp.exp(-0.5 * hidden * hidden))
+        active = (hidden * cdf).astype(bf16)
+        active_ref[:, at] = active
+        total_ref[...] += dot(active, downs[r][...])
 
     value = total_ref[...]
     centred = value - mean(value)
@@ -854,20 +945,12 @@
     sums_ref[3:4, :] = jnp.sum(back_feed.astype(f32), axis=0, keepdims=True)
     total_ref[...] = back_second
     for r in range(len(ups)):
-
-        def backward(step, carry):
-            at = pl.multiple_of(step * tile, tile)
-            whole = pl.multiple_of(r * units + at, tile)
-            back_active = dot_t(back_feed_ref[...], downs[r][pl.ds(at, tile), :])
-            back_hidden = (back_active * slope_ref[:, pl.ds(whole, tile)]).astype(bf16)
-            back_hidden_ref[:, pl.ds(whole, tile)] = back_hidden
-            up_sums_ref[:, pl.ds(whole, tile)] = jnp.sum(
-                back_hidden.astype(f32), axis=0, keepdims=True
-            )
-            total_ref[...] += dot_t(back_hidden, ups[r][:, pl.ds(at, tile)])
-            return carry
-
-        lax.fori_loop(0, steps, backward, 0)
+        at = slice(r * units, (r + 1) * units)
+        back_active = dot_t(back_feed_ref[...], downs[r][...])
+        back_hidden = (back_active * slope_ref[:, at]).astype(bf16)
+        back_hidden_ref[:, at] = back_hidden
+        up_sums_ref[:, at] = jnp.sum(back_hidden.astype(f32), axis=0, keepdims=True)
+        total_ref[...] += dot_t(back_hidden, ups[r][...])
 
     back_first = total_ref[...]
     first_normed = first_ref[...]
@@ -883,7 +966,7 @@
         back_context_ref[r] = dot_t(back_attention, outs[r][...]).astype(bf16)
 
 
-def feed_layer(flat, context, outputs, ups, downs, up_bias, params, cotangent):
+def feed_layer(flat, context, outputs, ups, downs, smalls, params, cotangent):
     width, model = flat.shape
     ranks, units = len(ups), ups[0].shape[1]
     channels = outputs[0].shape[0]
@@ -903,7 +986,7 @@
             shape((6, model), f32),
             shape((1, ranks * units), f32),
         ),
-        in_specs=[whole] * 17,
+        in_specs=[whole] * (15 + len(smalls) + len(params)),
         out_specs=(whole,) * 10,
         scratch_shapes=[
             pltpu.VMEM((width, ranks * units), f32),
@@ -911,9 +994,9 @@
             pltpu.VMEM((width, model), f32),
         ],
         compiler_params=pltpu.CompilerParams(vmem_limit_bytes=VMEM_LIMIT),
-        cost_estimate=cost(35.0),
+        cost_estimate=cost(19.0),
         name="feed_layer",
-    )(flat, context, *outputs, *ups, *downs, up_bias, params, cotangent)
+    )(flat, context, *outputs, *ups, *downs, *smalls, *params, cotangent)
 
 
 def per_device(
@@ -952,9 +1035,6 @@
     groups = segment_sizes.shape[0] // rows
     place = jnp.stack((rank * groups + device // group, device % group)).astype(jnp.int32)
 
-    def by_rank(stacked):
-        return jnp.take(stacked, jnp.arange(ranks) ^ rank, axis=0)
-
     half = ((2, width, channels), bf16)
     full = ((ranks, width, channels), bf16)
     full32 = ((ranks, width, channels), f32)
@@ -966,38 +1046,20 @@
     half_sweeps = SWEEPS // 2
     saved = ((half_sweeps, 4, heads // 2, marks, LANES), f32)
 
-    small = jnp.concatenate(
-        (
-            query_bias.reshape(-1),
-            value_bias.reshape(-1),
-            conv_weight.reshape(-1),
-            up_bias.reshape(-1),
-        )
-    )
-    small_rows = -(-small.shape[0] // model)
-    small_rows += -small_rows % 16
-    small = jnp.pad(small, (0, small_rows * model - small.shape[0])).reshape(small_rows, model)
     turned = [w.T for w in (query_weight, key_weight, value_weight)]
+    (small,) = call(small_kernel, (((16, model), bf16),), "small")(
+        query_bias, value_bias, conv_weight, conv_weight[:, ::-1], up_bias
+    )
     query_far, key_far = swap((turned[0], turned[1]), "tp", 2)
     query_core, key_core = swap((turned[0], turned[1]), "tp", 1)
     small_far = swap(small, "tp", 2)
-    small_core = swap(small, "tp", 1)
-    smalls = [s.reshape(-1).astype(f32) for s in (small, small_core, small_far, swap(small_far, "tp", 1))]
+    smalls = (small, swap(small, "tp", 1), small_far, swap(small_far, "tp", 1))
     member, member_turned, count, flags = call(
         layout_kernel,
         (((width, marks), bf16), ((marks, width), bf16), tall, ((16, LANES), f32)),
         "layout",
         scalars=1,
     )(place, segment_sizes)
-    query_bias_all = jnp.stack([s[:channels] for s in smalls])
-    value_bias_all = jnp.stack([s[channels : 2 * channels] for s in smalls])
-    taps_all = jnp.concatenate(
-        [s[2 * channels : 2 * channels + own_heads * TAPS].reshape(own_heads, TAPS) for s in smalls]
-    )
-    up_start = 2 * channels + own_heads * TAPS
-    up_bias_all = jnp.concatenate([s[up_start : up_start + hidden_units] for s in smalls])
-    taps_wide = jnp.pad(taps_all, ((0, 0), (0, 2 * LANES - TAPS)))
-    taps_flipped = jnp.pad(taps_all[:, ::-1], ((0, 0), (0, 2 * LANES - TAPS)))
     flat = lax.dynamic_index_in_dim(tokens, rank, axis=0, keepdims=False)
     upstream = lax.dynamic_index_in_dim(cotangent, rank, axis=0, keepdims=False)
 
@@ -1006,15 +1068,6 @@
 
     query_blocks = (turned[0], query_core, query_far, swap(query_far, "tp", 1))
     key_blocks = (turned[1], key_core, key_far, swap(key_far, "tp", 1))
-    value_far = swap(after(turned[2], key_far), "tp", 2)
-    output_far = swap(after(output_weight, value_far), "tp", 2)
-    up_far = swap(after(up_weight, output_far), "tp", 2)
-    down_far = swap(after(down_weight, up_far), "tp", 2)
-    value_blocks = shards(turned[2], value_far)
-    output_blocks = shards(output_weight, output_far)
-    up_blocks = shards(up_weight, up_far)
-    down_blocks = shards(down_weight, down_far)
-
     query, keys, sums = [], [], []
     for pair in range(2):
         q, k, part, sent = call(
@@ -1025,18 +1078,26 @@
             key_blocks[2 * pair],
             query_blocks[2 * pair + 1],
             key_blocks[2 * pair + 1],
-            query_bias_all[2 * pair : 2 * pair + 2],
+            *smalls[2 * pair : 2 * pair + 2],
             member_turned,
         )
         query.append(q)
         keys.append(k)
-        sums += exchange(plain_parts(), "land", flags, part, sent)
+        if pair == 0:
+            value_far = swap(after(turned[2], query_far, key_far, small_far, sent), "tp", 2)
+            output_far = swap(after(output_weight, query_far, key_far, small_far, sent), "tp", 2)
+        steps = []
+        sums += exchange(plain_parts(), "land", flags, part, sent, marks_of=steps)
+    up_far = swap(after(up_weight, value_far, steps[0]), "tp", 2)
+    value_blocks = shards(turned[2], value_far)
+    output_blocks = shards(output_weight, output_far)
+    up_blocks = shards(up_weight, up_far)
     land_query, land_key, kernel = call(land_kernel, (message, message, squares), "land")(
         flags, count, *sums
     )
     values, value_head, value_tail = call(
         value_kernel, (full, edge, edge), "values", us=2.0
-    )(flat, *value_blocks, value_bias_all)
+    )(after(flat, output_far), *value_blocks, *smalls)
 
     def neighbours(head, tail):
         count = lax.axis_size("seq")
@@ -1050,8 +1111,11 @@
         (((marks, model + LANES), f32), ((marks, model + LANES), bf16)),
         "key_softmax",
         us=1.4,
-    )(*keys, values, after(land_query, up_far))
-    state, state_got = exchange(soft_parts(heads), "soft", flags, state, sent)
+    )(*keys, values, land_query)
+    steps = []
+    state, state_got = exchange(soft_parts(heads), "soft", flags, state, sent, marks_of=steps)
+    down_far = swap(after(down_weight, up_far, steps[0]), "tp", 2)
+    down_blocks = shards(down_weight, after(down_far, steps[1]))
     (token_weights,) = call(
         token_kernel, (((ranks, own_heads * marks, width), f32),), "token_softmax", us=0.8,
     )(*query, land_key)
@@ -1063,12 +1127,10 @@
         context_kernel, (full, marked, message, tall), "context", us=2.0,
     )(
         after(state, down_far), state_got, inverse, token_weights, values, value_before, value_after, flags,
-        taps_wide,
-    )
-
-    params = jnp.stack(
-        (output_bias, first_gain, first_shift, down_bias, second_gain, second_shift)
-    ).astype(f32)
+        *smalls,
+    )
+
+    params = (output_bias, first_gain, first_shift, down_bias, second_gain, second_shift)
     (
         layer_out,
         back_input,
@@ -1081,130 +1143,115 @@
         norm_sums,
         up_sums,
     ) = feed_layer(
-        flat, context, output_blocks, up_blocks, down_blocks, up_bias_all[None, :], params, upstream
+        flat, context, output_blocks, up_blocks, down_blocks, smalls, params, upstream
     )
 
     layer_far = swap(layer_out, "tp", 2)
-    units_of = functools.partial(group_of, channels=hidden_units)
     positions = lax.axis_size("seq")
-    sizes = [1 << level for level in range(positions.bit_length() - 1)]
-    down = [outer(back_feed, units_of(active, r)).astype(bf16) for r in range(ranks)]
+    levels = list(range(positions.bit_length() - 1))
+    bits = jnp.stack([(device >> level) & 1 for level in levels]).astype(jnp.int32)
+    wide_tiles = (((2 * positions, model // positions, hidden_units), bf16),) * 2
+    weight_gradient = call(
+        weight_gradient_kernel, wide_tiles, "weight_gradient",
+        scratch=(pltpu.VMEM((model, width), bf16),), us=4.5,
+    )
+    up = Scatter("up", *weight_gradient(first_low, back_hidden), bits, levels + ["far"])
     part_back, sent_back, part_key, sent_key, query_direct, back_head, back_tail = call(
         token_back_kernel, (marked, message, marked, message, full32, edge, edge), "token_back",
         us=1.8,
-    )(after(back_context, *down), token_weights, mixed_low, *query, land_key)
-    down = scatter_start(down)
-    up = [outer(first_low, units_of(back_hidden, r)).astype(bf16) for r in range(ranks)]
+    )(after(back_context, up.send), token_weights, mixed_low, *query, land_key)
+    down = Scatter("down", *weight_gradient(back_feed, active), bits, ["far"] + levels)
     back_own, back_got = exchange(
-        plain_parts(), "back", flags, part_back, sent_back, (up[:2], up[2:] + down)
-    )
-    key_own, key_got = exchange(plain_parts(), "back_key", flags, part_key, sent_key)
+        plain_parts(), "back", flags, part_back, sent_back, ([down.send], ())
+    )
+    steps = []
+    key_own, key_got = exchange(plain_parts(), "back_key", flags, part_key, sent_key, marks_of=steps)
     back_before, back_after = neighbours(back_head, back_tail)
     conv_back, tap_rows = call(
         conv_back_kernel, (full32, ((heads, 2 * LANES), f32)), "conv_back", us=2.8
     )(
-        back_context, back_before, back_after, values, value_before, value_after, flags,
-        taps_flipped,
-    )
-    conv_part = tap_rows[:, STRIPE - 1 : STRIPE - 1 + TAPS]
-    up = scatter_start(up)
+        back_context, back_before, back_after, values, value_before, value_after, flags, *smalls
+    )
     back_inverse, back_mixed = call(seed_kernel, (squares, message), "seed")(
-        flags, after(back_own, conv_back, layer_far, *up), back_got, inverse, mixed
-    )
-    down = by_targets(scatter_far([down[0], after(down[1], layer_far)]), positions)
-    up = scatter_level(by_targets(up, positions), device, 1)
+        flags, after(back_own, conv_back, *up.hop(), *down.hop()), back_got, inverse, mixed
+    )
+    up.wait_for(back_before, back_after, steps[0])
+    down.wait_for(layer_far)
     part_query, sent_query, key_direct, back_values, value_bias_sums = call(
         key_back_kernel, (marked, message, full32, full, ((ranks, channels), f32)), "key_back",
         us=2.4,
     )(*keys, values, land_query, stats, mixed, back_mixed, conv_back)
-    newton_back = call(newton_back_kernel, (squares, squares), "newton_back", us=10.0)
+    newton_back = call(newton_back_kernel, (squares, squares), "newton_back", us=6.6)
     back_middle = newton_back(kernel, saved_last, back_inverse, jnp.zeros(*squares))
-    pairs = (((model, 2 * channels), bf16),) * ranks
-    value_output = call(value_output_kernel, pairs, "value_output", us=2.0)(
+    tiles = (((2 * positions, model // positions, 2 * channels), bf16),) * 2
+    value_output = call(value_output_kernel, tiles, "value_output", us=2.0)(
         flat, back_values, back_attention, context
     )
+    value_output = Scatter("value_output", *value_output, bits, ["far"] + levels)
+    steps = []
     query_own, query_got = exchange(
         plain_parts(), "back_query", flags, part_query, sent_query,
-        (list(back_middle), list(value_output)),
+        (list(back_middle), [value_output.send]), steps,
     )
     back_start, back_kernel = newton_back(kernel, saved_first, *back_middle)
     query_more, key_more = call(land_back_kernel, (marked, marked), "land_back")(
         kernel, back_start, back_kernel, land_query, land_key
     )
-    value_output = scatter_start(value_output)
-    grad_row, query_bias_sums, *projection = call(
+    bundle_rows = 4 * ranks + norm_sums.shape[0]
+    (bundle,) = call(
+        bundle_kernel, (((bundle_rows + -bundle_rows % 8, model), f32),), "bundle", scalars=1
+    )(rank.reshape(1).astype(jnp.int32), up_sums, value_bias_sums, tap_rows, norm_sums)
+    rows_here = model // positions
+    bias_rows = rows_here + -rows_here % 16
+    taller = (((2 * positions, bias_rows + 16, 2 * channels), bf16),) * 2
+    grad_row, *projection = call(
         input_back_kernel,
-        (((width, model), bf16), ((ranks, channels), f32)) + pairs,
+        (((width, model), bf16),) + taller,
         "input_back",
-        scratch=(pltpu.VMEM((model, width), bf16),),
-        us=7.0,
-        limit=32 << 20,
+        scratch=(
+            pltpu.VMEM((model, width), bf16),
+            pltpu.VMEM((width, 2 * model), bf16),
+            pltpu.VMEM((2 * model, model), bf16),
+        ),
+        us=5.0,
+        limit=24 << 20,
     )(
         flags, count, flat, query_direct, key_direct, back_values,
-        after(query_own, *down, *up, *value_output), query_got, query_more, key_own, key_got,
-        key_more, member, back_input, *query_blocks, *key_blocks, *value_blocks,
-    )
-    for size in sizes[1:]:
-        up = scatter_level(up, device, size)
-    for size in sizes:
-        down = scatter_level(down, device, size, size == sizes[-1])
-    grad_up_weight = scatter_far(up)[0][0].astype(f32)
-    grad_down_weight = down[0][0]
-    grad_up_bias = [units_of(up_sums, r)[0] for r in range(ranks)]
-    value_output = by_targets(scatter_far(value_output), positions)
-    for size in sizes:
-        value_output = scatter_level(value_output, device, size, size == sizes[-1])
-    grad_output_weight = value_output[0][0][:, :channels].T
-    grad_value_weight = value_output[0][0][:, channels:]
-    projection = by_targets(scatter_start(projection), positions)
-    for size in sizes:
-        projection = scatter_level(projection, device, size)
-    projection = scatter_far(projection)[0][0].astype(f32)
+        after(query_own, *up.hop(), *value_output.hop()), query_got, query_more,
+        key_own, key_got, key_more, member, back_input, *query_blocks, *key_blocks, *value_blocks,
+    )
+    projection = Scatter("projection", *projection, bits, levels + ["far"])
     grad_far = swap(grad_row, "tp", 2)
+    up.wait_for(steps[1])
+    layer_blocks = shards(layer_out, layer_far)
+    down.hop(value_output)
+    for scatter in (projection, down, up):
+        while scatter.hops:
+            scatter.hop()
+        scatter.hop()
+    grad_up_weight = up.keep[0]
+    grad_down_weight = down.keep[0][:, :hidden_units]
+    grad_output_weight = down.keep[0][:, hidden_units : hidden_units + channels].T
+    grad_value_weight = down.keep[0][:, hidden_units + channels :]
+    projection = projection.keep[0]
     grad_tokens = place_rows(rank, shards(grad_row, grad_far), f32)
-    layer_rows = place_rows(rank, shards(layer_out, layer_far), bf16)
-
-    ranked = jnp.stack(
-        [
-            jnp.concatenate(
-                (
-                    grad_up_bias[r],
-                    value_bias_sums[r],
-                    query_bias_sums[r],
-                    conv_part[r * own_heads : (r + 1) * own_heads].reshape(-1),
-                )
-            )
-            for r in range(ranks)
-        ]
-    )
-    ranked = by_rank(ranked)
-    ranked_size = ranked.size
-    shared = [norm_sums[k] for k in range(6)]
-    bundle = jnp.concatenate([ranked.reshape(-1)] + shared)
-    bundle = jnp.pad(bundle, (0, -bundle.shape[0] % (8 * LANES))).reshape(-1, LANES)
-    bundle = sum_everywhere(bundle).reshape(-1)
-    own_ranked = lax.dynamic_index_in_dim(
-        bundle[:ranked_size].reshape(ranks, -1), rank, axis=0, keepdims=False
-    )
-    grad_up_bias = own_ranked[:hidden_units]
-    at = hidden_units
-    grad_value_bias = own_ranked[at : at + channels].reshape(own_heads, HEAD_DIM)
-    at += channels
-    share = HEAD_DIM // lax.axis_size("seq")
+    layer_rows = place_rows(rank, (after(layer_blocks[0], grad_row),) + layer_blocks[1:], bf16)
+    share = HEAD_DIM // positions
     grad_query_bias = lax.dynamic_slice_in_dim(
-        own_ranked[at : at + channels].reshape(own_heads, HEAD_DIM), device * share, share, axis=1
-    )
-    at += channels
-    grad_conv_weight = own_ranked[at : at + own_heads * TAPS].reshape(own_heads, TAPS)
-    shared = [
-        bundle[ranked_size + k * model : ranked_size + (k + 1) * model] for k in range(len(shared))
-    ]
+        projection[rows_here, :channels].reshape(own_heads, HEAD_DIM), device * share, share, axis=1
+    )
+    bundle = sum_everywhere(bundle)
+    own = lax.dynamic_slice_in_dim(bundle, 4 * rank, 4, axis=0)
+    grad_up_bias = own[0]
+    grad_value_bias = own[1, :channels].reshape(own_heads, HEAD_DIM)
+    grad_conv_weight = own[2].reshape(own_heads, 2 * LANES)[:, STRIPE - 1 : STRIPE - 1 + TAPS]
+    shared = [bundle[4 * ranks + k] for k in range(6)]
     return (
         layer_rows,
         grad_tokens,
-        projection[:, :channels],
+        projection[:rows_here, :channels],
         grad_query_bias,
-        projection[:, channels:],
+        projection[:rows_here, channels:],
         grad_value_weight,
         grad_value_bias,
         grad_conv_weight,

time: 426 us -> 375 us (0.88)
  local copies, waits for them, and re-layouts: 74.1 us -> 32.4 us
  other arithmetic: 21.9 us -> 1.12 us
  matrix products: 10.3 us -> 0 us
  waiting for transfers between devices: 138 us -> 148 us
  starting transfers between devices: 72 us -> 79 us
  Pallas kernels: 98 us -> 104 us
    pallas_call x31 -> x51, Pallas kernels: 54.9 us -> 81.7 us  [run(): pl.pallas_call(kernel, out_shape=outs, in_specs=[pl.BlockSpec(memory_spac...]
    pallas_call x1, Pallas kernels: 36.1 us -> 15.4 us  [feed_layer(): pl.pallas_call(feed_kernel, out_shape=(shape((width, model), bf16), shape...]
    convert_element_type x26 -> x0, other arithmetic: 17 us -> none  [the longest x14 6.02 us: scatter_level(): return total if last else [t.astype(bf16) for t in total]]
    slice x22 -> x5, local copies, waits for them, and re-layouts: 14.2 us -> 2.1 us  [the longest x1 0.74 us: per_device(): projection[:rows_here, channels:]]
    dot_general x8 -> x0, matrix products: 10.3 us -> none  [outer(): lax.dot_general(a, b, (((0,), (0,)), ((), ())), preferred_element_type=f32)]
    reshape x17 -> x0, local copies, waits for them, and re-layouts: 9 us -> none  [the longest x4 2.37 us: per_device(): conv_part[r * own_heads:(r + 1) * own_heads].reshape(-1)]
    unnamed x245 -> x189, local copies, waits for them, and re-layouts: 33.5 us -> 24.6 us
    ppermute x80 -> x67, waiting for transfers between devices: 135 us -> 142 us  [swap(): lax.ppermute(value, axis, [(i, i ^ step) for i in range(lax.axis_size(axi...]
  transfers between devices with their start and end apart: 84 -> 71, of which waited for: 36 -> 33; matrix products, arithmetic and copies ran while one was open for 16% -> 2% of each run, Pallas kernels for 14% -> 22%
where the time goes in v2:
time: 375 us; the launch traced here: 367 us
  waiting for transfers between devices  148 us (39%)
  Pallas kernels  104 us (28%)
  starting transfers between devices  79 us (21%)
  local copies, waits for them, and re-layouts  32.4 us (9%)
    ppermute x67, waiting for transfers between devices, swap(): lax.ppermute(value, axis, [(i, i ^ step) for i in range(lax.axis_size(axi...  142 us
    pallas_call x51, Pallas kernels, run(): pl.pallas_call(kernel, out_shape=outs, in_specs=[pl.BlockSpec(memory_spac...  81.7 us
    ppermute x67, starting transfers between devices, swap(): lax.ppermute(value, axis, [(i, i ^ step) for i in range(lax.axis_size(axi...  69 us
    unnamed x189, local copies, waits for them, and re-layouts  24.6 us
    pallas_call x1, Pallas kernels, feed_layer(): pl.pallas_call(feed_kernel, out_shape=(shape((width, model), bf16), shape...  15.4 us
  transfers between devices with their start and end apart: 71, of which 33 were waited for; matrix products, arithmetic and copies ran while one was open for 2% of the time, Pallas kernels for 22%

profile of v2, /device:TPU:0, one launch (start us, length us, event | category | flops | bytes accessed | tf_op | source)
XLA Modules:
  0.0 367.5 jit_solution(9577884371374831146)
XLA Ops:
  0.7 3.0 collective-permute-start.3
  11.9 5.8 %collective-permute-done.4.k0.k2 = bf16[192,768]{1,0:T(8,128)(2,1)} collective-permute-done((bf16[192,768]{1,0:T(8,128)(2,1)}, bf16[192,768]{1,0:T(8,128)(2,1)}, u32[]{:S(2)}, u32[]{:S(2)}) %collective-permute-start.4) | collective-permute-done | bytes 294944 | tf_op jit(solution)/shard_map/ppermute | solution.py:26
  21.4 2.6 query_key.2
  27.1 2.7 query_key.3
  31.4 3.4 collective-permute-done.16.got_ref
  37.0 3.0 collective-permute-done.13.got_ref
  46.0 4.7 %collective-permute-done.17.got_ref = bf16[128,768]{1,0:T(8,128)(2,1)S(1)} collective-permute-done((bf16[128,768]{1,0:T(8,128)(2,1)S(1)}, bf16[128,768]{1,0:T(8,128)(2,1)S(1)}, u32[]{:S(2)}, u32[]{:S(2)}) %collective-permute-start.17) | collective-permute-done | bytes 196640 | tf_op jit(solution)/shard_map/ppermute | solution.py:26
  50.7 2.6 collective-permute-start.15
  53.5 15.1 %collective-permute-done.9.out2 = bf16[192,768]{1,0:T(8,128)(2,1)S(1)} collective-permute-done((bf16[192,768]{1,0:T(8,128)(2,1)S(1)}, bf16[192,768]{1,0:T(8,128)(2,1)S(1)}, u32[]{:S(2)}, u32[]{:S(2)}) %collective-permute-start.9) | collective-permute-done | bytes 294944 | tf_op jit(solution)/shard_map/ppermute | solution.py:26
  68.6 2.6 collective-permute-start.18
  77.7 3.3 collective-permute-done.19.got_ref
  84.9 3.8 %collective-permute-done.20.got_ref = bf16[128,896]{1,0:T(8,128)(2,1)S(1)} collective-permute-done((bf16[128,896]{1,0:T(8,128)(2,1)S(1)}, bf16[128,896]{1,0:T(8,128)(2,1)S(1)}, u32[]{:S(2)}, u32[]{:S(2)}) %collective-permute-start.20) | collective-permute-done | bytes 229408 | tf_op jit(solution)/shard_map/ppermute | solution.py:26
  89.9 16.4 %collective-permute-done.22.down2 = bf16[768,768]{1,0:T(8,128)(2,1)S(1)} collective-permute-done((bf16[768,768]{1,0:T(8,128)(2,1)S(1)}, bf16[768,768]{1,0:T(8,128)(2,1)S(1)}, u32[]{:S(2)}, u32[]{:S(2)}) %collective-permute-start.22) | collective-permute-done | bytes 1179680 | tf_op jit(solution)/shard_map/ppermute | solution.py:26
  106.9 2.8 collective-permute-done.26.out1
  109.6 3.2 collective-permute-start.24
  115.8 4.5 %collective-permute-done.25.after_ref.vafter_ref = bf16[16,768]{1,0:T(8,128)(2,1)S(1)} collective-permute-done((bf16[16,768]{1,0:T(8,128)(2,1)S(1)}, bf16[16,768]{1,0:T(8,128)(2,1)S(1)}, u32[]{:S(2)}, u32[]{:S(2)}) %collective-permute-start.25) | collective-permute-done | bytes 24608 | tf_op jit(solution)/shard_map/ppermute | solution.py:1105
  120.3 4.1 %collective-permute-start.23 = (bf16[64,896]{1,0:T(8,128)(2,1)S(1)}, bf16[64,896]{1,0:T(8,128)(2,1)S(1)}, u32[]{:S(2)}, u32[]{:S(2)}) collective-permute-start(bf16[64,896]{1,0:T(8,128)(2,1)S(1)} %get-tuple-element.184), channel_id=1, source_target_pairs={{0,16},{4,20},{8,24},{12,28},{16,0},{20,4},{24,8},{28,12},{1,17},{... | collective-permute-start | bytes 344072 | tf_op jit(solution)/shard_map/ppermute | solution.py:26
  124.5 3.0 collective-permute-done.23.got_ref
  128.6 2.5 newton_first.1
  132.6 2.3 newton_next.1
  139.9 15.4 %feed_layer.1 = (bf16[512,768]{1,0:T(8,128)(2,1)S(1)}, f32[512,768]{1,0:T(8,128)S(1)}, bf16[512,768]{1,0:T(8,128)(2,1)S(1)}, bf16[4,512,192]{2,1,0:T(8,128)(2,1)...) custom-call(bf16[512,768]{1,0:T(8,128)(2,1)S(1)} %copy-done.3, ...), custom_call_target="tpu_custom_call" | custom-call | bytes 62700000 | tf_op jit(solution)/shard_map/feed_layer/pallas_call | solution.py:975
  155.4 4.0 %weight_gradient.2 = (bf16[16,96,768]{2,1,0:T(8,128)(2,1)S(1)}, bf16[16,96,768]{2,1,0:T(8,128)(2,1)}) custom-call(bf16[512,768]{1,0:T(8,128)(2,1)S(1)} %get-tuple-element.197.side_ref, bf16[512,3072]{1,0:T(8,128)(2,1)S(1)} %get-tuple-element.198.units_ref), custom_call_target="tpu_custom_call" | custom-call | bytes 14850000 | tf_op jit(solution)/shard_map/weight_gradient/pallas_call | solution.py:163
  161.4 4.1 %weight_gradient.3 = (bf16[16,96,768]{2,1,0:T(8,128)(2,1)S(1)}, bf16[16,96,768]{2,1,0:T(8,128)(2,1)}) custom-call(bf16[512,768]{1,0:T(8,128)(2,1)S(1)} %get-tuple-element.206.side_ref, bf16[512,3072]{1,0:T(8,128)(2,1)S(1)} %get-tuple-element.207.units_ref), custom_call_target="tpu_custom_call" | custom-call | bytes 14850000 | tf_op jit(solution)/shard_map/weight_gradient/pallas_call | solution.py:163
  166.9 2.5 token_back.1
  173.1 3.6 collective-permute-done.32.got_ref
  180.3 3.9 %collective-permute-start.34 = (bf16[16,768]{1,0:T(8,128)(2,1)}, bf16[16,768]{1,0:T(8,128)(2,1)}, u32[]{:S(2)}, u32[]{:S(2)}) collective-permute-start(bf16[16,768]{1,0:T(8,128)(2,1)} %get-tuple-element.214), channel_id=1, source_target_pairs={{0,4},{4,8},{8,12},{12,16},{16,20},{20,24},{24,28},{1,5},{5,9},{9,... | collective-permute-start | bytes 73736 | tf_op jit(solution)/shard_map/ppermute | solution.py:1104
  189.0 5.0 %collective-permute-start.38 = (bf16[64,768]{1,0:T(8,128)(2,1)S(1)}, bf16[64,768]{1,0:T(8,128)(2,1)S(1)}, u32[]{:S(2)}, u32[]{:S(2)}) collective-permute-start(bf16[64,768]{1,0:T(8,128)(2,1)S(1)} %get-tuple-element.224), channel_id=1, source_target_pairs={{0,16},{4,20},{8,24},{12,28},{16,0},{20,4},{24,8},{28,12},{1,17},{... | collective-permute-start | bytes 294920 | tf_op jit(solution)/shard_map/ppermute | solution.py:26
  197.0 3.6 conv_back.1
  200.8 2.4 up_route.5
  204.2 2.3 down_route.5
  207.2 2.3 key_back.1
  214.8 6.9 %newton_back.2 = (f32[6,64,128]{2,1,0:T(8,128)S(1)}, f32[6,64,128]{2,1,0:T(8,128)S(1)}) custom-call(f32[6,64,128]{2,1,0:T(8,128)S(1)} %get-tuple-element.185.kernel_ref, f32[3,4,6,64,128]{4,3,2,1,0:T(8,128)S(1)} %copy-done.9, f32[6,64,128]{2,1,0:T(8,128)S(1)} %get-tuple-element.230.inverse_in, f32[6,64,128]{2,1,0:T(8,128)S(1)} %broadcast_in_dim.3.kernel_in), custom_call_target="tpu_custom_call" | custom-call | bytes 21780000 | tf_op jit(solution)/shard_map/newton_back/pallas_call | solution.py:163
  221.6 9.6 %collective-permute-done.39.got_ref = bf16[64,768]{1,0:T(8,128)(2,1)S(1)} collective-permute-done((bf16[64,768]{1,0:T(8,128)(2,1)S(1)}, bf16[64,768]{1,0:T(8,128)(2,1)S(1)}, u32[]{:S(2)}, u32[]{:S(2)}) %collective-permute-start.39) | collective-permute-done | bytes 98336 | tf_op jit(solution)/shard_map/ppermute | solution.py:26
  234.4 4.2 %collective-permute-done.40.got_ref = bf16[128,768]{1,0:T(8,128)(2,1)S(1)} collective-permute-done((bf16[128,768]{1,0:T(8,128)(2,1)S(1)}, bf16[128,768]{1,0:T(8,128)(2,1)S(1)}, u32[]{:S(2)}, u32[]{:S(2)}) %collective-permute-start.40) | collective-permute-done | bytes 196640 | tf_op jit(solution)/shard_map/ppermute | solution.py:26
  238.9 6.6 %newton_back.3 = (f32[6,64,128]{2,1,0:T(8,128)S(1)}, f32[6,64,128]{2,1,0:T(8,128)S(1)}) custom-call(f32[6,64,128]{2,1,0:T(8,128)S(1)} %get-tuple-element.185.kernel_ref, f32[3,4,6,64,128]{4,3,2,1,0:T(8,128)S(1)} %copy-done.7, f32[6,64,128]{2,1,0:T(8,128)S(1)} %get-tuple-element.231.inverse_in, f32[6,64,128]{2,1,0:T(8,128)S(1)} %get-tuple-element.232.kernel_in), custom_call_target="tpu_custom_call" | custom-call | bytes 21780000 | tf_op jit(solution)/shard_map/newton_back/pallas_call | solution.py:163
  249.4 8.0 %input_back.1 = (bf16[512,768]{1,0:T(8,128)(2,1)}, bf16[16,112,384]{2,1,0:T(8,128)(2,1)S(1)}, bf16[16,112,384]{2,1,0:T(8,128)(2,1)S(1)}) custom-call(f32[16,128]{1,0:T(8,128)S(1)} %get-tuple-element.154.flags_ref, f32[64,128]{1,0:T(8,128)S(1)} %copy-done.71, bf16[512,768]{1,0:T(8,128)(2,1)S(1)} %copy-done.3, f32[4,512,192]{2,1,0:T(8,128)S(1)} %copy-done.19, ...), custom_call_target="tpu_custom_call" | custom-call | bytes 16500000 | tf_op jit(solution)/shard_map/input_back/pallas_call | solution.py:163
  259.0 14.2 %collective-permute-done.59.refs_3_ = bf16[8,96,384]{2,1,0:T(8,128)(2,1)S(1)} collective-permute-done((bf16[8,96,384]{2,1,0:T(8,128)(2,1)S(1)}, bf16[8,96,384]{2,1,0:T(8,128)(2,1)S(1)}, u32[]{:S(2)}, u32[]{:S(2)}) %collective-permute-start.59) | collective-permute-done | bytes 589856 | tf_op jit(solution)/shard_map/ppermute | solution.py:26
  282.4 13.2 %collective-permute-done.51.r2 = bf16[512,768]{1,0:T(8,128)(2,1)} collective-permute-done((bf16[512,768]{1,0:T(8,128)(2,1)}, bf16[512,768]{1,0:T(8,128)(2,1)}, u32[]{:S(2)}, u32[]{:S(2)}) %collective-permute-start.51) | collective-permute-done | bytes 786464 | tf_op jit(solution)/shard_map/ppermute | solution.py:26
  298.0 3.3 collective-permute-done.64
  301.3 2.3 collective-permute-start.61
  305.1 7.2 %collective-permute-done.65 = f32[24,768]{1,0:T(8,128)S(1)} collective-permute-done((f32[24,768]{1,0:T(8,128)S(1)}, f32[24,768]{1,0:T(8,128)S(1)}, u32[]{:S(2)}, u32[]{:S(2)}) %collective-permute-start.65) | collective-permute-done | bytes 73760 | tf_op jit(solution)/shard_map/ppermute | solution.py:26
  312.3 2.7 collective-permute-start.69
  318.2 3.7 collective-permute-done.66
  321.9 2.5 collective-permute-start.55
  330.6 3.3 collective-permute-done.67
  342.4 5.0 %place_rows.3 = f32[4,512,768]{2,1,0:T(8,128)} custom-call(s32[1]{0:T(128)} %bitcast.rank_ref, bf16[512,768]{1,0:T(8,128)(2,1)} %get-tuple-element.262.r0, bf16[512,768]{1,0:T(8,128)(2,1)} %collective-permute-done.50.r1, bf16[512,768]{1,0:T(8,128)(2,1)} %collective-permute-done.51.r2, bf16[512,768]{1,0:T(8,128)(2,1)} %collective-permute-done.52.r3), custom_call_target="tpu_custom_call" | custom-call | bytes 8250000 | tf_op jit(solution)/shard_map/place_rows/pallas_call | solution.py:882
  351.0 3.6 collective-permute-start.56
  355.3 4.5 %collective-permute-done.56.refs_1_ = bf16[2,112,384]{2,1,0:T(8,128)(2,1)S(1)} collective-permute-done((bf16[2,112,384]{2,1,0:T(8,128)(2,1)S(1)}, bf16[2,112,384]{2,1,0:T(8,128)(2,1)S(1)}, u32[]{:S(2)}, u32[]{:S(2)}) %collective-permute-start.56) | collective-permute-done | bytes 172064 | tf_op jit(solution)/shard_map/ppermute | solution.py:26
  (359 shorter events, 123.7 us)
Async XLA Ops:
  0.7 11.2 %collective-permute-start.3 = (bf16[192,768]{1,0:T(8,128)(2,1)}, bf16[192,768]{1,0:T(8,128)(2,1)}, u32[]{:S(2)}, u32[]{:S(2)}) collective-permute-start(bf16[192,768]{1,0:T(8,128)(2,1)} %bitcast.22), channel_id=1, source_target_pairs={{0,2},{1,3},{2,0},{3,1},{4,6},{5,7},{6,4},{7,5},{8,10},{9,11},{10,... | collective-permute-start | bytes 884744 | tf_op jit(solution)/shard_map/ppermute | solution.py:26
  3.7 13.9 %collective-permute-start.4 = (bf16[192,768]{1,0:T(8,128)(2,1)}, bf16[192,768]{1,0:T(8,128)(2,1)}, u32[]{:S(2)}, u32[]{:S(2)}) collective-permute-start(bf16[192,768]{1,0:T(8,128)(2,1)} %bitcast.26), channel_id=1, source_target_pairs={{0,2},{1,3},{2,0},{3,1},{4,6},{5,7},{6,4},{7,5},{8,10},{9,11},{10,... | collective-permute-start | bytes 884744 | tf_op jit(solution)/shard_map/ppermute | solution.py:26
  3.8 15.5 %collective-permute-start = (bf16[192,768]{1,0:T(8,128)(2,1)}, bf16[192,768]{1,0:T(8,128)(2,1)}, u32[]{:S(2)}, u32[]{:S(2)}) collective-permute-start(bf16[192,768]{1,0:T(8,128)(2,1)} %bitcast.23), channel_id=1, source_target_pairs={{0,1},{1,0},{2,3},{3,2},{4,5},{5,4},{6,7},{7,6},{8,9},{9,8},{10,11... | collective-permute-start | bytes 884744 | tf_op jit(solution)/shard_map/ppermute | solution.py:26
  3.8 15.5 %collective-permute-start.1 = (bf16[192,768]{1,0:T(8,128)(2,1)}, bf16[192,768]{1,0:T(8,128)(2,1)}, u32[]{:S(2)}, u32[]{:S(2)}) collective-permute-start(bf16[192,768]{1,0:T(8,128)(2,1)} %bitcast.27), channel_id=1, source_target_pairs={{0,1},{1,0},{2,3},{3,2},{4,5},{5,4},{6,7},{7,6},{8,9},{9,8},{10,11... | collective-permute-start | bytes 884744 | tf_op jit(solution)/shard_map/ppermute | solution.py:26
  9.1 14.9 %collective-permute-start.7 = (bf16[16,768]{1,0:T(8,128)(2,1)S(1)}, bf16[16,768]{1,0:T(8,128)(2,1)S(1)}, u32[]{:S(2)}, u32[]{:S(2)}) collective-permute-start(bf16[16,768]{1,0:T(8,128)(2,1)S(1)} %small.1.s0), channel_id=1, source_target_pairs={{0,2},{1,3},{2,0},{3,1},{4,6},{5,7},{6,4},{7,5},{8,10},{9,11},{10,... | collective-permute-start | bytes 73736 | tf_op jit(solution)/shard_map/ppermute | solution.py:26
  11.9 15.2 %collective-permute-start.5 = (bf16[192,768]{1,0:T(8,128)(2,1)}, bf16[192,768]{1,0:T(8,128)(2,1)S(1)}, u32[]{:S(2)}, u32[]{:S(2)}) collective-permute-start(bf16[192,768]{1,0:T(8,128)(2,1)} %collective-permute-done.3.q0.q2), channel_id=1, source_target_pairs={{0,1},{1,0},{2,3},{3,2},{4,5},{5,4},{6,7},{7,6},{8,9},{9,8},{10,11... | collective-permute-start | bytes 884744 | tf_op jit(solution)/shard_map/ppermute | solution.py:26
  17.6 9.4 %collective-permute-start.6 = (bf16[192,768]{1,0:T(8,128)(2,1)}, bf16[192,768]{1,0:T(8,128)(2,1)S(1)}, u32[]{:S(2)}, u32[]{:S(2)}) collective-permute-start(bf16[192,768]{1,0:T(8,128)(2,1)} %collective-permute-done.4.k0.k2), channel_id=1, source_target_pairs={{0,1},{1,0},{2,3},{3,2},{4,5},{5,4},{6,7},{7,6},{8,9},{9,8},{10,11... | collective-permute-start | bytes 884744 | tf_op jit(solution)/shard_map/ppermute | solution.py:26
  24.1 10.8 %collective-permute-start.11 = (bf16[192,768]{1,0:T(8,128)(2,1)S(1)}, bf16[192,768]{1,0:T(8,128)(2,1)S(1)}, u32[]{:S(2)}, u32[]{:S(2)}) collective-permute-start(bf16[192,768]{1,0:T(8,128)(2,1)S(1)} %bitcast.30), channel_id=1, source_target_pairs={{0,2},{1,3},{2,0},{3,1},{4,6},{5,7},{6,4},{7,5},{8,10},{9,11},{10,... | collective-permute-start | bytes 884744 | tf_op jit(solution)/shard_map/ppermute | solution.py:26
  34.9 47.1 %collective-permute-start.21 = (bf16[768,768]{1,0:T(8,128)(2,1)S(1)}, bf16[768,768]{1,0:T(8,128)(2,1)S(1)}, u32[]{:S(2)}, u32[]{:S(2)}) collective-permute-start(bf16[768,768]{1,0:T(8,128)(2,1)S(1)} %copy-done.22), channel_id=1, source_target_pairs={{0,2},{1,3},{2,0},{3,1},{4,6},{5,7},{6,4},{7,5},{8,10},{9,11},{10,... | collective-permute-start | bytes 3538952 | tf_op jit(solution)/shard_map/ppermute | solution.py:26
  41.9 26.7 %collective-permute-start.9 = (bf16[192,768]{1,0:T(8,128)(2,1)S(1)}, bf16[192,768]{1,0:T(8,128)(2,1)S(1)}, u32[]{:S(2)}, u32[]{:S(2)}) collective-permute-start(bf16[192,768]{1,0:T(8,128)(2,1)S(1)} %copy-done.59), channel_id=1, source_target_pairs={{0,2},{1,3},{2,0},{3,1},{4,6},{5,7},{6,4},{7,5},{8,10},{9,11},{10,... | collective-permute-start | bytes 884744 | tf_op jit(solution)/shard_map/ppermute | solution.py:26
  43.4 27.8 %collective-permute-start.10 = (bf16[192,768]{1,0:T(8,128)(2,1)S(1)}, bf16[192,768]{1,0:T(8,128)(2,1)S(1)}, u32[]{:S(2)}, u32[]{:S(2)}) collective-permute-start(bf16[192,768]{1,0:T(8,128)(2,1)S(1)} %bitcast.31), channel_id=1, source_target_pairs={{0,1},{1,0},{2,3},{3,2},{4,5},{5,4},{6,7},{7,6},{8,9},{9,8},{10,11... | collective-permute-start | bytes 884744 | tf_op jit(solution)/shard_map/ppermute | solution.py:26
  45.8 25.4 %collective-permute-start.12 = (bf16[192,768]{1,0:T(8,128)(2,1)S(1)}, bf16[192,768]{1,0:T(8,128)(2,1)S(1)}, u32[]{:S(2)}, u32[]{:S(2)}) collective-permute-start(bf16[192,768]{1,0:T(8,128)(2,1)S(1)} %collective-permute-done.11.w2.v2), channel_id=1, source_target_pairs={{0,1},{1,0},{2,3},{3,2},{4,5},{5,4},{6,7},{7,6},{8,9},{9,8},{10,11... | collective-permute-start | bytes 884744 | tf_op jit(solution)/shard_map/ppermute | solution.py:26
  50.7 21.6 %collective-permute-start.15 = (bf16[64,768]{1,0:T(8,128)(2,1)S(1)}, bf16[64,768]{1,0:T(8,128)(2,1)S(1)}, u32[]{:S(2)}, u32[]{:S(2)}) collective-permute-start(bf16[64,768]{1,0:T(8,128)(2,1)S(1)} %get-tuple-element.168), channel_id=1, source_target_pairs={{0,16},{4,20},{8,24},{12,28},{16,0},{20,4},{24,8},{28,12},{1,17},{... | collective-permute-start | bytes 294920 | tf_op jit(solution)/shard_map/ppermute | solution.py:26
  82.1 24.3 %collective-permute-start.22 = (bf16[768,768]{1,0:T(8,128)(2,1)S(1)}, bf16[768,768]{1,0:T(8,128)(2,1)S(1)}, u32[]{:S(2)}, u32[]{:S(2)}) collective-permute-start(bf16[768,768]{1,0:T(8,128)(2,1)S(1)} %copy-done.23), channel_id=1, source_target_pairs={{0,2},{1,3},{2,0},{3,1},{4,6},{5,7},{6,4},{7,5},{8,10},{9,11},{10,... | collective-permute-start | bytes 3538952 | tf_op jit(solution)/shard_map/ppermute | solution.py:26
  84.4 55.4 %collective-permute-start.28 = (bf16[768,768]{1,0:T(8,128)(2,1)S(1)}, bf16[768,768]{1,0:T(8,128)(2,1)S(1)}, u32[]{:S(2)}, u32[]{:S(2)}) collective-permute-start(bf16[768,768]{1,0:T(8,128)(2,1)S(1)} %copy-done.22), channel_id=1, source_target_pairs={{0,1},{1,0},{2,3},{3,2},{4,5},{5,4},{6,7},{7,6},{8,9},{9,8},{10,11... | collective-permute-start | bytes 3538952 | tf_op jit(solution)/shard_map/ppermute | solution.py:26
  84.4 55.4 %collective-permute-start.30 = (bf16[768,768]{1,0:T(8,128)(2,1)S(1)}, bf16[768,768]{1,0:T(8,128)(2,1)S(1)}, u32[]{:S(2)}, u32[]{:S(2)}) collective-permute-start(bf16[768,768]{1,0:T(8,128)(2,1)S(1)} %copy-done.23), channel_id=1, source_target_pairs={{0,1},{1,0},{2,3},{3,2},{4,5},{5,4},{6,7},{7,6},{8,9},{9,8},{10,11... | collective-permute-start | bytes 3538952 | tf_op jit(solution)/shard_map/ppermute | solution.py:26
  89.8 50.0 %collective-permute-start.29 = (bf16[768,768]{1,0:T(8,128)(2,1)S(1)}, bf16[768,768]{1,0:T(8,128)(2,1)S(1)}, u32[]{:S(2)}, u32[]{:S(2)}) collective-permute-start(bf16[768,768]{1,0:T(8,128)(2,1)S(1)} %collective-permute-done.21.up2), channel_id=1, source_target_pairs={{0,1},{1,0},{2,3},{3,2},{4,5},{5,4},{6,7},{7,6},{8,9},{9,8},{10,11... | collective-permute-start | bytes 3538952 | tf_op jit(solution)/shard_map/ppermute | solution.py:26
  106.4 33.5 %collective-permute-start.31 = (bf16[768,768]{1,0:T(8,128)(2,1)S(1)}, bf16[768,768]{1,0:T(8,128)(2,1)S(1)}, u32[]{:S(2)}, u32[]{:S(2)}) collective-permute-start(bf16[768,768]{1,0:T(8,128)(2,1)S(1)} %collective-permute-done.22.down2), channel_id=1, source_target_pairs={{0,1},{1,0},{2,3},{3,2},{4,5},{5,4},{6,7},{7,6},{8,9},{9,8},{10,11... | collective-permute-start | bytes 3538952 | tf_op jit(solution)/shard_map/ppermute | solution.py:26
  127.5 12.3 %collective-permute-start.27 = (bf16[192,768]{1,0:T(8,128)(2,1)S(1)}, bf16[192,768]{1,0:T(8,128)(2,1)S(1)}, u32[]{:S(2)}, u32[]{:S(2)}) collective-permute-start(bf16[192,768]{1,0:T(8,128)(2,1)S(1)} %collective-permute-done.9.out2), channel_id=1, source_target_pairs={{0,1},{1,0},{2,3},{3,2},{4,5},{5,4},{6,7},{7,6},{8,9},{9,8},{10,11... | collective-permute-start | bytes 884744 | tf_op jit(solution)/shard_map/ppermute | solution.py:26
  160.9 39.8 %collective-permute-start.36 = (bf16[16,96,768]{2,1,0:T(8,128)(2,1)}, bf16[16,96,768]{2,1,0:T(8,128)(2,1)}, u32[]{:S(2)}, u32[]{:S(2)}) collective-permute-start(bf16[16,96,768]{2,1,0:T(8,128)(2,1)} %get-tuple-element.199), channel_id=1, source_target_pairs={{0,1},{1,0},{2,3},{3,2},{4,5},{5,4},{6,7},{7,6},{8,9},{9,8},{10,11... | collective-permute-start | bytes 7077896 | tf_op jit(solution)/shard_map/ppermute | solution.py:26
  166.9 37.2 %collective-permute-start.37 = (bf16[16,96,768]{2,1,0:T(8,128)(2,1)}, bf16[16,96,768]{2,1,0:T(8,128)(2,1)}, u32[]{:S(2)}, u32[]{:S(2)}) collective-permute-start(bf16[16,96,768]{2,1,0:T(8,128)(2,1)} %get-tuple-element.208), channel_id=1, source_target_pairs={{0,1},{1,0},{2,3},{3,2},{4,5},{5,4},{6,7},{7,6},{8,9},{9,8},{10,11... | collective-permute-start | bytes 7077896 | tf_op jit(solution)/shard_map/ppermute | solution.py:26
  184.2 16.4 %collective-permute-start.41 = (bf16[64,768]{1,0:T(8,128)(2,1)}, bf16[64,768]{1,0:T(8,128)(2,1)S(1)}, u32[]{:S(2)}, u32[]{:S(2)}) collective-permute-start(bf16[64,768]{1,0:T(8,128)(2,1)} %copy-done.91), channel_id=1, source_target_pairs={{0,4},{4,0},{8,12},{12,8},{16,20},{20,16},{24,28},{28,24},{1,5},{5... | collective-permute-start | bytes 294920 | tf_op jit(solution)/shard_map/ppermute | solution.py:26
  189.0 17.5 %collective-permute-start.38 = (bf16[64,768]{1,0:T(8,128)(2,1)S(1)}, bf16[64,768]{1,0:T(8,128)(2,1)S(1)}, u32[]{:S(2)}, u32[]{:S(2)}) collective-permute-start(bf16[64,768]{1,0:T(8,128)(2,1)S(1)} %get-tuple-element.224), channel_id=1, source_target_pairs={{0,16},{4,20},{8,24},{12,28},{16,0},{20,4},{24,8},{28,12},{1,17},{... | collective-permute-start | bytes 294920 | tf_op jit(solution)/shard_map/ppermute | solution.py:26
  203.1 43.6 %collective-permute-start.42 = (bf16[8,96,768]{2,1,0:T(8,128)(2,1)S(1)}, bf16[8,96,768]{2,1,0:T(8,128)(2,1)S(1)}, u32[]{:S(2)}, u32[]{:S(2)}) collective-permute-start(bf16[8,96,768]{2,1,0:T(8,128)(2,1)S(1)} %get-tuple-element.244), channel_id=1, source_target_pairs={{0,4},{4,0},{8,12},{12,8},{16,20},{20,16},{24,28},{28,24},{1,5},{5... | collective-permute-start | bytes 3538952 | tf_op jit(solution)/shard_map/ppermute | solution.py:26
  211.4 36.2 %collective-permute-start.43 = (bf16[16,96,384]{2,1,0:T(8,128)(2,1)S(1)}, bf16[16,96,384]{2,1,0:T(8,128)(2,1)S(1)}, u32[]{:S(2)}, u32[]{:S(2)}) collective-permute-start(bf16[16,96,384]{2,1,0:T(8,128)(2,1)S(1)} %get-tuple-element.237), channel_id=1, source_target_pairs={{0,1},{1,0},{2,3},{3,2},{4,5},{5,4},{6,7},{7,6},{8,9},{9,8},{10,11... | collective-permute-start | bytes 3538952 | tf_op jit(solution)/shard_map/ppermute | solution.py:26
  211.5 21.4 %collective-permute-start.48 = (bf16[512,768]{1,0:T(8,128)(2,1)S(1)}, bf16[512,768]{1,0:T(8,128)(2,1)S(1)}, u32[]{:S(2)}, u32[]{:S(2)}) collective-permute-start(bf16[512,768]{1,0:T(8,128)(2,1)S(1)} %copy-done.46), channel_id=1, source_target_pairs={{0,2},{1,3},{2,0},{3,1},{4,6},{5,7},{6,4},{7,5},{8,10},{9,11},{10,... | collective-permute-start | bytes 2359304 | tf_op jit(solution)/shard_map/ppermute | solution.py:26
  212.3 18.9 %collective-permute-start.39 = (bf16[64,768]{1,0:T(8,128)(2,1)S(1)}, bf16[64,768]{1,0:T(8,128)(2,1)S(1)}, u32[]{:S(2)}, u32[]{:S(2)}) collective-permute-start(bf16[64,768]{1,0:T(8,128)(2,1)S(1)} %get-tuple-element.234), channel_id=1, source_target_pairs={{0,4},{4,0},{8,12},{12,8},{16,20},{20,16},{24,28},{28,24},{1,5},{5... | collective-permute-start | bytes 294920 | tf_op jit(solution)/shard_map/ppermute | solution.py:26
  213.4 20.2 %collective-permute-start.45 = (bf16[128,768]{1,0:T(8,128)(2,1)S(1)}, bf16[128,768]{1,0:T(8,128)(2,1)S(1)}, u32[]{:S(2)}, u32[]{:S(2)}) collective-permute-start(bf16[128,768]{1,0:T(8,128)(2,1)S(1)} %get-tuple-element.256.sent_ref), channel_id=1, source_target_pairs={{0,8},{4,12},{8,0},{12,4},{16,24},{20,28},{24,16},{28,20},{1,9},{5... | collective-permute-start | bytes 589832 | tf_op jit(solution)/shard_map/ppermute | solution.py:26
  233.0 26.0 %collective-permute-start.58 = (bf16[8,96,768]{2,1,0:T(8,128)(2,1)S(1)}, bf16[8,96,768]{2,1,0:T(8,128)(2,1)S(1)}, u32[]{:S(2)}, u32[]{:S(2)}) collective-permute-start(bf16[8,96,768]{2,1,0:T(8,128)(2,1)S(1)} %get-tuple-element.274), channel_id=1, source_target_pairs={{0,2},{1,3},{2,0},{3,1},{4,6},{5,7},{6,4},{7,5},{8,10},{9,11},{10,... | collective-permute-start | bytes 3538952 | tf_op jit(solution)/shard_map/ppermute | solution.py:26
  233.8 14.7 %collective-permute-start.46 = (bf16[64,768]{1,0:T(8,128)(2,1)S(1)}, bf16[64,768]{1,0:T(8,128)(2,1)S(1)}, u32[]{:S(2)}, u32[]{:S(2)}) collective-permute-start(bf16[64,768]{1,0:T(8,128)(2,1)S(1)} %get-tuple-element.258), channel_id=1, source_target_pairs={{0,16},{4,20},{8,24},{12,28},{16,0},{20,4},{24,8},{28,12},{1,17},{... | collective-permute-start | bytes 294920 | tf_op jit(solution)/shard_map/ppermute | solution.py:26
  238.8 9.7 %collective-permute-start.44 = (bf16[64,768]{1,0:T(8,128)(2,1)S(1)}, bf16[64,768]{1,0:T(8,128)(2,1)S(1)}, u32[]{:S(2)}, u32[]{:S(2)}) collective-permute-start(bf16[64,768]{1,0:T(8,128)(2,1)S(1)} %get-tuple-element.251), channel_id=1, source_target_pairs={{0,16},{4,20},{8,24},{12,28},{16,0},{20,4},{24,8},{28,12},{1,17},{... | collective-permute-start | bytes 294920 | tf_op jit(solution)/shard_map/ppermute | solution.py:26
  257.4 19.3 %collective-permute-start.53 = (bf16[16,112,384]{2,1,0:T(8,128)(2,1)S(1)}, bf16[16,112,384]{2,1,0:T(8,128)(2,1)S(1)}, u32[]{:S(2)}, u32[]{:S(2)}) collective-permute-start(bf16[16,112,384]{2,1,0:T(8,128)(2,1)S(1)} %get-tuple-element.265), channel_id=1, source_target_pairs={{0,1},{1,0},{2,3},{3,2},{4,5},{5,4},{6,7},{7,6},{8,9},{9,8},{10,11... | collective-permute-start | bytes 4128776 | tf_op jit(solution)/shard_map/ppermute | solution.py:26
  257.4 15.7 %collective-permute-start.59 = (bf16[8,96,384]{2,1,0:T(8,128)(2,1)S(1)}, bf16[8,96,384]{2,1,0:T(8,128)(2,1)S(1)}, u32[]{:S(2)}, u32[]{:S(2)}) collective-permute-start(bf16[8,96,384]{2,1,0:T(8,128)(2,1)S(1)} %get-tuple-element.249), channel_id=1, source_target_pairs={{0,2},{1,3},{2,0},{3,1},{4,6},{5,7},{6,4},{7,5},{8,10},{9,11},{10,... | collective-permute-start | bytes 1769480 | tf_op jit(solution)/shard_map/ppermute | solution.py:26
  257.7 20.9 %collective-permute-start.47 = (bf16[512,768]{1,0:T(8,128)(2,1)S(1)}, bf16[512,768]{1,0:T(8,128)(2,1)S(1)}, u32[]{:S(2)}, u32[]{:S(2)}) collective-permute-start(bf16[512,768]{1,0:T(8,128)(2,1)S(1)} %copy-done.46), channel_id=1, source_target_pairs={{0,1},{1,0},{2,3},{3,2},{4,5},{5,4},{6,7},{7,6},{8,9},{9,8},{10,11... | collective-permute-start | bytes 2359304 | tf_op jit(solution)/shard_map/ppermute | solution.py:26
  257.9 22.2 %collective-permute-start.49 = (bf16[512,768]{1,0:T(8,128)(2,1)S(1)}, bf16[512,768]{1,0:T(8,128)(2,1)S(1)}, u32[]{:S(2)}, u32[]{:S(2)}) collective-permute-start(bf16[512,768]{1,0:T(8,128)(2,1)S(1)} %collective-permute-done.48.r2), channel_id=1, source_target_pairs={{0,1},{1,0},{2,3},{3,2},{4,5},{5,4},{6,7},{7,6},{8,9},{9,8},{10,11... | collective-permute-start | bytes 2359304 | tf_op jit(solution)/shard_map/ppermute | solution.py:26
  274.4 22.6 %collective-permute-start.60 = (bf16[4,96,1152]{2,1,0:T(8,128)(2,1)S(1)}, bf16[4,96,1152]{2,1,0:T(8,128)(2,1)S(1)}, u32[]{:S(2)}, u32[]{:S(2)}) collective-permute-start(bf16[4,96,1152]{2,1,0:T(8,128)(2,1)S(1)} %get-tuple-element.276), channel_id=1, source_target_pairs={{0,4},{4,0},{8,12},{12,8},{16,20},{20,16},{24,28},{28,24},{1,5},{5... | collective-permute-start | bytes 2654216 | tf_op jit(solution)/shard_map/ppermute | solution.py:26
  276.4 19.2 %collective-permute-start.51 = (bf16[512,768]{1,0:T(8,128)(2,1)}, bf16[512,768]{1,0:T(8,128)(2,1)}, u32[]{:S(2)}, u32[]{:S(2)}) collective-permute-start(bf16[512,768]{1,0:T(8,128)(2,1)} %get-tuple-element.262.r0), channel_id=1, source_target_pairs={{0,2},{1,3},{2,0},{3,1},{4,6},{5,7},{6,4},{7,5},{8,10},{9,11},{10,... | collective-permute-start | bytes 2359304 | tf_op jit(solution)/shard_map/ppermute | solution.py:26
  276.7 27.0 %collective-permute-start.68 = (bf16[4,96,768]{2,1,0:T(8,128)(2,1)S(1)}, bf16[4,96,768]{2,1,0:T(8,128)(2,1)S(1)}, u32[]{:S(2)}, u32[]{:S(2)}) collective-permute-start(bf16[4,96,768]{2,1,0:T(8,128)(2,1)S(1)} %get-tuple-element.285), channel_id=1, source_target_pairs={{0,8},{4,12},{8,0},{12,4},{16,24},{20,28},{24,16},{28,20},{1,9},{5... | collective-permute-start | bytes 1769480 | tf_op jit(solution)/shard_map/ppermute | solution.py:26
  278.6 36.3 %collective-permute-start.54 = (bf16[8,112,384]{2,1,0:T(8,128)(2,1)S(1)}, bf16[8,112,384]{2,1,0:T(8,128)(2,1)S(1)}, u32[]{:S(2)}, u32[]{:S(2)}) collective-permute-start(bf16[8,112,384]{2,1,0:T(8,128)(2,1)S(1)} %get-tuple-element.267), channel_id=1, source_target_pairs={{0,4},{4,0},{8,12},{12,8},{16,20},{20,16},{24,28},{28,24},{1,5},{5... | collective-permute-start | bytes 2064392 | tf_op jit(solution)/shard_map/ppermute | solution.py:26
  282.3 60.1 %collective-permute-start.50 = (bf16[512,768]{1,0:T(8,128)(2,1)}, bf16[512,768]{1,0:T(8,128)(2,1)}, u32[]{:S(2)}, u32[]{:S(2)}) collective-permute-start(bf16[512,768]{1,0:T(8,128)(2,1)} %get-tuple-element.262.r0), channel_id=1, source_target_pairs={{0,1},{1,0},{2,3},{3,2},{4,5},{5,4},{6,7},{7,6},{8,9},{9,8},{10,11... | collective-permute-start | bytes 2359304 | tf_op jit(solution)/shard_map/ppermute | solution.py:26
  295.6 46.7 %collective-permute-start.52 = (bf16[512,768]{1,0:T(8,128)(2,1)}, bf16[512,768]{1,0:T(8,128)(2,1)}, u32[]{:S(2)}, u32[]{:S(2)}) collective-permute-start(bf16[512,768]{1,0:T(8,128)(2,1)} %collective-permute-done.51.r2), channel_id=1, source_target_pairs={{0,1},{1,0},{2,3},{3,2},{4,5},{5,4},{6,7},{7,6},{8,9},{9,8},{10,11... | collective-permute-start | bytes 2359304 | tf_op jit(solution)/shard_map/ppermute | solution.py:26
  301.3 23.0 %collective-permute-start.61 = (bf16[2,96,1152]{2,1,0:T(8,128)(2,1)S(1)}, bf16[2,96,1152]{2,1,0:T(8,128)(2,1)S(1)}, u32[]{:S(2)}, u32[]{:S(2)}) collective-permute-start(bf16[2,96,1152]{2,1,0:T(8,128)(2,1)S(1)} %get-tuple-element.278), channel_id=1, source_target_pairs={{0,8},{4,12},{8,0},{12,4},{16,24},{20,28},{24,16},{28,20},{1,9},{5... | collective-permute-start | bytes 1327112 | tf_op jit(solution)/shard_map/ppermute | solution.py:26
  303.7 8.6 %collective-permute-start.65 = (f32[24,768]{1,0:T(8,128)S(1)}, f32[24,768]{1,0:T(8,128)S(1)}, u32[]{:S(2)}, u32[]{:S(2)}) collective-permute-start(f32[24,768]{1,0:T(8,128)S(1)} %add.39), channel_id=1, source_target_pairs={{0,4},{4,0},{8,12},{12,8},{16,20},{20,16},{24,28},{28,24},{1,5},{5... | collective-permute-start | bytes 221192 | tf_op jit(solution)/shard_map/ppermute | solution.py:26
  312.3 16.1 %collective-permute-start.69 = (bf16[2,96,768]{2,1,0:T(8,128)(2,1)S(1)}, bf16[2,96,768]{2,1,0:T(8,128)(2,1)S(1)}, u32[]{:S(2)}, u32[]{:S(2)}) collective-permute-start(bf16[2,96,768]{2,1,0:T(8,128)(2,1)S(1)} %get-tuple-element.287), channel_id=1, source_target_pairs={{0,16},{4,20},{8,24},{12,28},{16,0},{20,4},{24,8},{28,12},{1,17},{... | collective-permute-start | bytes 884744 | tf_op jit(solution)/shard_map/ppermute | solution.py:26
  321.9 27.7 %collective-permute-start.55 = (bf16[4,112,384]{2,1,0:T(8,128)(2,1)}, bf16[4,112,384]{2,1,0:T(8,128)(2,1)}, u32[]{:S(2)}, u32[]{:S(2)}) collective-permute-start(bf16[4,112,384]{2,1,0:T(8,128)(2,1)} %get-tuple-element.269), channel_id=1, source_target_pairs={{0,8},{4,12},{8,0},{12,4},{16,24},{20,28},{24,16},{28,20},{1,9},{5... | collective-permute-start | bytes 1032200 | tf_op jit(solution)/shard_map/ppermute | solution.py:26
  324.4 9.6 %collective-permute-start.67 = (f32[24,768]{1,0:T(8,128)S(1)}, f32[24,768]{1,0:T(8,128)}, u32[]{:S(2)}, u32[]{:S(2)}) collective-permute-start(f32[24,768]{1,0:T(8,128)S(1)} %add.41), channel_id=1, source_target_pairs={{0,16},{4,20},{8,24},{12,28},{16,0},{20,4},{24,8},{28,12},{1,17},{... | collective-permute-start | bytes 221192 | tf_op jit(solution)/shard_map/ppermute | solution.py:26
  328.4 18.9 %collective-permute-start.62 = (bf16[1,96,1152]{2,1,0:T(8,128)(2,1)}, bf16[1,96,1152]{2,1,0:T(8,128)(2,1)S(1)}, u32[]{:S(2)}, u32[]{:S(2)}) collective-permute-start(bf16[1,96,1152]{2,1,0:T(8,128)(2,1)} %get-tuple-element.280), channel_id=1, source_target_pairs={{0,16},{4,20},{8,24},{12,28},{16,0},{20,4},{24,8},{28,12},{1,17},{... | collective-permute-start | bytes 663560 | tf_op jit(solution)/shard_map/ppermute | solution.py:26
  351.0 8.8 %collective-permute-start.56 = (bf16[2,112,384]{2,1,0:T(8,128)(2,1)S(1)}, bf16[2,112,384]{2,1,0:T(8,128)(2,1)S(1)}, u32[]{:S(2)}, u32[]{:S(2)}) collective-permute-start(bf16[2,112,384]{2,1,0:T(8,128)(2,1)S(1)} %get-tuple-element.271), channel_id=1, source_target_pairs={{0,16},{4,20},{8,24},{12,28},{16,0},{20,4},{24,8},{28,12},{1,17},{... | collective-permute-start | bytes 516104 | tf_op jit(solution)/shard_map/ppermute | solution.py:26
  (117 other events, 1201.3 us)
